TPU v7x, 32 devices: a whole 2x2x4 slice. The times are simulated.
32 devices in a mesh: section: 2 (over x), dp: 4 (over z), tensor: 4 (over y, core).
Axes of the slice: x: 2, y: 2, z: 4, core: 2. Of those that a mesh axis runs over, the one named last changes fastest.
Arguments:
- boundary: bfloat16 [2, 8, 1024, 1024], P('section', 'dp', 'tensor'), may hold values from -6 to 6
- conditioning: bfloat16 [8, 1024], P('dp'), may hold values from -6 to 6
- query_key_value_weight: bfloat16 [2, 1024, 3, 1024], P('section', None, None, 'tensor'), may hold values from -0.1875 to 0.1875
- query_value_bias: bfloat16 [2, 2, 1024], P('section', None, 'tensor'), may hold values from -3 to 3
- attention_output_weight: bfloat16 [2, 1024, 1024], P('section', None, 'tensor'), may hold values from -1.5 to 1.5
- output_biases: bfloat16 [2, 2, 1024], P('section'), may hold values from -3 to 3
- first_mlp_weight: bfloat16 [2, 1024, 4096], P('section', None, 'tensor'), may hold values from -0.1875 to 0.1875
- first_mlp_bias: bfloat16 [2, 4096], P('section', 'tensor'), may hold values from -3 to 3
- second_mlp_weight: bfloat16 [2, 1024, 4096], P('section', None, 'tensor'), may hold values from -0.09375 to 0.09375
- w_ada: bfloat16 [2, 1024, 6144], P('section'), may hold values from -0.1875 to 0.1875
- ada_bias: bfloat16 [2, 6144], P('section'), may hold values from -3 to 3
Outputs:
- boundary_out: bfloat16 [2, 8, 1024, 1024], P('section', 'dp', 'tensor')
- cond_grad: float32 [8, 1024], P('dp')
- grad_qkv: float32 [2, 1024, 3, 1024], P('section', 'dp', None, 'tensor')
- grad_qv_bias: float32 [2, 2048], P('section', ('dp', 'tensor'))
- grad_proj: float32 [2, 1024, 1024], P('section', 'dp', 'tensor')
- grad_out_bias: float32 [2, 2048], P('section', ('dp', 'tensor'))
- grad_fc1: float32 [2, 1024, 4096], P('section', 'dp', 'tensor')
- grad_fc1_bias: float32 [2, 4096], P('section', ('dp', 'tensor'))
- grad_fc2: float32 [2, 1024, 4096], P('section', 'dp', 'tensor')
- grad_ada: float32 [2, 1024, 6144], P('section', ('dp', 'tensor'))
- grad_ada_bias: float32 [2, 6144], P('section', ('dp', 'tensor'))
All inputs are finite; a program needn't handle non-finite values.
Results may differ from a plain program's by a relative error of at most 0.015.
Values may be sent and summed in bfloat16 or wider, within the bound.
No kernel may reach another device: no remote copies, remote signals or barrier semaphores. Data moves between devices by JAX's collectives and lax.ppermute only.
A program may use at most 256 MiB of HBM per device.

v0:
```python
import jax
import jax.numpy as jnp
from jax import lax
from jax.sharding import PartitionSpec as P

HD = 64


precise = lax.Precision.HIGHEST


def shifted(block, axis, distance):
    devices = range(lax.axis_size(axis))
    route = [(i - distance, i) for i in devices if i - distance in devices]
    return lax.ppermute(block, axis, route)


def norm_modulate(incoming_tokens, offset, factor):
    center = incoming_tokens - jnp.mean(incoming_tokens, axis=-1, keepdims=True)
    spread = jnp.mean(center * center, axis=-1, keepdims=True)
    return center * lax.rsqrt(spread + 1e-06) * (1.0 + factor) + offset


def gelu_tanh(inputs):
    return jax.nn.gelu(inputs, approximate=True)


def contract_last(left, right):
    return lax.dot_general(
        left, right, (((1,), (1,)), ((), ())), preferred_element_type=jnp.float32
    )


def contract_first(left, right):
    return lax.dot_general(
        left, right, (((0,), (0,)), ((), ())), preferred_element_type=jnp.float32
    )


def attend_forward(queries, key_rows, values, factor):
    row_count = queries.shape[0]
    block_rows = min(512, row_count)
    outputs, log_sums = ([], [])
    for first_row in range(0, row_count, block_rows):
        query_part = queries[first_row : first_row + block_rows]
        scores = (
            jnp.einsum("qhe,khe->hqk", query_part, key_rows, preferred_element_type=jnp.float32)
            * factor
        )
        row_peak = jnp.max(scores, axis=-1, keepdims=True)
        expo_rows = jnp.exp(scores - row_peak)
        row_total = jnp.sum(expo_rows, axis=-1, keepdims=True)
        softmax_w = (expo_rows / row_total).astype(jnp.bfloat16)
        outputs.append(
            jnp.einsum("hqk,khe->qhe", softmax_w, values, preferred_element_type=jnp.float32)
        )
        log_sums.append((row_peak + jnp.log(row_total))[..., 0])
    return (jnp.concatenate(outputs, 0), jnp.concatenate(log_sums, 1))


def attend_backward(queries, key_rows, values, log_sums, grad_out, factor):
    row_count = queries.shape[0]
    block_rows = min(512, row_count)
    grad_queries = []
    grad_keys = jnp.zeros(key_rows.shape, jnp.float32)
    grad_values = jnp.zeros(values.shape, jnp.float32)
    for first_row in range(0, row_count, block_rows):
        query_part = queries[first_row : first_row + block_rows]
        grad_part = grad_out[first_row : first_row + block_rows]
        scores = (
            jnp.einsum("qhe,khe->hqk", query_part, key_rows, preferred_element_type=jnp.float32)
            * factor
        )
        softmax_f = jnp.exp(scores - log_sums[:, first_row : first_row + block_rows, None])
        grad_weights = jnp.einsum(
            "qhe,khe->hqk", grad_part, values, preferred_element_type=jnp.float32
        )
        inner_sum = jnp.sum(grad_weights * softmax_f, axis=-1, keepdims=True)
        grad_scores = (softmax_f * (grad_weights - inner_sum)).astype(jnp.bfloat16)
        grad_queries.append(
            jnp.einsum("hqk,khe->qhe", grad_scores, key_rows, preferred_element_type=jnp.float32)
            * factor
        )
        grad_keys = (
            grad_keys
            + jnp.einsum(
                "hqk,qhe->khe", grad_scores, query_part, preferred_element_type=jnp.float32
            )
            * factor
        )
        grad_values = grad_values + jnp.einsum(
            "hqk,qhe->khe",
            softmax_f.astype(jnp.bfloat16),
            grad_part,
            preferred_element_type=jnp.float32,
        )
    return (jnp.concatenate(grad_queries, 0), grad_keys, grad_values)


def layer_forward(incoming_tokens, modulation_rows, weights):
    (
        query_key_value_weight,
        query_value_bias,
        attention_output_weight,
        output_biases,
        first_mlp_weight,
        first_mlp_bias,
        second_mlp_weight,
    ) = weights
    local_width = query_key_value_weight.shape[2]
    factor = HD ** (-0.5)
    normed_rows = norm_modulate(incoming_tokens, modulation_rows[0], modulation_rows[1]).astype(
        jnp.bfloat16
    )
    normed = lax.all_gather(normed_rows, "tensor", axis=0, tiled=True)
    row_count = normed.shape[0]
    biases = jnp.stack(
        [query_value_bias[0], jnp.zeros_like(query_value_bias[0]), query_value_bias[1]]
    ).astype(jnp.float32)
    triple = (
        jnp.einsum(
            "sd,dje->sje", normed, query_key_value_weight, preferred_element_type=jnp.float32
        )
        + biases
    ).astype(jnp.bfloat16)
    shaped = triple.reshape(row_count, 3, local_width // HD, HD)
    queries, key_rows, values = (shaped[:, 0], shaped[:, 1], shaped[:, 2])
    mixed_heads, log_sums = attend_forward(queries, key_rows, values, factor)
    mixed_heads = mixed_heads.reshape(row_count, local_width).astype(jnp.bfloat16)
    branch = lax.psum_scatter(
        contract_last(mixed_heads, attention_output_weight),
        "tensor",
        scatter_dimension=0,
        tiled=True,
    ) + output_biases[0].astype(jnp.float32)
    middle = incoming_tokens + modulation_rows[2] * branch
    second_rows = norm_modulate(middle, modulation_rows[3], modulation_rows[4]).astype(jnp.bfloat16)
    second = lax.all_gather(second_rows, "tensor", axis=0, tiled=True)
    hidden_pre = jnp.dot(
        second, first_mlp_weight, preferred_element_type=jnp.float32
    ) + first_mlp_bias.astype(jnp.float32)
    activated = gelu_tanh(hidden_pre).astype(jnp.bfloat16)
    feed = lax.psum_scatter(
        contract_last(activated, second_mlp_weight), "tensor", scatter_dimension=0, tiled=True
    ) + output_biases[1].astype(jnp.float32)
    result = middle + modulation_rows[5] * feed
    saved_state = (
        incoming_tokens,
        normed,
        queries,
        key_rows,
        values,
        log_sums,
        mixed_heads,
        branch,
        middle,
        second,
        hidden_pre,
        activated,
        feed,
    )
    return (result, saved_state)


def layer_backward(grad_result, modulation_rows, weights, saved_state, col_start):
    (
        query_key_value_weight,
        query_value_bias,
        attention_output_weight,
        output_biases,
        first_mlp_weight,
        first_mlp_bias,
        second_mlp_weight,
    ) = weights
    (
        incoming_tokens,
        normed,
        queries,
        key_rows,
        values,
        log_sums,
        mixed_heads,
        branch,
        middle,
        second,
        hidden_pre,
        activated,
        feed,
    ) = saved_state
    row_count = normed.shape[0]
    width = normed.shape[1]
    local_width = query_key_value_weight.shape[2]
    factor = HD ** (-0.5)
    grad_gate2 = jnp.sum(grad_result * feed, axis=0)
    grad_feed_rows = (modulation_rows[5] * grad_result).astype(jnp.bfloat16)
    grad_feed = lax.all_gather(grad_feed_rows, "tensor", axis=0, tiled=True)
    grad_fc2 = contract_first(grad_feed, activated)
    grad_act = jnp.dot(grad_feed, second_mlp_weight, preferred_element_type=jnp.float32)
    grad_hidden = jax.vjp(gelu_tanh, hidden_pre)[1](grad_act)[0].astype(jnp.bfloat16)
    grad_fc1 = contract_first(second, grad_hidden)
    fc1_local = jnp.sum(grad_hidden.astype(jnp.float32), axis=0)
    grad_second = lax.psum_scatter(
        contract_last(grad_hidden, first_mlp_weight).astype(jnp.bfloat16),
        "tensor",
        scatter_dimension=0,
        tiled=True,
    ).astype(jnp.float32)
    second_pull = jax.vjp(norm_modulate, middle, modulation_rows[3], modulation_rows[4])[1]
    grad_middle, grad_shift2, grad_scale2 = second_pull(grad_second)
    grad_middle = grad_middle + grad_result
    grad_gate1 = jnp.sum(grad_middle * branch, axis=0)
    grad_branch_rows = (modulation_rows[2] * grad_middle).astype(jnp.bfloat16)
    grad_branch = lax.all_gather(grad_branch_rows, "tensor", axis=0, tiled=True)
    grad_proj = contract_first(grad_branch, mixed_heads)
    grad_mixed = jnp.dot(
        grad_branch, attention_output_weight, preferred_element_type=jnp.float32
    ).astype(jnp.bfloat16)
    grad_mixed = grad_mixed.reshape(row_count, local_width // HD, HD)
    grad_queries, grad_keys, grad_values = attend_backward(
        queries, key_rows, values, log_sums, grad_mixed, factor
    )
    grad_triple = jnp.stack([grad_queries, grad_keys, grad_values], 1).astype(jnp.bfloat16)
    grad_triple = grad_triple.reshape(row_count, 3, local_width)
    grad_qkv = jnp.einsum("sd,sje->dje", normed, grad_triple, preferred_element_type=jnp.float32)
    triple_sums = jnp.sum(grad_triple.astype(jnp.float32), axis=0)
    qv_local = jnp.stack([triple_sums[0], triple_sums[2]])
    grad_normed = lax.psum_scatter(
        jnp.einsum(
            "sje,dje->sd", grad_triple, query_key_value_weight, preferred_element_type=jnp.float32
        ).astype(jnp.bfloat16),
        "tensor",
        scatter_dimension=0,
        tiled=True,
    ).astype(jnp.float32)
    first_pull = jax.vjp(norm_modulate, incoming_tokens, modulation_rows[0], modulation_rows[1])[1]
    grad_tokens, grad_shift1, grad_scale1 = first_pull(grad_normed)
    grad_tokens = grad_tokens + grad_middle
    grad_mod = jnp.stack(
        [grad_shift1, grad_scale1, grad_gate1, grad_shift2, grad_scale2, grad_gate2]
    )
    zero_index = jnp.zeros((), jnp.int32)
    qv_full = lax.dynamic_update_slice(
        jnp.zeros((2, width), jnp.float32), qv_local, (zero_index, col_start)
    )
    fc1_width = grad_hidden.shape[1]
    fc1_full = lax.dynamic_update_slice(
        jnp.zeros((fc1_width * (width // local_width),), jnp.float32),
        fc1_local,
        (col_start * (fc1_width // local_width),),
    )
    out_partial = jnp.stack(
        [
            jnp.sum(grad_branch_rows.astype(jnp.float32), axis=0),
            jnp.sum(grad_feed_rows.astype(jnp.float32), axis=0),
        ]
    )
    return (
        grad_tokens,
        grad_mod,
        (grad_qkv, grad_proj, grad_fc1, grad_fc2),
        (qv_full, out_partial, fc1_full),
    )


def body(
    boundary,
    conditioning,
    query_key_value_weight,
    query_value_bias,
    attention_output_weight,
    output_biases,
    first_mlp_weight,
    first_mlp_bias,
    second_mlp_weight,
    w_ada,
    ada_bias,
):
    section_no = lax.axis_index("section")
    leading = section_no == 0
    micro_count = boundary.shape[1]
    tick_count = micro_count + 1
    weights = (
        query_key_value_weight[0],
        query_value_bias[0],
        attention_output_weight[0],
        output_biases[0],
        first_mlp_weight[0],
        first_mlp_bias[0],
        second_mlp_weight[0],
    )
    ada_weight = w_ada[0]
    width = ada_weight.shape[0]
    col_start = lax.axis_index("tensor") * query_key_value_weight.shape[3]
    cond_vals = conditioning.astype(jnp.float32)
    cond_act = jax.nn.silu(cond_vals).astype(jnp.bfloat16)
    mod_all = jnp.dot(cond_act, ada_weight, preferred_element_type=jnp.float32) + ada_bias[
        0
    ].astype(jnp.float32)
    mod_all = mod_all.reshape(micro_count, 6, width)
    slot_ids = jnp.arange(micro_count)
    incoming = jnp.zeros(boundary.shape[2:], jnp.bfloat16)
    saved_ticks, forward_rows = ([], [])
    for tick_no in range(tick_count):
        clipped = jnp.clip(tick_no - section_no, 0, micro_count - 1)
        source = jnp.where(leading, boundary[0, min(tick_no, micro_count - 1)], incoming)
        modulation_rows = lax.dynamic_index_in_dim(mod_all, clipped, 0, keepdims=False)
        result, saved_state = layer_forward(source.astype(jnp.float32), modulation_rows, weights)
        sent_rows = result.astype(jnp.bfloat16)
        saved_ticks.append((saved_state, modulation_rows))
        forward_rows.append(sent_rows)
        if tick_no + 1 < tick_count:
            incoming = shifted(sent_rows, "section", 1)
    returning = jnp.zeros(boundary.shape[2:], jnp.bfloat16)
    backward_rows = []
    totals = None
    small_totals = None
    mod_totals = jnp.zeros((micro_count, 6 * width), jnp.float32)
    for back_no in range(tick_count):
        saved_state, modulation_rows = saved_ticks[tick_count - 1 - back_no]
        latent_no = micro_count - back_no - section_no
        valid_flag = ((latent_no >= 0) & (latent_no < micro_count)).astype(jnp.float32)
        clipped = jnp.clip(latent_no, 0, micro_count - 1)
        seed_grad = jnp.where(leading, returning, boundary[0, max(micro_count - 1 - back_no, 0)])
        grad_result = seed_grad.astype(jnp.float32) * valid_flag
        grad_tokens, grad_mod, weight_parts, bias_parts = layer_backward(
            grad_result, modulation_rows, weights, saved_state, col_start
        )
        grad_sent = grad_tokens.astype(jnp.bfloat16)
        backward_rows.append(grad_sent)
        if back_no + 1 < tick_count:
            returning = shifted(grad_sent, "section", -1)
        mod_totals = mod_totals + (slot_ids == clipped).astype(jnp.float32)[
            :, None
        ] * grad_mod.reshape(1, -1)
        summed = (
            lax.psum_scatter(
                weight_parts[0][None].astype(jnp.bfloat16), "dp", scatter_dimension=1, tiled=True
            ).astype(jnp.float32),
            lax.psum_scatter(
                weight_parts[1][None].astype(jnp.bfloat16), "dp", scatter_dimension=1, tiled=True
            ).astype(jnp.float32),
            lax.psum_scatter(
                weight_parts[2][None].astype(jnp.bfloat16), "dp", scatter_dimension=1, tiled=True
            ).astype(jnp.float32),
            lax.psum_scatter(
                weight_parts[3][None].astype(jnp.bfloat16), "dp", scatter_dimension=1, tiled=True
            ).astype(jnp.float32),
        )
        totals = (
            summed if totals is None else tuple((old + new for old, new in zip(totals, summed)))
        )
        small_totals = (
            bias_parts
            if small_totals is None
            else tuple((old + new for old, new in zip(small_totals, bias_parts)))
        )
    ada_grad = lax.dot_general(
        cond_act.astype(jnp.float32),
        mod_totals,
        (((0,), (0,)), ((), ())),
        precision=precise,
        preferred_element_type=jnp.float32,
    )
    ada_bias_grad = jnp.sum(mod_totals, axis=0)
    small_sums = (
        lax.psum_scatter(ada_grad[None], ("dp", "tensor"), scatter_dimension=1, tiled=True),
        lax.psum_scatter(ada_bias_grad[None], ("dp", "tensor"), scatter_dimension=1, tiled=True),
        lax.psum_scatter(
            small_totals[0].reshape(1, -1), ("dp", "tensor"), scatter_dimension=1, tiled=True
        ),
        lax.psum_scatter(
            small_totals[1].reshape(1, -1), ("dp", "tensor"), scatter_dimension=1, tiled=True
        ),
        lax.psum_scatter(small_totals[2][None], ("dp", "tensor"), scatter_dimension=1, tiled=True),
    )
    back_cond = lax.dot_general(
        mod_totals,
        ada_weight.astype(jnp.float32),
        (((1,), (1,)), ((), ())),
        precision=precise,
        preferred_element_type=jnp.float32,
    )
    cond_total = lax.psum(back_cond, ("section", "tensor"))
    sigmoid_c = jax.nn.sigmoid(cond_vals)
    cond_grad = cond_total * sigmoid_c * (1.0 + cond_vals * (1.0 - sigmoid_c))
    layer_out = jnp.stack(forward_rows[1:tick_count])
    input_grads = jnp.stack(
        [backward_rows[micro_count - micro_no] for micro_no in range(micro_count)]
    )
    ends = jnp.where(leading, input_grads, layer_out)[None]
    return (
        ends,
        cond_grad,
        totals[0],
        small_sums[2],
        totals[1],
        small_sums[3],
        totals[2],
        small_sums[4],
        totals[3],
        small_sums[0],
        small_sums[1],
    )


def solution(mesh):
    in_specs = (
        P("section", "dp", "tensor", None),
        P("dp", None),
        P("section", None, None, "tensor"),
        P("section", None, "tensor"),
        P("section", None, "tensor"),
        P("section", None, None),
        P("section", None, "tensor"),
        P("section", "tensor"),
        P("section", None, "tensor"),
        P("section", None, None),
        P("section", None),
    )
    out_specs = (
        P("section", "dp", "tensor", None),
        P("dp", None),
        P("section", "dp", None, "tensor"),
        P("section", ("dp", "tensor")),
        P("section", "dp", "tensor"),
        P("section", ("dp", "tensor")),
        P("section", "dp", "tensor"),
        P("section", ("dp", "tensor")),
        P("section", "dp", "tensor"),
        P("section", ("dp", "tensor"), None),
        P("section", ("dp", "tensor")),
    )
    return jax.shard_map(body, mesh=mesh, in_specs=in_specs, out_specs=out_specs, check_vma=False)
```

profile of v0, /device:TPU:0, one launch (start us, length us, event | category | flops | bytes accessed | tf_op | source)
XLA Modules:
  0.0 2057.7 jit_solution(15180203561014488627)
XLA Ops:
  10.8 6.4 fusion.10
  19.2 25.2 %all-gather.13.cloned.1.call-done = bf16[1024,1024]{1,0:T(8,128)(2,1)} async-done(((bf16[256,1024]{1,0:T(8,128)(2,1)}), bf16[1024,1024]{1,0:T(8,128)(2,1)}) %all-gather.13.cloned.1.call-update) | async-done | bytes 2097168 | tf_op jit(solution)/shard_map/all_gather | solution.py:115
  63.6 44.1 %reduce-scatter.38.cloned.1.call-done = f32[256,1024]{1,0:T(8,128)} async-done(((f32[1024,1024]{1,0:T(8,128)}), f32[256,1024]{1,0:T(8,128)}) %reduce-scatter.38.cloned.1.call-update) | async-done | bytes 1048592 | tf_op jit(solution)/shard_map/reduce_scatter | solution.py:130
  112.8 22.7 %all-gather.15.cloned.1.call-done = bf16[1024,1024]{1,0:T(8,128)(2,1)} async-done(((bf16[256,1024]{1,0:T(8,128)(2,1)}), bf16[1024,1024]{1,0:T(8,128)(2,1)}) %all-gather.15.cloned.1.call-update) | async-done | bytes 2097168 | tf_op jit(solution)/shard_map/all_gather | solution.py:138
  146.8 44.6 %reduce-scatter.40.cloned.1.call-done = f32[256,1024]{1,0:T(8,128)} async-done(((f32[1024,1024]{1,0:T(8,128)}), f32[256,1024]{1,0:T(8,128)}) %reduce-scatter.40.cloned.1.call-update) | async-done | bytes 1048592 | tf_op jit(solution)/shard_map/reduce_scatter | solution.py:143
  196.6 11.1 collective-permute-done
  209.9 23.7 %all-gather.17.cloned.1.call-done = bf16[1024,1024]{1,0:T(8,128)(2,1)} async-done(((bf16[256,1024]{1,0:T(8,128)(2,1)}), bf16[1024,1024]{1,0:T(8,128)(2,1)}) %all-gather.17.cloned.1.call-update) | async-done | bytes 2097168 | tf_op jit(solution)/shard_map/all_gather | solution.py:115
  252.4 44.6 %reduce-scatter.42.cloned.1.call-done = f32[256,1024]{1,0:T(8,128)} async-done(((f32[1024,1024]{1,0:T(8,128)}), f32[256,1024]{1,0:T(8,128)}) %reduce-scatter.42.cloned.1.call-update) | async-done | bytes 1048592 | tf_op jit(solution)/shard_map/reduce_scatter | solution.py:130
  300.9 22.5 %all-gather.19.cloned.1.call-done = bf16[1024,1024]{1,0:T(8,128)(2,1)} async-done(((bf16[256,1024]{1,0:T(8,128)(2,1)}), bf16[1024,1024]{1,0:T(8,128)(2,1)}) %all-gather.19.cloned.1.call-update) | async-done | bytes 2097168 | tf_op jit(solution)/shard_map/all_gather | solution.py:138
  334.8 44.6 %reduce-scatter.44.cloned.1.call-done = f32[256,1024]{1,0:T(8,128)} async-done(((f32[1024,1024]{1,0:T(8,128)}), f32[256,1024]{1,0:T(8,128)}) %reduce-scatter.44.cloned.1.call-update) | async-done | bytes 1048592 | tf_op jit(solution)/shard_map/reduce_scatter | solution.py:143
  384.6 11.1 collective-permute-done.1
  397.9 23.7 %all-gather.21.cloned.1.call-done = bf16[1024,1024]{1,0:T(8,128)(2,1)} async-done(((bf16[256,1024]{1,0:T(8,128)(2,1)}), bf16[1024,1024]{1,0:T(8,128)(2,1)}) %all-gather.21.cloned.1.call-update) | async-done | bytes 2097168 | tf_op jit(solution)/shard_map/all_gather | solution.py:115
  440.3 44.6 %reduce-scatter.46.cloned.1.call-done = f32[256,1024]{1,0:T(8,128)} async-done(((f32[1024,1024]{1,0:T(8,128)}), f32[256,1024]{1,0:T(8,128)}) %reduce-scatter.46.cloned.1.call-update) | async-done | bytes 1048592 | tf_op jit(solution)/shard_map/reduce_scatter | solution.py:130
  489.4 21.9 %all-gather.25.cloned.1.call-done = bf16[1024,1024]{1,0:T(8,128)(2,1)} async-done(((bf16[256,1024]{1,0:T(8,128)(2,1)}), bf16[1024,1024]{1,0:T(8,128)(2,1)}) %all-gather.25.cloned.1.call-update) | async-done | bytes 2097168 | tf_op jit(solution)/shard_map/all_gather | solution.py:138
  511.4 6.5 fusion.102
  517.9 18.2 all-gather.23.cloned.1.call-done
  536.1 8.0 convert_reduce_fusion.2
  549.2 31.5 %reduce-scatter.48.cloned.1.call-done = bf16[256,1024]{1,0:T(8,128)(2,1)} async-done(((bf16[1024,1024]{1,0:T(8,128)(2,1)}), bf16[256,1024]{1,0:T(8,128)(2,1)}) %reduce-scatter.48.cloned.1.call-update) | async-done | bytes 524304 | tf_op jit(solution)/shard_map/reduce_scatter | solution.py:202
  589.0 22.3 %all-gather.27.cloned.1.call-done = bf16[1024,1024]{1,0:T(8,128)(2,1)} async-done(((bf16[256,1024]{1,0:T(8,128)(2,1)}), bf16[1024,1024]{1,0:T(8,128)(2,1)}) %all-gather.27.cloned.1.call-update) | async-done | bytes 2097168 | tf_op jit(solution)/shard_map/all_gather | solution.py:213
  613.9 7.9 multiply_reduce_fusion.5
  640.7 7.0 multiply_convert_fusion.4
  660.9 31.4 %reduce-scatter.50.cloned.1.call-done = bf16[256,1024]{1,0:T(8,128)(2,1)} async-done(((bf16[1024,1024]{1,0:T(8,128)(2,1)}), bf16[256,1024]{1,0:T(8,128)(2,1)}) %reduce-scatter.50.cloned.1.call-update) | async-done | bytes 524304 | tf_op jit(solution)/shard_map/reduce_scatter | solution.py:227
  700.2 14.6 collective-permute-done.2
  717.8 21.8 %all-gather.29.cloned.1.call-done = bf16[1024,1024]{1,0:T(8,128)(2,1)} async-done(((bf16[256,1024]{1,0:T(8,128)(2,1)}), bf16[1024,1024]{1,0:T(8,128)(2,1)}) %all-gather.29.cloned.1.call-update) | async-done | bytes 2097168 | tf_op jit(solution)/shard_map/all_gather | solution.py:196
  739.5 7.4 convert_reduce_fusion.1
  752.1 31.5 %reduce-scatter.52.cloned.1.call-done = bf16[256,1024]{1,0:T(8,128)(2,1)} async-done(((bf16[1024,1024]{1,0:T(8,128)(2,1)}), bf16[256,1024]{1,0:T(8,128)(2,1)}) %reduce-scatter.52.cloned.1.call-update) | async-done | bytes 524304 | tf_op jit(solution)/shard_map/reduce_scatter | solution.py:202
  791.9 22.4 %all-gather.31.cloned.1.call-done = bf16[1024,1024]{1,0:T(8,128)(2,1)} async-done(((bf16[256,1024]{1,0:T(8,128)(2,1)}), bf16[1024,1024]{1,0:T(8,128)(2,1)}) %all-gather.31.cloned.1.call-update) | async-done | bytes 2097168 | tf_op jit(solution)/shard_map/all_gather | solution.py:213
  840.9 7.0 multiply_convert_fusion.2
  855.9 5.1 bitcast_convert_fusion.1
  861.5 31.2 %reduce-scatter.54.cloned.1.call-done = bf16[256,1024]{1,0:T(8,128)(2,1)} async-done(((bf16[1024,1024]{1,0:T(8,128)(2,1)}), bf16[256,1024]{1,0:T(8,128)(2,1)}) %reduce-scatter.54.cloned.1.call-update) | async-done | bytes 524304 | tf_op jit(solution)/shard_map/reduce_scatter | solution.py:227
  900.0 14.6 collective-permute-done.3
  916.9 21.8 %all-gather.33.cloned.1.call-done = bf16[1024,1024]{1,0:T(8,128)(2,1)} async-done(((bf16[256,1024]{1,0:T(8,128)(2,1)}), bf16[1024,1024]{1,0:T(8,128)(2,1)}) %all-gather.33.cloned.1.call-update) | async-done | bytes 2097168 | tf_op jit(solution)/shard_map/all_gather | solution.py:196
  938.8 7.4 convert_reduce_fusion
  951.3 31.5 %reduce-scatter.56.cloned.1.call-done = bf16[256,1024]{1,0:T(8,128)(2,1)} async-done(((bf16[1024,1024]{1,0:T(8,128)(2,1)}), bf16[256,1024]{1,0:T(8,128)(2,1)}) %reduce-scatter.56.cloned.1.call-update) | async-done | bytes 524304 | tf_op jit(solution)/shard_map/reduce_scatter | solution.py:202
  989.8 6.9 fusion.78
  997.4 15.0 all-gather.35.cloned.1.call-done
  1019.5 7.1 fusion.187
  1028.6 6.3 multiply_reduce_fusion.1
  1068.2 6.0 convert_bitcast_fusion.5
  1074.3 6.0 convert_bitcast_fusion.4
  1080.4 6.0 convert_bitcast_fusion.3
  1086.9 6.8 convert_bitcast_fusion.2
  1093.7 6.8 convert_bitcast_fusion.1
  1100.6 6.8 convert_bitcast_fusion
  1139.0 5.1 fusion.163
  1159.7 13.4 convolution_bitcast_fusion
  1174.7 33.0 %reduce-scatter.74.cloned.1.call-done = bf16[1,256,1024]{2,1,0:T(8,128)(2,1)} async-done(((bf16[1,1024,1024]{2,1,0:T(8,128)(2,1)}), bf16[1,256,1024]{2,1,0:T(8,128)(2,1)}) %reduce-scatter.74.cloned.1.call-update) | async-done | bytes 524304 | tf_op jit(solution)/shard_map/reduce_scatter | solution.py:342
  1207.7 45.4 %reduce-scatter.76.cloned.1.call-done = bf16[1,256,1024]{2,1,0:T(8,128)(2,1)} async-done(((bf16[1,1024,1024]{2,1,0:T(8,128)(2,1)}), bf16[1,256,1024]{2,1,0:T(8,128)(2,1)}) %reduce-scatter.76.cloned.1.call-update) | async-done | bytes 524304 | tf_op jit(solution)/shard_map/reduce_scatter | solution.py:342
  1253.1 45.6 %reduce-scatter.78.cloned.1.call-done = bf16[1,256,1024]{2,1,0:T(8,128)(2,1)} async-done(((bf16[1,1024,1024]{2,1,0:T(8,128)(2,1)}), bf16[1,256,1024]{2,1,0:T(8,128)(2,1)}) %reduce-scatter.78.cloned.1.call-update) | async-done | bytes 524304 | tf_op jit(solution)/shard_map/reduce_scatter | solution.py:342
  1301.3 42.9 %reduce-scatter.80.cloned.1.call-done = bf16[1,256,1024]{2,1,0:T(8,128)(2,1)} async-done(((bf16[1,1024,1024]{2,1,0:T(8,128)(2,1)}), bf16[1,256,1024]{2,1,0:T(8,128)(2,1)}) %reduce-scatter.80.cloned.1.call-update) | async-done | bytes 524304 | tf_op jit(solution)/shard_map/reduce_scatter | solution.py:345
  1344.2 45.5 %reduce-scatter.82.cloned.1.call-done = bf16[1,256,1024]{2,1,0:T(8,128)(2,1)} async-done(((bf16[1,1024,1024]{2,1,0:T(8,128)(2,1)}), bf16[1,256,1024]{2,1,0:T(8,128)(2,1)}) %reduce-scatter.82.cloned.1.call-update) | async-done | bytes 524304 | tf_op jit(solution)/shard_map/reduce_scatter | solution.py:345
  1389.7 45.5 %reduce-scatter.84.cloned.1.call-done = bf16[1,256,1024]{2,1,0:T(8,128)(2,1)} async-done(((bf16[1,1024,1024]{2,1,0:T(8,128)(2,1)}), bf16[1,256,1024]{2,1,0:T(8,128)(2,1)}) %reduce-scatter.84.cloned.1.call-update) | async-done | bytes 524304 | tf_op jit(solution)/shard_map/reduce_scatter | solution.py:345
  1437.8 58.1 %reduce-scatter.90.cloned.1.call-done = f32[128,1]{1,0:T(8,128)} async-done(((f32[2048,1]{1,0:T(8,128)}), f32[128,1]{1,0:T(8,128)}) %reduce-scatter.90.cloned.1.call-update) | async-done | bytes 528
  1497.3 58.5 %reduce-scatter.88.cloned.1.call-done = f32[128,1]{1,0:T(8,128)} async-done(((f32[2048,1]{1,0:T(8,128)}), f32[128,1]{1,0:T(8,128)}) %reduce-scatter.88.cloned.1.call-update) | async-done | bytes 528
  1557.3 21.7 %reduce-scatter.68.cloned.1.call-done = bf16[1,256,256]{2,1,0:T(8,128)(2,1)} async-done(((bf16[1,1024,256]{2,1,0:T(8,128)(2,1)}), bf16[1,256,256]{2,1,0:T(8,128)(2,1)}) %reduce-scatter.68.cloned.1.call-update) | async-done | bytes 131088 | tf_op jit(solution)/shard_map/reduce_scatter | solution.py:339
  1579.0 22.3 %reduce-scatter.70.cloned.1.call-done = bf16[1,256,256]{2,1,0:T(8,128)(2,1)} async-done(((bf16[1,1024,256]{2,1,0:T(8,128)(2,1)}), bf16[1,256,256]{2,1,0:T(8,128)(2,1)}) %reduce-scatter.70.cloned.1.call-update) | async-done | bytes 131088 | tf_op jit(solution)/shard_map/reduce_scatter | solution.py:339
  1601.2 22.8 %reduce-scatter.72.cloned.1.call-done = bf16[1,256,256]{2,1,0:T(8,128)(2,1)} async-done(((bf16[1,1024,256]{2,1,0:T(8,128)(2,1)}), bf16[1,256,256]{2,1,0:T(8,128)(2,1)}) %reduce-scatter.72.cloned.1.call-update) | async-done | bytes 131088 | tf_op jit(solution)/shard_map/reduce_scatter | solution.py:339
  1625.8 34.0 %reduce-scatter.62.cloned.1.call-done = bf16[1,256,3,256]{3,1,2,0:T(8,128)(2,1)} async-done(((bf16[1,1024,3,256]{3,1,2,0:T(8,128)(2,1)}), bf16[1,256,3,256]{3,1,2,0:T(8,128)(2,1)}) %reduce-scatter.62.cloned.1.call-update) | async-done | bytes 393232 | tf_op jit(solution)/shard_map/reduce_scatter | solution.py:336
  1659.8 36.7 %reduce-scatter.64.cloned.1.call-done = bf16[1,256,3,256]{3,1,2,0:T(8,128)(2,1)} async-done(((bf16[1,1024,3,256]{3,1,2,0:T(8,128)(2,1)}), bf16[1,256,3,256]{3,1,2,0:T(8,128)(2,1)}) %reduce-scatter.64.cloned.1.call-update) | async-done | bytes 393232 | tf_op jit(solution)/shard_map/reduce_scatter | solution.py:336
  1696.5 36.6 %reduce-scatter.66.cloned.1.call-done = bf16[1,256,3,256]{3,1,2,0:T(8,128)(2,1)} async-done(((bf16[1,1024,3,256]{3,1,2,0:T(8,128)(2,1)}), bf16[1,256,3,256]{3,1,2,0:T(8,128)(2,1)}) %reduce-scatter.66.cloned.1.call-update) | async-done | bytes 393232 | tf_op jit(solution)/shard_map/reduce_scatter | solution.py:336
  1735.3 12.8 fusion
  1748.1 13.7 psum.7
  1764.8 37.7 %reduce-scatter.94.cloned.1.call-done = f32[384,1]{1,0:T(8,128)} async-done(((f32[6144,1]{1,0:T(8,128)}), f32[384,1]{1,0:T(8,128)}) %reduce-scatter.94.cloned.1.call-update) | async-done | bytes 1552
  1804.1 246.5 %reduce-scatter.86.cloned.1.call-done = f32[1,64,6144]{2,1,0:T(8,128)} async-done(((f32[1,1024,6144]{2,1,0:T(8,128)}), f32[1,64,6144]{2,1,0:T(8,128)}) %reduce-scatter.86.cloned.1.call-update) | async-done | bytes 1572880 | tf_op jit(solution)/shard_map/reduce_scatter | solution.py:366
  (553 shorter events, 349.6 us)
Async XLA Ops:
  7.2 134.8 %copy-start = (bf16[1,1024,1024]{2,1,0:T(8,128)(2,1)S(1)}, bf16[1,1024,1024]{2,1,0:T(8,128)(2,1)}, u32[]{:S(2)}) copy-start(bf16[1,1024,1024]{2,1,0:T(8,128)(2,1)} %param.19) | copy-start | bytes 6291460
  7.2 37.3 %all-gather.13.cloned.1.call-start = ((), (), s32[]{:S(2)}) async-start(), calls=%async_computation.29 | async-start | bytes 2621440 | tf_op jit(solution)/shard_map/all_gather | solution.py:115
  17.3 90.4 %copy-start.65 = (f32[1,1,1024]{2,1,0:T(1,128)}, f32[1,1,1024]{2,1,0:T(1,128)S(1)}, u32[]{:S(2)}) copy-start(f32[1,1,1024]{2,1,0:T(1,128)S(1)} %get-tuple-element.75) | copy-start | bytes 12292
  17.4 90.4 %copy-start.73 = (f32[1,1,1024]{2,1,0:T(1,128)}, f32[1,1,1024]{2,1,0:T(1,128)S(1)}, u32[]{:S(2)}) copy-start(f32[1,1,1024]{2,1,0:T(1,128)S(1)} %get-tuple-element.87) | copy-start | bytes 12292
  17.4 93.6 %copy-start.54 = (f32[1,1,1024]{2,1,0:T(1,128)}, f32[1,1,1024]{2,1,0:T(1,128)S(1)}, u32[]{:S(2)}) copy-start(f32[1,1,1024]{2,1,0:T(1,128)S(1)} %get-tuple-element.85) | copy-start | bytes 12292
  17.4 174.0 %copy-start.67 = (f32[1,1,1024]{2,1,0:T(1,128)}, f32[1,1,1024]{2,1,0:T(1,128)S(1)}, u32[]{:S(2)}) copy-start(f32[1,1,1024]{2,1,0:T(1,128)S(1)} %get-tuple-element.86) | copy-start | bytes 12292
  17.4 190.9 %copy-start.50 = (f32[1,1,1024]{2,1,0:T(1,128)}, f32[1,1,1024]{2,1,0:T(1,128)S(1)}, u32[]{:S(2)}) copy-start(f32[1,1,1024]{2,1,0:T(1,128)S(1)} %get-tuple-element.84) | copy-start | bytes 12292
  19.0 88.7 %reduce-scatter.38.cloned.1.call-start = ((), (), s32[]{:S(2)}) async-start(), calls=%async_computation.30 | async-start | bytes 5242880 | tf_op jit(solution)/shard_map/reduce_scatter | solution.py:130
  63.1 49.8 %copy-start.106 = (bf16[1,1024]{1,0:T(2,128)(2,1)S(1)}, bf16[1,1024]{1,0:T(2,128)(2,1)}, u32[]{:S(2)}) copy-start(bf16[1,1024]{1,0:T(2,128)(2,1)} %param.18) | copy-start | bytes 6148
  63.1 72.4 %all-gather.15.cloned.1.call-start = ((), (), s32[]{:S(2)}) async-start(), calls=%async_computation.31 | async-start | bytes 2621440 | tf_op jit(solution)/shard_map/all_gather | solution.py:138
  63.6 315.8 %copy-start.62 = (f32[1,1,1024]{2,1,0:T(1,128)}, f32[1,1,1024]{2,1,0:T(1,128)S(1)}, u32[]{:S(2)}) copy-start(f32[1,1,1024]{2,1,0:T(1,128)S(1)} %get-tuple-element.99) | copy-start | bytes 12292
  63.6 421.3 %copy-start.52 = (f32[1,1,1024]{2,1,0:T(1,128)}, f32[1,1,1024]{2,1,0:T(1,128)S(1)}, u32[]{:S(2)}) copy-start(f32[1,1,1024]{2,1,0:T(1,128)S(1)} %get-tuple-element.100) | copy-start | bytes 12292
  112.8 78.6 %reduce-scatter.40.cloned.1.call-start = ((), (), s32[]{:S(2)}) async-start(), calls=%async_computation.32 | async-start | bytes 5242880 | tf_op jit(solution)/shard_map/reduce_scatter | solution.py:143
  146.7 86.9 %all-gather.17.cloned.1.call-start = ((), (), s32[]{:S(2)}) async-start(), calls=%async_computation.33 | async-start | bytes 2621440 | tf_op jit(solution)/shard_map/all_gather | solution.py:115
  193.2 14.6 collective-permute-start
  209.8 87.2 %reduce-scatter.42.cloned.1.call-start = ((), (), s32[]{:S(2)}) async-start(), calls=%async_computation.34 | async-start | bytes 5242880 | tf_op jit(solution)/shard_map/reduce_scatter | solution.py:130
  252.4 71.1 %all-gather.19.cloned.1.call-start = ((), (), s32[]{:S(2)}) async-start(), calls=%async_computation.35 | async-start | bytes 2621440 | tf_op jit(solution)/shard_map/all_gather | solution.py:138
  300.7 78.7 %reduce-scatter.44.cloned.1.call-start = ((), (), s32[]{:S(2)}) async-start(), calls=%async_computation.36 | async-start | bytes 5242880 | tf_op jit(solution)/shard_map/reduce_scatter | solution.py:143
  334.8 86.9 %all-gather.21.cloned.1.call-start = ((), (), s32[]{:S(2)}) async-start(), calls=%async_computation.37 | async-start | bytes 2621440 | tf_op jit(solution)/shard_map/all_gather | solution.py:115
  381.2 14.6 collective-permute-start.1
  397.9 87.0 %reduce-scatter.46.cloned.1.call-start = ((), (), s32[]{:S(2)}) async-start(), calls=%async_computation.39 | async-start | bytes 5242880 | tf_op jit(solution)/shard_map/reduce_scatter | solution.py:130
  440.3 71.1 %all-gather.25.cloned.1.call-start = ((), (), s32[]{:S(2)}) async-start(), calls=%async_computation.40 | async-start | bytes 2621440 | tf_op jit(solution)/shard_map/all_gather | solution.py:138
  488.6 47.4 %all-gather.23.cloned.1.call-start = ((), (), s32[]{:S(2)}) async-start(), calls=%async_computation.38 | async-start | bytes 2621440 | tf_op jit(solution)/shard_map/all_gather | solution.py:196
  489.2 91.5 %reduce-scatter.48.cloned.1.call-start = ((), (), s32[]{:S(2)}) async-start(), calls=%async_computation.41 | async-start | bytes 2621440 | tf_op jit(solution)/shard_map/reduce_scatter | solution.py:202
  549.1 62.2 %all-gather.27.cloned.1.call-start = ((), (), s32[]{:S(2)}) async-start(), calls=%async_computation.42 | async-start | bytes 2621440 | tf_op jit(solution)/shard_map/all_gather | solution.py:213
  588.5 103.8 %reduce-scatter.50.cloned.1.call-start = ((), (), s32[]{:S(2)}) async-start(), calls=%async_computation.43 | async-start | bytes 2621440 | tf_op jit(solution)/shard_map/reduce_scatter | solution.py:227
  660.7 78.8 %all-gather.29.cloned.1.call-start = ((), (), s32[]{:S(2)}) async-start(), calls=%async_computation.44 | async-start | bytes 2621440 | tf_op jit(solution)/shard_map/all_gather | solution.py:196
  699.0 15.9 collective-permute-start.2
  717.7 65.9 %reduce-scatter.52.cloned.1.call-start = ((), (), s32[]{:S(2)}) async-start(), calls=%async_computation.45 | async-start | bytes 2621440 | tf_op jit(solution)/shard_map/reduce_scatter | solution.py:202
  752.0 39.8 %copy-start.61 = (f32[4,512]{1,0:T(4,128)S(1)}, f32[4,512]{1,0:T(4,128)}, u32[]{:S(2)}) copy-start(f32[4,512]{1,0:T(4,128)} %copy-done.60) | copy-start | bytes 24580
  752.0 39.8 %copy-start.82 = (f32[4,512]{1,0:T(4,128)S(1)}, f32[4,512]{1,0:T(4,128)}, u32[]{:S(2)}) copy-start(f32[4,512]{1,0:T(4,128)} %copy-done.81) | copy-start | bytes 24580
  752.1 62.3 %all-gather.31.cloned.1.call-start = ((), (), s32[]{:S(2)}) async-start(), calls=%async_computation.46 | async-start | bytes 2621440 | tf_op jit(solution)/shard_map/all_gather | solution.py:213
  791.6 101.0 %reduce-scatter.54.cloned.1.call-start = ((), (), s32[]{:S(2)}) async-start(), calls=%async_computation.47 | async-start | bytes 2621440 | tf_op jit(solution)/shard_map/reduce_scatter | solution.py:227
  855.9 36.7 %copy-start.51 = (f32[1,1,1024]{2,1,0:T(1,128)S(1)}, f32[1,1,1024]{2,1,0:T(1,128)}, u32[]{:S(2)}) copy-start(f32[1,1,1024]{2,1,0:T(1,128)} %copy-done.50) | copy-start | bytes 12292
  855.9 36.7 %copy-start.70 = (f32[256]{0:T(256)S(1)}, f32[256]{0:T(256)}, u32[]{:S(2)}) copy-start(f32[256]{0:T(256)} %copy-done.69) | copy-start | bytes 3076
  855.9 38.2 %copy-start.103 = (f32[256]{0:T(256)S(1)}, f32[256]{0:T(256)}, u32[]{:S(2)}) copy-start(f32[256]{0:T(256)} %copy-done.102) | copy-start | bytes 3076
  855.9 38.3 %copy-start.84 = (f32[256]{0:T(256)S(1)}, f32[256]{0:T(256)}, u32[]{:S(2)}) copy-start(f32[256]{0:T(256)} %copy-done.83) | copy-start | bytes 3076
  861.0 53.6 %copy-start.68 = (f32[1,1,1024]{2,1,0:T(1,128)S(1)}, f32[1,1,1024]{2,1,0:T(1,128)}, u32[]{:S(2)}) copy-start(f32[1,1,1024]{2,1,0:T(1,128)} %copy-done.67) | copy-start | bytes 12292
  861.0 77.8 %all-gather.33.cloned.1.call-start = ((), (), s32[]{:S(2)}) async-start(), calls=%async_computation.48 | async-start | bytes 2621440 | tf_op jit(solution)/shard_map/all_gather | solution.py:196
  898.7 15.8 collective-permute-start.3
  916.9 66.0 %reduce-scatter.56.cloned.1.call-start = ((), (), s32[]{:S(2)}) async-start(), calls=%async_computation.49 | async-start | bytes 2621440 | tf_op jit(solution)/shard_map/reduce_scatter | solution.py:202
  947.5 35.4 %copy-start.76 = (f32[256]{0:T(256)S(1)}, f32[256]{0:T(256)}, u32[]{:S(2)}) copy-start(f32[256]{0:T(256)} %copy-done.75) | copy-start | bytes 3076
  947.5 37.1 %copy-start.105 = (f32[256]{0:T(256)S(1)}, f32[256]{0:T(256)}, u32[]{:S(2)}) copy-start(f32[256]{0:T(256)} %copy-done.104) | copy-start | bytes 3076
  947.5 37.1 %copy-start.99 = (f32[256]{0:T(256)S(1)}, f32[256]{0:T(256)}, u32[]{:S(2)}) copy-start(f32[256]{0:T(256)} %copy-done.98) | copy-start | bytes 3076
  951.3 61.2 %all-gather.35.cloned.1.call-start = ((), (), s32[]{:S(2)}) async-start(), calls=%async_computation.50 | async-start | bytes 2621440 | tf_op jit(solution)/shard_map/all_gather | solution.py:213
  989.7 159.6 %reduce-scatter.60.cloned.1.call-start = ((), (), s32[]{:S(2)}) async-start(), calls=%async_computation.52 | async-start | bytes 5242880 | tf_op jit(solution)/shard_map/reduce_scatter | solution.py:143
  996.7 152.7 %reduce-scatter.58.cloned.1.call-start = ((), (), s32[]{:S(2)}) async-start(), calls=%async_computation.51 | async-start | bytes 2621440 | tf_op jit(solution)/shard_map/reduce_scatter | solution.py:227
  1065.8 107.4 %reduce-scatter.92.cloned.1.call-start = ((), (), s32[]{:S(2)}) async-start(), calls=%async_computation.68 | async-start | bytes 2228224
  1068.1 139.6 %reduce-scatter.74.cloned.1.call-start = ((), (), s32[]{:S(2)}) async-start(), calls=%async_computation.59 | async-start | bytes 2621440 | tf_op jit(solution)/shard_map/reduce_scatter | solution.py:342
  1074.2 178.8 %reduce-scatter.76.cloned.1.call-start = ((), (), s32[]{:S(2)}) async-start(), calls=%async_computation.60 | async-start | bytes 2621440 | tf_op jit(solution)/shard_map/reduce_scatter | solution.py:342
  1080.4 218.3 %reduce-scatter.78.cloned.1.call-start = ((), (), s32[]{:S(2)}) async-start(), calls=%async_computation.61 | async-start | bytes 2621440 | tf_op jit(solution)/shard_map/reduce_scatter | solution.py:342
  1086.4 257.8 %reduce-scatter.80.cloned.1.call-start = ((), (), s32[]{:S(2)}) async-start(), calls=%async_computation.62 | async-start | bytes 2621440 | tf_op jit(solution)/shard_map/reduce_scatter | solution.py:345
  1093.7 296.0 %reduce-scatter.82.cloned.1.call-start = ((), (), s32[]{:S(2)}) async-start(), calls=%async_computation.63 | async-start | bytes 2621440 | tf_op jit(solution)/shard_map/reduce_scatter | solution.py:345
  1100.5 334.6 %reduce-scatter.84.cloned.1.call-start = ((), (), s32[]{:S(2)}) async-start(), calls=%async_computation.64 | async-start | bytes 2621440 | tf_op jit(solution)/shard_map/reduce_scatter | solution.py:345
  1107.4 388.5 %reduce-scatter.90.cloned.1.call-start = ((), (), s32[]{:S(2)}) async-start(), calls=%async_computation.67 | async-start | bytes 1114112
  1116.4 439.4 %reduce-scatter.88.cloned.1.call-start = ((), (), s32[]{:S(2)}) async-start(), calls=%async_computation.66 | async-start | bytes 1114112
  1121.9 457.1 %reduce-scatter.68.cloned.1.call-start = ((), (), s32[]{:S(2)}) async-start(), calls=%async_computation.56 | async-start | bytes 655360 | tf_op jit(solution)/shard_map/reduce_scatter | solution.py:339
  1125.2 476.0 %reduce-scatter.70.cloned.1.call-start = ((), (), s32[]{:S(2)}) async-start(), calls=%async_computation.57 | async-start | bytes 655360 | tf_op jit(solution)/shard_map/reduce_scatter | solution.py:339
  1129.5 494.5 %reduce-scatter.72.cloned.1.call-start = ((), (), s32[]{:S(2)}) async-start(), calls=%async_computation.58 | async-start | bytes 655360 | tf_op jit(solution)/shard_map/reduce_scatter | solution.py:339
  1133.9 525.9 %reduce-scatter.62.cloned.1.call-start = ((), (), s32[]{:S(2)}) async-start(), calls=%async_computation.53 | async-start | bytes 1966080 | tf_op jit(solution)/shard_map/reduce_scatter | solution.py:336
  1139.0 557.5 %reduce-scatter.64.cloned.1.call-start = ((), (), s32[]{:S(2)}) async-start(), calls=%async_computation.54 | async-start | bytes 1966080 | tf_op jit(solution)/shard_map/reduce_scatter | solution.py:336
  1144.2 588.9 %reduce-scatter.66.cloned.1.call-start = ((), (), s32[]{:S(2)}) async-start(), calls=%async_computation.55 | async-start | bytes 1966080 | tf_op jit(solution)/shard_map/reduce_scatter | solution.py:336
  1149.3 653.3 %reduce-scatter.94.cloned.1.call-start = ((), (), s32[]{:S(2)}) async-start(), calls=%async_computation.69 | async-start | bytes 3342336
  1159.4 891.3 %reduce-scatter.86.cloned.1.call-start = ((), (), s32[]{:S(2)}) async-start(), calls=%async_computation.65 | async-start | bytes 26738688 | tf_op jit(solution)/shard_map/reduce_scatter | solution.py:366
  (108 other events, 747.9 us)
Sparse Core Ops, SparseCore 0:
  19.1 25.2 all-gather.12
  63.2 44.4 reduce-scatter.37
  112.9 22.5 all-gather.14
  146.9 44.4 reduce-scatter.39
  210.0 23.5 all-gather.16
  252.5 44.4 reduce-scatter.41
  300.8 22.5 all-gather.18
  334.9 44.4 reduce-scatter.43
  398.0 23.5 all-gather.20
  440.4 44.4 reduce-scatter.45
  488.7 22.5 all-gather.24
  513.4 22.5 all-gather.22
  549.2 31.3 reduce-scatter.47
  588.7 22.5 all-gather.26
  660.8 31.4 reduce-scatter.49
  717.8 21.6 all-gather.28
  752.2 31.3 reduce-scatter.51
  791.7 22.5 all-gather.30
  861.1 31.4 reduce-scatter.53
  917.0 21.7 all-gather.32
  951.4 31.4 reduce-scatter.55
  989.9 22.5 all-gather.34
  1015.0 44.4 reduce-scatter.59
  1065.9 31.3 reduce-scatter.57
  1101.0 61.5 reduce-scatter.91
  1164.8 42.8 reduce-scatter.73
  1209.8 43.1 reduce-scatter.75
  1255.5 43.1 reduce-scatter.77
  1301.0 43.1 reduce-scatter.79
  1346.4 43.1 reduce-scatter.81
  1392.0 43.1 reduce-scatter.83
  1439.3 56.6 reduce-scatter.89
  1499.4 56.3 reduce-scatter.87
  1558.2 20.7 reduce-scatter.67
  1581.3 19.8 reduce-scatter.69
  1604.0 19.9 reduce-scatter.71
  1626.2 33.4 reduce-scatter.61
  1662.2 34.2 reduce-scatter.63
  1698.7 34.2 reduce-scatter.65
  1737.3 65.1 reduce-scatter.93
  1807.8 242.8 reduce-scatter.85
where the time goes:
time: 2070 us; the launch traced here: 2060 us
  waiting for transfers between devices  1530 us (74%)
  matrix products  299 us (14%)
  other arithmetic  134 us (6%)
  local copies, waits for them, and re-layouts  53.5 us (3%)
    reduce_scatter x1, waiting for transfers between devices, body(): lax.psum_scatter(ada_grad[None], ('dp', 'tensor'), scatter_dimension=1, t...  247 us
    unnamed x45, waiting for transfers between devices  156 us
    reduce_scatter x3, waiting for transfers between devices, body(): lax.psum_scatter(weight_parts[3][None].astype(jnp.bfloat16), 'dp', scatte...  134 us
    reduce_scatter x3, waiting for transfers between devices, layer_forward(): lax.psum_scatter(contract_last(mixed_heads, attention_output_weight), 'te...  133 us
    reduce_scatter x3, waiting for transfers between devices, body(): lax.psum_scatter(weight_parts[2][None].astype(jnp.bfloat16), 'dp', scatte...  124 us
    reduce_scatter x3, waiting for transfers between devices, body(): lax.psum_scatter(weight_parts[0][None].astype(jnp.bfloat16), 'dp', scatte...  107 us
    reduce_scatter x3, waiting for transfers between devices, layer_backward(): lax.psum_scatter(contract_last(grad_hidden, first_mlp_weight).astype(jnp....  94.5 us
    reduce_scatter x3, waiting for transfers between devices, layer_forward(): lax.psum_scatter(contract_last(activated, second_mlp_weight), 'tensor', s...  89.2 us
  transfers between devices with their start and end apart: 45, of which 42 were waited for; matrix products, arithmetic and copies ran while one was open for 10% of the time, Pallas kernels for 0%

commit v1 on v0

v1 whole, which is shorter than its diff:
```python
import functools

import jax
import jax.numpy as jnp
from jax import lax
from jax.experimental import pallas as pl
from jax.experimental.pallas import tpu as pltpu
from jax.sharding import PartitionSpec as P

HD = 64
SLAB = 2 * HD
EXPO = HD ** (-0.5) * 1.4426950408889634
BF = jnp.bfloat16
F32 = jnp.float32
precise = lax.Precision.HIGHEST


def swap(block, bit):
    count = lax.axis_size("tensor")
    return lax.ppermute(block, "tensor", [(i, i ^ bit) for i in range(count)])


def tensor_sum(block):
    count = lax.axis_size("tensor")
    bit = 1
    while bit < count:
        block = block + swap(block, bit)
        bit *= 2
    return block


def call(kernel, ins, outs, scratch=(), token=None, flag=None, flops=0):
    vmem = pl.BlockSpec(memory_space=pltpu.VMEM)
    specs = [vmem] * len(ins)
    if flag is not None:
        ins = (flag, *ins)
        specs = [pl.BlockSpec(memory_space=pltpu.SMEM), *specs]
    body = kernel
    if token is not None:
        token = token if isinstance(token, tuple) else (token,)
        place = len(ins)
        ins = (*ins, *token)
        specs += [pl.BlockSpec(memory_space=pl.ANY)] * len(token)

        def body(*refs):
            kernel(*refs[:place], *refs[len(ins) :])

    return pl.pallas_call(
        body,
        in_specs=specs,
        out_specs=[vmem] * len(outs),
        out_shape=list(outs),
        scratch_shapes=list(scratch),
        compiler_params=pltpu.CompilerParams(vmem_limit_bytes=24 << 20),
        cost_estimate=pl.CostEstimate(flops=flops, bytes_accessed=0, transcendentals=0),
    )(*ins)


def like(rows, cols, kind):
    return jax.ShapeDtypeStruct((rows, cols), kind)


def dot_nn(left, right):
    return jnp.dot(left, right, preferred_element_type=F32)


def dot_nt(left, right):
    return lax.dot_general(left, right, (((1,), (1,)), ((), ())), preferred_element_type=F32)


def unit_rows(rows):
    center = rows - jnp.mean(rows, axis=-1, keepdims=True)
    spread = jnp.mean(center * center, axis=-1, keepdims=True)
    inverse = lax.rsqrt(spread + 1e-06)
    return center * inverse, inverse


def norm_back(unit, inverse, grad, factor):
    grad_unit = grad * (1.0 + factor)
    return inverse * (
        grad_unit
        - jnp.mean(grad_unit, axis=-1, keepdims=True)
        - unit * jnp.mean(grad_unit * unit, axis=-1, keepdims=True)
    )


def gelu_both(u):
    root = 0.7978845608028654
    square = u * u
    inner = root * (1.0 + 0.044715 * square)
    tanh = jnp.tanh(u * inner)
    half = 0.5 * (1.0 + tanh)
    slope = half + (0.5 * u) * (1.0 - tanh * tanh) * (root + (3.0 * 0.044715 * root) * square)
    return u * half, slope


def total(ref):
    return jnp.sum(ref, axis=0, keepdims=True)


def first_norm_kernel(rows_ref, mod_ref, out_ref):
    unit, _ = unit_rows(rows_ref[...].astype(F32))
    out_ref[...] = (unit * (1.0 + mod_ref[1:2]) + mod_ref[0:1]).astype(BF)


def triple_kernel(rows_ref, own_w_ref, other_w_ref, bias_ref, triple_ref, *send_refs):
    width = own_w_ref.shape[1]
    third = width // 3
    for group, w_ref in enumerate((own_w_ref, other_w_ref)):
        cols = slice(group * width, (group + 1) * width)
        part = (dot_nn(rows_ref[...], w_ref[...]) + bias_ref[:, cols]).astype(BF)
        triple_ref[:, cols] = part
        send_refs[1 - group][...] = part[:, third:]


def slabs(width):
    return [(group, first) for group in range(2) for first in range(0, width, SLAB)]


def key_blocks(near_ref, far_ref, away_near_ref, away_far_ref, group, first, width, which):
    here = group * 3 * width + which * width + first
    away = (which - 1) * width + first
    return [ref[:, here : here + SLAB] for ref in (near_ref, far_ref)] + [
        refs[group][:, away : away + SLAB] for refs in (away_near_ref, away_far_ref)
    ]


def sum_of(terms):
    return functools.reduce(lambda one, two: one + two, terms)


def attend_kernel(
    query_ref, near_ref, far_ref, an0_ref, an1_ref, af0_ref, af1_ref, own_w_ref, other_w_ref, mixed_ref, log_ref, out_ref
):
    away_near_ref, away_far_ref = (an0_ref, an1_ref), (af0_ref, af1_ref)
    block = mixed_ref.shape[0]
    width = mixed_ref.shape[1] // 2
    upper = lax.broadcasted_iota(jnp.int32, (SLAB, block), 0) >= HD
    for group, first in slabs(width):
        start = group * 3 * width + first
        queries = query_ref[:, start : start + SLAB].T
        tokens = (near_ref, far_ref, away_near_ref, away_far_ref, group, first, width)
        keys = key_blocks(*tokens, 1)
        values = [part.T for part in key_blocks(*tokens, 2)]
        outs = []
        for h in range(2):
            part = jnp.where(upper == (h == 1), queries, jnp.zeros_like(queries))
            scores = [dot_nn(key, part) for key in keys]
            peak = functools.reduce(jnp.maximum, [jnp.max(x, axis=0, keepdims=True) for x in scores])
            expo = [jnp.exp2((x - peak) * EXPO) for x in scores]
            weight = sum_of([total(x) for x in expo])
            out = sum_of(
                [dot_nn(value[h * HD : (h + 1) * HD], x.astype(BF)) for value, x in zip(values, expo)]
            )
            outs.append(out * (1.0 / weight))
            head = (group * width + first) // HD + h
            log_ref[head : head + 1, :] = peak * EXPO + jnp.log2(weight)
        at = group * width + first
        mixed_ref[:, at : at + SLAB] = jnp.concatenate(outs, 0).T.astype(BF)
    branch = dot_nt(mixed_ref[:, :width], own_w_ref[...]) + dot_nt(mixed_ref[:, width:], other_w_ref[...])
    out_ref[...] = branch.astype(out_ref.dtype)


def middle_kernel(keep_ref, far_ref, bias_ref, rows_ref, mod_ref, branch_ref, middle_ref, second_ref):
    branch = keep_ref[...] + far_ref[...].astype(F32) + bias_ref[...]
    middle = rows_ref[...].astype(F32) + mod_ref[2:3] * branch
    unit, _ = unit_rows(middle)
    branch_ref[...] = branch
    middle_ref[...] = middle
    second_ref[...] = (unit * (1.0 + mod_ref[4:5]) + mod_ref[3:4]).astype(BF)


def mlp_kernel(rows_ref, own_w1_ref, other_w1_ref, bias_ref, own_w2_ref, other_w2_ref, act_ref, slope_ref, out_ref):
    width = own_w1_ref.shape[1]
    tile = 256
    for group, w1_ref in enumerate((own_w1_ref, other_w1_ref)):
        for first in range(0, width, tile):
            cols = slice(group * width + first, group * width + first + tile)
            value, slope = gelu_both(dot_nn(rows_ref[...], w1_ref[:, first : first + tile]) + bias_ref[:, cols])
            act_ref[:, cols] = value.astype(BF)
            slope_ref[:, cols] = slope.astype(BF)
    feed = dot_nt(act_ref[:, :width], own_w2_ref[...]) + dot_nt(act_ref[:, width:], other_w2_ref[...])
    out_ref[...] = feed.astype(out_ref.dtype)


def layer_end_kernel(keep_ref, far_ref, bias_ref, middle_ref, mod_ref, feed_ref, out_ref):
    feed = keep_ref[...] + far_ref[...].astype(F32) + bias_ref[...]
    feed_ref[...] = feed
    out_ref[...] = (middle_ref[...] + mod_ref[5:6] * feed).astype(BF)


def grad_feed_kernel(grad_ref, feed_ref, mod_ref, out_ref, sums_ref):
    grad = grad_ref[...].astype(F32)
    out = (mod_ref[5:6] * grad).astype(BF)
    out_ref[...] = out
    sums_ref[0:1] = total(grad * feed_ref[...])
    sums_ref[1:2] = total(out.astype(F32))


def grad_mlp_kernel(rows_ref, own_w2_ref, other_w2_ref, slope_ref, own_w1_ref, other_w1_ref, hidden_ref, sums_ref, out_ref):
    width = own_w2_ref.shape[1]
    tile = 256
    for group, w2_ref in enumerate((own_w2_ref, other_w2_ref)):
        for first in range(0, width, tile):
            cols = slice(group * width + first, group * width + first + tile)
            grad = dot_nn(rows_ref[...], w2_ref[:, first : first + tile])
            grad = (grad * slope_ref[:, cols].astype(F32)).astype(BF)
            hidden_ref[:, cols] = grad
            sums_ref[:, cols] = total(grad.astype(F32))
    second = dot_nt(hidden_ref[:, :width], own_w1_ref[...]) + dot_nt(hidden_ref[:, width:], other_w1_ref[...])
    out_ref[...] = second.astype(out_ref.dtype)


def grad_middle_kernel(keep_ref, far_ref, middle_ref, branch_ref, grad_ref, mod_ref, out_ref, rows_ref, sums_ref):
    grad = keep_ref[...] + far_ref[...].astype(F32)
    unit, inverse = unit_rows(middle_ref[...])
    sums_ref[0:1] = total(grad)
    sums_ref[1:2] = total(grad * unit)
    grad = norm_back(unit, inverse, grad, mod_ref[4:5]) + grad_ref[...].astype(F32)
    out_ref[...] = grad
    sums_ref[2:3] = total(grad * branch_ref[...])
    rows = (mod_ref[2:3] * grad).astype(BF)
    rows_ref[...] = rows
    sums_ref[3:4] = total(rows.astype(F32))


def grad_attend_kernel(last, *refs):
    rows_ref, own_w_ref, other_w_ref, query_ref, near_ref, far_ref = refs[:6]
    away_near_ref, away_far_ref = refs[6:8], refs[8:10]
    mixed_ref, log_ref = refs[10:12]
    if last:
        held_ref, out_ref, keep_ref, send_ref, grad_ref = refs[12:]
    else:
        out_ref, keep_ref, grad_ref = refs[12:]
    block = mixed_ref.shape[0]
    width = mixed_ref.shape[1] // 2
    scale = HD ** (-0.5)
    for group, w_ref in enumerate((own_w_ref, other_w_ref)):
        grad_ref[:, group * width : (group + 1) * width] = dot_nn(rows_ref[...], w_ref[...]).astype(BF)
    upper = lax.broadcasted_iota(jnp.int32, (SLAB, block), 0) >= HD
    right = lax.broadcasted_iota(jnp.int32, (block, SLAB), 1) >= HD
    for group, first in slabs(width):
        at = group * width + first
        start = group * 3 * width + first
        queries = query_ref[:, start : start + SLAB]
        grad = grad_ref[:, at : at + SLAB]
        queries_t, grad_t = queries.T, grad.T
        tokens = (near_ref, far_ref, away_near_ref, away_far_ref, group, first, width)
        inner = grad_t.astype(F32) * mixed_ref[:, at : at + SLAB].T.astype(F32)
        none = jnp.zeros_like(queries_t)
        none_r = jnp.zeros_like(queries)
        heads = []
        for h in range(2):
            heads.append(
                (
                    jnp.where(upper == (h == 1), queries_t, none),
                    jnp.where(upper == (h == 1), grad_t, none),
                    jnp.where(right == (h == 1), queries, none_r),
                    jnp.where(right == (h == 1), grad, none_r),
                    total(inner[h * HD : (h + 1) * HD]),
                )
            )
        outs = [None, None]
        for place, (keys, values) in enumerate(zip(key_blocks(*tokens, 1), key_blocks(*tokens, 2))):
            keys_t = keys.T
            key_terms, value_terms = [], []
            for h, (query_t, grad_out_t, query, grad_out, delta) in enumerate(heads):
                head = at // HD + h
                probs = jnp.exp2(dot_nn(keys, query_t) * EXPO - log_ref[head : head + 1, :])
                grad_s = (probs * (dot_nn(values, grad_out_t) - delta)).astype(BF)
                value_terms.append(dot_nn(probs.astype(BF), grad_out))
                key_terms.append(dot_nn(grad_s, query))
                out = dot_nn(keys_t[h * HD : (h + 1) * HD], grad_s)
                outs[h] = out if outs[h] is None else outs[h] + out
            for which, term in enumerate((sum_of(key_terms) * scale, sum_of(value_terms))):
                rows = slice(place * block, (place + 1) * block)
                cols = slice(group * 2 * width + which * width + first, group * 2 * width + which * width + first + SLAB)
                if not last:
                    keep_ref[rows, cols] = term
                elif place < 2:
                    keep_ref[rows, cols] = held_ref[rows, cols] + term
                else:
                    there = slice((place - 2) * block, (place - 1) * block)
                    turned = (1 - group) * 2 * width + which * width + first
                    send_ref[there, turned : turned + SLAB] = (held_ref[rows, cols] + term).astype(BF)
        out_ref[:, at : at + SLAB] = (jnp.concatenate(outs, 0).T * scale).astype(BF)


def grad_normed_kernel(part, query_ref, keep_ref, got_ref, own_w_ref, other_w_ref, triple_ref, out_ref, sums_ref):
    size, width = query_ref.shape[0], query_ref.shape[1] // 2
    rows = slice(part * size, (part + 1) * size)
    for group in range(2):
        at = group * 3 * width
        cols = slice(group * 2 * width, (group + 1) * 2 * width)
        triple_ref[:, at : at + width] = query_ref[:, group * width : (group + 1) * width]
        triple_ref[:, at + width : at + 3 * width] = (
            keep_ref[rows, cols] + got_ref[rows, cols].astype(F32)
        ).astype(BF)
    out = dot_nt(triple_ref[:, : 3 * width], own_w_ref[...]) + dot_nt(triple_ref[:, 3 * width :], other_w_ref[...])
    out_ref[...] = out.astype(out_ref.dtype)
    sums_ref[...] = total(triple_ref[...].astype(F32))


def grad_rows_kernel(keep_ref, far_ref, rows_ref, middle_ref, mod_ref, out_ref, sums_ref):
    grad = keep_ref[...] + far_ref[...].astype(F32)
    unit, inverse = unit_rows(rows_ref[...].astype(F32))
    sums_ref[0:1] = total(grad)
    sums_ref[1:2] = total(grad * unit)
    out_ref[...] = (norm_back(unit, inverse, grad, mod_ref[1:2]) + middle_ref[...]).astype(BF)


CHUNKS = 4


def weight_kernel(lefts, rights, wanted, flag_ref, *refs):
    left_refs, right_refs = refs[:lefts], refs[lefts : lefts + rights]
    rest = refs[lefts + rights : -2]
    left_all, right_all = refs[-2:]
    out_refs = rest[-1 - CHUNKS :]

    @pl.when(flag_ref[0] == wanted)
    def _():
        at = 0
        for ref in left_refs:
            left_all[:, at : at + ref.shape[0]] = ref[...].T
            at += ref.shape[0]
        at = 0
        for ref in right_refs:
            right_all[at : at + ref.shape[0]] = ref[...]
            at += ref.shape[0]
        rows, width = out_refs[0].shape
        tile = rows // CHUNKS
        for i in range(CHUNKS):
            left = left_all[i * tile : (i + 1) * tile]
            out_refs[0][i * tile : (i + 1) * tile] = dot_nn(left, right_all[:, :width]).astype(BF)
            out_refs[i + 1][...] = dot_nn(left, right_all[:, width:]).astype(BF)

    @pl.when(flag_ref[0] != wanted)
    def _():
        for i, out_ref in enumerate(out_refs):
            out_ref[...] = jnp.zeros_like(out_ref) if len(rest) == len(out_refs) else rest[i][...]


def weight_grad(operands, section, old, token):
    lefts, rights = operands
    tokens = sum(x.shape[0] for x in lefts)
    rows, cols = lefts[0].shape[1], rights[0].shape[1]
    return call(
        functools.partial(weight_kernel, len(lefts), len(rights), 1 if old is None else 0),
        (*lefts, *rights) if old is None else (*lefts, *rights, *old),
        [like(rows, cols // 2, BF)] + [like(rows // CHUNKS, cols // 2, BF)] * CHUNKS,
        scratch=[pltpu.VMEM((rows, tokens), BF), pltpu.VMEM((tokens, cols), BF)],
        token=token,
        flag=section,
    )


def add_kernel(one_ref, *refs):
    out_ref = refs[-1]
    size = out_ref.shape[0] // CHUNKS
    for i, two_ref in enumerate(refs[:-1]):
        rows = slice(i * size, (i + 1) * size)
        out_ref[rows] = (one_ref[rows].astype(F32) + two_ref[...].astype(F32)).astype(BF)


def tied(block, token):
    if token is None:
        return block
    token = token if isinstance(token, tuple) else (token,)
    return lax.optimization_barrier((block, *token))[0]


def forward_steps(rows, mod, weights):
    w_qkv, b_qkv, w_out, b_out, w_fc1, b_fc1, w_fc2 = weights
    size, width = rows.shape
    local = w_out[0].shape[1]
    hidden = w_fc1[0].shape[1]
    token = yield None, ()
    (normed,) = call(first_norm_kernel, (rows, mod), [like(size, width, BF)], token=token)
    normed_far = swap(normed, 2)
    triple_outs = [like(size, 6 * local, BF), like(size, 2 * local, BF), like(size, 2 * local, BF)]
    triple, *sends = call(triple_kernel, (normed, *w_qkv, b_qkv), triple_outs)
    away = [swap(send, 1) for send in sends]
    token = yield triple, ()
    normed_far = tied(normed_far, token)
    triple_far, *sends = call(triple_kernel, (normed_far, *w_qkv, b_qkv), triple_outs, token=token)
    tokens = (triple, triple_far, *away, *(swap(send, 1) for send in sends))
    outs = [like(size, 2 * local, BF), like(2 * local // HD, size, F32)]
    mixed_far, log_far, send = call(
        attend_kernel, (triple_far, *tokens, *w_out), [*outs, like(size, width, BF)], token=token
    )
    far = swap(send, 2)
    mixed, log, keep = call(
        attend_kernel, (triple, *tokens, *w_out), [*outs, like(size, width, F32)], token=send
    )
    token = yield keep, ()
    branch, middle, second = call(
        middle_kernel,
        (keep, tied(far, token), b_out[0:1], rows, mod),
        [like(size, width, F32), like(size, width, F32), like(size, width, BF)],
        token=token,
    )
    second_far = swap(second, 2)
    outs = [like(size, 2 * hidden, BF), like(size, 2 * hidden, BF)]
    act, slope, keep = call(mlp_kernel, (second, *w_fc1, b_fc1, *w_fc2), [*outs, like(size, width, F32)])
    token = yield keep, ()
    second_far = tied(second_far, token)
    act_far, slope_far, send = call(
        mlp_kernel, (second_far, *w_fc1, b_fc1, *w_fc2), [*outs, like(size, width, BF)], token=token
    )
    far = swap(send, 2)
    token = yield send, ()
    feed, result = call(
        layer_end_kernel,
        (keep, tied(far, token), b_out[1:2], middle, mod),
        [like(size, width, F32), like(size, width, BF)],
        token=token,
    )
    state = (
        rows, (normed, normed_far), tokens, (mixed, mixed_far), (log, log_far), branch, middle,
        (second, second_far), (act, act_far), (slope, slope_far), feed,
    )
    return result, state


def backward_steps(grad, mod, weights, state, flops=0):
    w_qkv, b_qkv, w_out, b_out, w_fc1, b_fc1, w_fc2 = weights
    rows, normed, tokens, mixed, logs, branch, middle, second, acts, slopes, feed = state
    size, width = rows.shape
    local = w_out[0].shape[1]
    hidden = w_fc1[0].shape[1]
    token = yield None, ()
    feed_rows, sums_feed = call(
        grad_feed_kernel, (grad, feed, mod), [like(size, width, BF), like(2, width, F32)], token=token
    )
    feed_far = swap(feed_rows, 2)
    outs = [like(size, 2 * hidden, BF), like(1, 2 * hidden, F32)]
    hidden_near, sums_near, keep = call(
        grad_mlp_kernel, (feed_rows, *w_fc2, slopes[0], *w_fc1), [*outs, like(size, width, F32)]
    )
    token = yield keep, ()
    feed_far = tied(feed_far, token)
    hidden_far, sums_far, send = call(
        grad_mlp_kernel, (feed_far, *w_fc2, slopes[1], *w_fc1), [*outs, like(size, width, BF)], token=token
    )
    far = swap(send, 2)
    token = yield send, ((3, (feed_rows, feed_far), acts),)
    grad_middle, branch_rows, sums_middle = call(
        grad_middle_kernel,
        (keep, tied(far, token), middle, branch, grad, mod),
        [like(size, width, F32), like(size, width, BF), like(4, width, F32)],
        token=token,
    )
    branch_far = swap(branch_rows, 2)
    scratch = [pltpu.VMEM((size, 2 * local), BF)]
    query_near, held = call(
        functools.partial(grad_attend_kernel, False),
        (branch_rows, *w_out, tokens[0], *tokens, mixed[0], logs[0]),
        [like(size, 2 * local, BF), like(4 * size, 4 * local, F32)],
        scratch=scratch,
    )
    token = yield query_near, ((2, second, (hidden_near, hidden_far)),)
    branch_far = tied(branch_far, token)
    query_far, kept, send = call(
        functools.partial(grad_attend_kernel, True),
        (branch_far, *w_out, tokens[1], *tokens, mixed[1], logs[1], held),
        [like(size, 2 * local, BF), like(2 * size, 4 * local, F32), like(2 * size, 4 * local, BF)],
        scratch=scratch,
        token=token,
        flops=flops,
    )
    got = swap(send, 1)
    token = yield kept, ((1, (branch_rows, branch_far), mixed),)
    outs = [like(size, 6 * local, BF), like(size, width, BF), like(1, 6 * local, F32)]
    triple_far, send, sums_triple_far = call(
        functools.partial(grad_normed_kernel, 1), (query_far, kept, got, *w_qkv), outs, token=token
    )
    far = swap(send, 2)
    outs[1] = like(size, width, F32)
    triple_near, keep, sums_triple = call(
        functools.partial(grad_normed_kernel, 0), (query_near, kept, got, *w_qkv), outs, token=send
    )
    token = yield keep, ((0, normed, (triple_near, triple_far)),)
    grad_rows, sums_rows = call(
        grad_rows_kernel,
        (keep, tied(far, token), rows, grad_middle, mod),
        [like(size, width, BF), like(2, width, F32)],
        token=token,
    )
    grad_mod = jnp.concatenate(
        [sums_rows, sums_middle[2:3], sums_middle[0:2], sums_feed[0:1]], 0
    ).reshape(1, -1)
    sums = (
        (sums_triple + sums_triple_far)[0],
        (sums_near + sums_far)[0],
        jnp.concatenate([sums_middle[3:4], sums_feed[1:2]], 0),
    )
    return grad_rows, grad_mod, sums


def chain_steps(ends, mod, weights, flops):
    sent, state_one = yield from forward_steps(ends, mod, weights)
    arrived = lax.ppermute(sent, "section", [(0, 1)])
    yield sent, ()
    out, state_two = yield from forward_steps(arrived, mod, weights)
    yield out, ()
    back_two = yield from backward_steps(ends, mod, weights, state_two)
    arrived = lax.ppermute(back_two[0], "section", [(1, 0)])
    yield back_two[0], ()
    back_one = yield from backward_steps(arrived, mod, weights, state_one, flops)
    yield back_one[0], ()
    return out, back_two, back_one


def side_by_side(chains, section):
    results = [None] * len(chains)
    products, sums, pending = {}, {}, []
    after = {0: 2}
    for chain in chains:
        next(chain)
    token = None
    while pending or any(result is None for result in results):
        ready = {}
        if any(which == 0 for which, _, _ in pending):
            token = (token, sums[3])
        for i, chain in enumerate(chains):
            try:
                token, made = chain.send(token)
            except StopIteration as stop:
                results[i] = stop.value
                continue
            for which, lefts, rights in made:
                both = ready.setdefault(which, ([], []))
                both[0].extend(lefts)
                both[1].extend(rights)
        for which, keep, got in pending:
            if which in after:
                token = (token, sums[after[which]])
            (token,) = call(add_kernel, (keep, *got), [like(*keep.shape, BF)], token=token)
            sums[which] = lax.psum_scatter(token, "dp", scatter_dimension=0, tiled=True)
        pending = []
        for which, operands in ready.items():
            old = products.get(which)
            products[which] = keep, *sends = weight_grad(operands, section, old, token)
            token = keep
            if old is not None:
                pending.append((which, keep, [swap(send, 1) for send in sends]))
    return results, sums


def body(
    boundary,
    conditioning,
    query_key_value_weight,
    query_value_bias,
    attention_output_weight,
    output_biases,
    first_mlp_weight,
    first_mlp_bias,
    second_mlp_weight,
    w_ada,
    ada_bias,
):
    leading = lax.axis_index("section") == 0
    ends = boundary[0]
    width, _, local = query_key_value_weight.shape[1:]
    tensor_no = lax.axis_index("tensor")
    dp_no = lax.axis_index("dp")
    tensor_count = lax.axis_size("tensor")
    dp_count = lax.axis_size("dp")
    w_qkv = jnp.concatenate([query_key_value_weight[0, :, i] for i in range(3)], 1)
    qv = query_value_bias[0].astype(F32)
    b_qkv = jnp.concatenate([qv[0], jnp.zeros_like(qv[0]), qv[1]])[None]
    w_out, w_fc1, w_fc2 = attention_output_weight[0], first_mlp_weight[0], second_mlp_weight[0]
    hidden = w_fc1.shape[1]
    vectors = jnp.concatenate([b_qkv, first_mlp_bias.astype(F32)], 1)
    other = swap(vectors, 1)
    weights = (
        (w_qkv, swap(w_qkv, 1)),
        jnp.concatenate([b_qkv, other[:, : 3 * local]], 1),
        (w_out, swap(w_out, 1)),
        output_biases[0].astype(F32),
        (w_fc1, swap(w_fc1, 1)),
        jnp.concatenate([vectors[:, 3 * local :], other[:, 3 * local :]], 1),
        (w_fc2, swap(w_fc2, 1)),
    )
    ada_weight = w_ada[0]
    cond_vals = conditioning.astype(F32)
    cond_act = jax.nn.silu(cond_vals).astype(BF)
    mods = (dot_nn(cond_act, ada_weight) + ada_bias[0].astype(F32)).reshape(2, 6, width)

    section = lax.axis_index("section").astype(jnp.int32).reshape(1)
    chains, sums = side_by_side(
        [chain_steps(ends[b], mods[b], weights, b * 10**11) for b in range(ends.shape[0])], section
    )
    outs = [chain[0] for chain in chains]
    backs_two = [chain[1] for chain in chains]
    backs_one = [chain[2] for chain in chains]

    g_qkv, g_proj, g_fc1, g_fc2 = (sums[i].astype(F32) for i in range(4))
    g_qkv = jnp.stack([g_qkv[:, i * local : (i + 1) * local] for i in range(3)], 1)

    pick = lambda one, two: jnp.where(leading, one, two)
    grad_mods = jnp.concatenate(
        [pick(one[1], two[1]) for one, two in zip(backs_one, backs_two)], 0
    )
    owned_triple, owned_hidden, partial = (
        pick(
            backs_one[0][2][i] + backs_one[1][2][i],
            backs_two[0][2][i] + backs_two[1][2][i],
        )
        for i in range(3)
    )
    def placed(vector):
        size = vector.shape[0] // 2
        full = jnp.zeros((tensor_count * size,), F32)
        for part, where in ((vector[:size], tensor_no), (vector[size:], tensor_no ^ 1)):
            full = lax.dynamic_update_slice(full, part, (where * size,))
        return full

    span = 3 * local
    queries = jnp.concatenate([owned_triple[:local], owned_triple[span : span + local]])
    values = jnp.concatenate([owned_triple[2 * local : span], owned_triple[span + 2 * local :]])
    flat = tensor_sum(
        jnp.concatenate(
            [
                grad_mods.reshape(-1),
                placed(queries),
                placed(values),
                placed(owned_hidden),
                partial.reshape(-1),
            ]
        )
    )
    grad_mods = flat[: 12 * width].reshape(2, 6 * width)
    biases = flat[12 * width :]
    everything = lax.all_gather(
        jnp.concatenate([grad_mods.reshape(-1), biases, cond_act.astype(F32).reshape(-1)]), "dp", axis=0
    )
    mods_end = 12 * width
    all_mods = everything[:, :mods_end].reshape(2 * dp_count, 6 * width)
    all_acts = everything[:, -2 * width :].reshape(2 * dp_count, width)
    biases = jnp.sum(everything[:, mods_end : -2 * width], axis=0)
    place = dp_no * tensor_count + tensor_no
    shares = dp_count * tensor_count

    def own_share(vector):
        size = vector.shape[0] // shares
        return lax.dynamic_slice(vector, (place * size,), (size,))[None]

    hidden_all = biases.shape[0] - 4 * width
    g_qv_bias = own_share(biases[: 2 * width])
    g_fc1_bias = own_share(biases[2 * width : 2 * width + hidden_all])
    g_out_bias = own_share(biases[2 * width + hidden_all :])
    g_ada_bias = own_share(jnp.sum(all_mods, axis=0))
    share = width // shares
    act_share = lax.dynamic_slice(all_acts, (0, place * share), (all_acts.shape[0], share))
    g_ada = lax.dot_general(
        act_share, all_mods, (((0,), (0,)), ((), ())), precision=precise, preferred_element_type=F32
    )

    cut = 6 * width // tensor_count
    mods_cut = lax.dynamic_slice(grad_mods, (0, tensor_no * cut), (2, cut))
    ada_cut = lax.dynamic_slice(ada_weight, (0, tensor_no * cut), (width, cut))
    back_cond = lax.dot_general(
        mods_cut,
        ada_cut.astype(F32),
        (((1,), (1,)), ((), ())),
        precision=precise,
        preferred_element_type=F32,
    )
    back_cond = back_cond + lax.ppermute(back_cond, "section", [(0, 1), (1, 0)])
    cond_total = tensor_sum(back_cond)
    sig = jax.nn.sigmoid(cond_vals)
    cond_grad = cond_total * sig * (1.0 + cond_vals * (1.0 - sig))

    rows_out = jnp.stack([pick(back[0], out) for back, out in zip(backs_one, outs)])[None]
    return (
        rows_out,
        cond_grad,
        g_qkv[None],
        g_qv_bias,
        g_proj[None],
        g_out_bias,
        g_fc1[None],
        g_fc1_bias,
        g_fc2[None],
        g_ada[None],
        g_ada_bias,
    )


def solution(mesh):
    in_specs = (
        P("section", "dp", "tensor", None),
        P("dp", None),
        P("section", None, None, "tensor"),
        P("section", None, "tensor"),
        P("section", None, "tensor"),
        P("section", None, None),
        P("section", None, "tensor"),
        P("section", "tensor"),
        P("section", None, "tensor"),
        P("section", None, None),
        P("section", None),
    )
    out_specs = (
        P("section", "dp", "tensor", None),
        P("dp", None),
        P("section", "dp", None, "tensor"),
        P("section", ("dp", "tensor")),
        P("section", "dp", "tensor"),
        P("section", ("dp", "tensor")),
        P("section", "dp", "tensor"),
        P("section", ("dp", "tensor")),
        P("section", "dp", "tensor"),
        P("section", ("dp", "tensor"), None),
        P("section", ("dp", "tensor")),
    )
    return jax.shard_map(body, mesh=mesh, in_specs=in_specs, out_specs=out_specs, check_vma=False)
```

time: 2070 us -> 631 us (0.30)
  waiting for transfers between devices: 1530 us -> 97.7 us
  Pallas kernels: 0 us -> 302 us
  matrix products: 299 us -> 13.5 us
  other arithmetic: 134 us -> 9.26 us
  starting transfers between devices: 14.1 us -> 64 us
  local copies, waits for them, and re-layouts: 53.5 us -> 97.6 us
    reduce_scatter x25 -> x4, waiting for transfers between devices: 1060 us -> 5.87 us  [side_by_side(): sums[which] = lax.psum_scatter(token, 'dp', scatter_dimension=0, tiled=True)]
    pallas_call x0 -> x84, Pallas kernels: none -> 302 us  [call(): pl.pallas_call(body, in_specs=specs, out_specs=[vmem] * len(outs), out_sh...]
    dot_general x75 -> x3, matrix products: 299 us -> 13.5 us  [the longest x1 6.31 us: dot_nn(): return jnp.dot(left, right, preferred_element_type=F32)]
    all_gather x12 -> x0, waiting for transfers between devices: 261 us -> none  [the longest x3 72.6 us: layer_forward(): normed = lax.all_gather(normed_rows, 'tensor', axis=0, tiled=True)]
    unnamed x45 -> x4, waiting for transfers between devices: 156 us -> 0.07 us
    reduce_sum x40 -> x2, other arithmetic: 68.7 us -> 0.12 us  [the longest x1 0.07 us: body(): biases = jnp.sum(everything[:, mods_end:-2 * width], axis=0)]
    unnamed x266 -> x642, local copies, waits for them, and re-layouts: 34.3 us -> 89.9 us
    ppermute x4 -> x82, starting transfers between devices: 9.37 us -> 63.9 us  [the longest x77 52.4 us: swap(): return lax.ppermute(block, 'tensor', [(i, i ^ bit) for i in range(count)])]
  transfers between devices with their start and end apart: 45 -> 86, of which waited for: 42 -> 33; matrix products, arithmetic and copies ran while one was open for 10% -> 4% of each run, Pallas kernels for 0% -> 49%
where the time goes in v1:
time: 631 us; the launch traced here: 620 us
  Pallas kernels  302 us (48%)
  waiting for transfers between devices  97.7 us (15%)
  local copies, waits for them, and re-layouts  97.6 us (15%)
  starting transfers between devices  64 us (10%)
  between operations  18.1 us (3%)
  blocking collectives  18 us (3%)
  matrix products  13.5 us (2%)
  other arithmetic  9.26 us (1%)
    pallas_call x84, Pallas kernels, call(): pl.pallas_call(body, in_specs=specs, out_specs=[vmem] * len(outs), out_sh...  302 us
    unnamed x642, local copies, waits for them, and re-layouts  89.9 us
    ppermute x77, waiting for transfers between devices, swap(): return lax.ppermute(block, 'tensor', [(i, i ^ bit) for i in range(count)])  68.4 us
    ppermute x77, starting transfers between devices, swap(): return lax.ppermute(block, 'tensor', [(i, i ^ bit) for i in range(count)])  52.4 us
    all_gather x1, blocking collectives, body(): lax.all_gather(jnp.concatenate([grad_mods.reshape(-1), biases, cond_act.a...  18 us
    ppermute x2, waiting for transfers between devices, chain_steps(): arrived = lax.ppermute(back_two[0], 'section', [(1, 0)])  15 us
  transfers between devices with their start and end apart: 86, of which 33 were waited for; matrix products, arithmetic and copies ran while one was open for 4% of the time, Pallas kernels for 49%

profile of v1, /device:TPU:0, one launch (start us, length us, event | category | flops | bytes accessed | tf_op | source)
XLA Modules:
  0.0 619.9 jit_solution(9570234328798958062)
XLA Ops:
  10.5 6.3 %fusion.2 = f32[2,6144]{1,0:T(2,128)S(1)} fusion(bf16[1,1024,6144]{2,1,0:T(8,128)(2,1)} %param.20, f32[6144]{0:T(1024)S(1)} %bitcast.138, bf16[2,1024]{1,0:T(2,128)(2,1)S(1)} %copy-done.311), kind=kOutput, calls=%fused_computation.3 | convolution fusion | flops 25190400 | bytes 12660736 | tf_op jit(solution)/shard_map/dot_general | solution.py:64
  23.8 4.0 collective-permute-done.1
  28.0 3.1 shard_map.195
  31.5 3.1 shard_map.197
  35.8 3.0 shard_map.198
  43.2 5.2 shard_map.199
  49.2 4.1 collective-permute-done.9.refs_0_.refs_4_
  55.1 5.6 shard_map.200
  66.3 5.2 shard_map.202
  72.7 5.4 shard_map.203
  80.6 5.7 shard_map.205
  91.2 5.7 shard_map.207
  98.3 6.0 shard_map.208
  109.0 6.3 %shard_map.209 = (bf16[256,2048]{1,0:T(8,128)(2,1)S(1)}, bf16[256,2048]{1,0:T(8,128)(2,1)S(1)}, bf16[256,1024]{1,0:T(8,128)(2,1)S(1)}) custom-call(bf16[256,1024]{1,0:T(8,128)(2,1)S(1)} %collective-permute-done.19.refs_0_.refs_4_, bf16[1024,1024]{1,0:T(8,128)(2,1)S(1)} %bitcast.90, bf16[1024,1024]{1,0:T(8,128)(2,1)} %collective-permute-done.14.other_w1_ref.refs_2_.refs_5_, ...), custom_call_target="tpu_custom_call" | custom-call | tf_op jit(solution)/shard_map/pallas_call | solution.py:48
  116.5 4.6 collective-permute-done.18.refs_1_
  121.4 3.4 collective-permute-start.20
  124.8 6.4 %collective-permute-done.22.refs_1_ = bf16[256,1024]{1,0:T(8,128)(2,1)S(1)} collective-permute-done((bf16[256,1024]{1,0:T(8,128)(2,1)S(1)}, bf16[256,1024]{1,0:T(8,128)(2,1)S(1)}, u32[]{:S(2)}, u32[]{:S(2)}) %collective-permute-start.22) | collective-permute-done | bytes 524320 | tf_op jit(solution)/shard_map/ppermute | solution.py:20
  132.5 3.4 collective-permute-start.23
  139.9 6.3 %collective-permute-done.23.refs_0_.refs_3_.refs_2_ = bf16[256,1024]{1,0:T(8,128)(2,1)S(1)} collective-permute-done((bf16[256,1024]{1,0:T(8,128)(2,1)S(1)}, bf16[256,1024]{1,0:T(8,128)(2,1)S(1)}, u32[]{:S(2)}, u32[]{:S(2)}) %collective-permute-start.23) | collective-permute-done | bytes 524320 | tf_op jit(solution)/shard_map/ppermute | solution.py:503
  150.6 3.3 shard_map.216
  155.9 5.2 shard_map.217
  161.9 5.4 shard_map.218
  168.1 3.1 shard_map.219
  173.4 5.2 shard_map.220
  180.8 5.2 shard_map.221
  189.7 6.1 shard_map.223
  200.9 5.7 shard_map.225
  209.0 5.9 shard_map.226
  216.7 3.6 collective-permute-done.37.refs_0_.refs_4_
  220.2 5.9 shard_map.227
  234.3 4.9 shard_map.230
  239.2 3.5 collective-permute-done.39.refs_1_
  245.5 4.7 shard_map.233
  250.3 3.6 collective-permute-done.38.refs_0_.refs_2_
  254.0 5.7 shard_map.234
  265.2 5.8 shard_map.235
  288.1 8.2 %shard_map.238 = (bf16[256,512]{1,0:T(8,128)(2,1)S(1)}, f32[1024,1024]{1,0:T(8,128)S(1)}) custom-call(bf16[256,1024]{1,0:T(8,128)(2,1)S(1)} %get-tuple-element.359.refs_0_.refs_1_, bf16[1024,256]{1,0:T(8,128)(2,1)S(1)} %bitcast.129, bf16[1024,256]{1,0:T(8,128)(2,1)S(1)} %collective-permute-done.7.refs_8_.refs_2_, bf16[256,1536]{1,0:T(8,128)(2,1)S(1)} %copy-done.9, ...), custom_call_target="tpu_custom_call" | custom-call | tf_op jit(solution)/shard_map/pallas_call | solution.py:48
  300.5 8.6 %shard_map.240 = (bf16[256,512]{1,0:T(8,128)(2,1)S(1)}, f32[1024,1024]{1,0:T(8,128)S(1)}) custom-call(bf16[256,1024]{1,0:T(8,128)(2,1)S(1)} %get-tuple-element.369.refs_0_.refs_3_, bf16[1024,256]{1,0:T(8,128)(2,1)S(1)} %bitcast.130, bf16[1024,256]{1,0:T(8,128)(2,1)S(1)} %collective-permute-done.7.refs_8_.refs_2_, bf16[256,1536]{1,0:T(8,128)(2,1)S(1)} %copy-done.5, ...), custom_call_target="tpu_custom_call" | custom-call | tf_op jit(solution)/shard_map/pallas_call | solution.py:48
  313.5 8.2 %shard_map.242 = (bf16[256,512]{1,0:T(8,128)(2,1)S(1)}, f32[512,1024]{1,0:T(8,128)S(1)}, bf16[512,1024]{1,0:T(8,128)(2,1)S(1)}) custom-call(bf16[256,1024]{1,0:T(8,128)(2,1)S(1)} %collective-permute-done.42.refs_0_.refs_2_, bf16[1024,256]{1,0:T(8,128)(2,1)S(1)} %bitcast.131, bf16[1024,256]{1,0:T(8,128)(2,1)S(1)} %collective-permute-done.7.refs_8_.refs_2_, ...), custom_call_target="tpu_custom_call" | custom-call | tf_op jit(solution)/shard_map/pallas_call | solution.py:48
  321.8 8.6 %shard_map.243 = (bf16[256,512]{1,0:T(8,128)(2,1)S(1)}, f32[512,1024]{1,0:T(8,128)S(1)}, bf16[512,1024]{1,0:T(8,128)(2,1)S(1)}) custom-call(bf16[256,1024]{1,0:T(8,128)(2,1)S(1)} %collective-permute-done.45.refs_0_.refs_4_, bf16[1024,256]{1,0:T(8,128)(2,1)S(1)} %bitcast.132, bf16[1024,256]{1,0:T(8,128)(2,1)S(1)} %collective-permute-done.7.refs_8_.refs_2_, ...), custom_call_target="tpu_custom_call" | custom-call | tf_op jit(solution)/shard_map/pallas_call | solution.py:48
  331.7 3.2 shard_map.245
  346.6 3.2 collective-permute-done.46.refs_1_
  353.0 7.2 %collective-permute-done.50.refs_1_ = bf16[256,1024]{1,0:T(8,128)(2,1)S(1)} collective-permute-done((bf16[256,1024]{1,0:T(8,128)(2,1)S(1)}, bf16[256,1024]{1,0:T(8,128)(2,1)S(1)}, u32[]{:S(2)}, u32[]{:S(2)}) %collective-permute-start.50) | collective-permute-done | bytes 524320 | tf_op jit(solution)/shard_map/ppermute | solution.py:20
  362.5 12.2 %collective-permute-done.48.grad_ref.refs_4_ = bf16[256,1024]{1,0:T(8,128)(2,1)S(1)} collective-permute-done((bf16[256,1024]{1,0:T(8,128)(2,1)S(1)}, bf16[256,1024]{1,0:T(8,128)(2,1)S(1)}, u32[]{:S(2)}, u32[]{:S(2)}) %collective-permute-start.48) | collective-permute-done | bytes 524320 | tf_op jit(solution)/shard_map/ppermute | solution.py:508
  376.1 4.8 shard_map.252
  386.1 4.8 shard_map.255
  391.0 5.1 shard_map.256
  398.6 4.9 shard_map.257
  405.1 4.8 shard_map.258
  413.9 6.9 %collective-permute-done.59.refs_1_ = bf16[256,1024]{1,0:T(8,128)(2,1)S(1)} collective-permute-done((bf16[256,1024]{1,0:T(8,128)(2,1)S(1)}, bf16[256,1024]{1,0:T(8,128)(2,1)S(1)}, u32[]{:S(2)}, u32[]{:S(2)}) %collective-permute-start.59) | collective-permute-done | bytes 524320 | tf_op jit(solution)/shard_map/ppermute | solution.py:20
  422.3 9.3 %shard_map.260 = (bf16[256,512]{1,0:T(8,128)(2,1)S(1)}, f32[1024,1024]{1,0:T(8,128)S(1)}) custom-call(bf16[256,1024]{1,0:T(8,128)(2,1)} %get-tuple-element.429.refs_0_.refs_1_, bf16[1024,256]{1,0:T(8,128)(2,1)S(1)} %bitcast.133, bf16[1024,256]{1,0:T(8,128)(2,1)S(1)} %collective-permute-done.7.refs_8_.refs_2_, bf16[256,1536]{1,0:T(8,128)(2,1)S(1)} %copy-done.7, ...), custom_call_target="tpu_custom_call" | custom-call | tf_op jit(solution)/shard_map/pallas_call | solution.py:48
  437.3 9.6 %shard_map.262 = (bf16[256,512]{1,0:T(8,128)(2,1)S(1)}, f32[1024,1024]{1,0:T(8,128)S(1)}) custom-call(bf16[256,1024]{1,0:T(8,128)(2,1)} %get-tuple-element.447.refs_0_.refs_3_, bf16[1024,256]{1,0:T(8,128)(2,1)S(1)} %bitcast.134, bf16[1024,256]{1,0:T(8,128)(2,1)S(1)} %collective-permute-done.7.refs_8_.refs_2_, bf16[256,1536]{1,0:T(8,128)(2,1)S(1)} %copy-done.11, ...), custom_call_target="tpu_custom_call" | custom-call | tf_op jit(solution)/shard_map/pallas_call | solution.py:48
  468.1 4.7 shard_map.264
  474.0 9.4 %shard_map.265 = (bf16[256,512]{1,0:T(8,128)(2,1)S(1)}, f32[512,1024]{1,0:T(8,128)S(1)}, bf16[512,1024]{1,0:T(8,128)(2,1)S(1)}) custom-call(bf16[256,1024]{1,0:T(8,128)(2,1)} %collective-permute-done.54.refs_0_.refs_2_, bf16[1024,256]{1,0:T(8,128)(2,1)S(1)} %bitcast.135, bf16[1024,256]{1,0:T(8,128)(2,1)S(1)} %collective-permute-done.7.refs_8_.refs_2_, ...), custom_call_target="tpu_custom_call" | custom-call | tf_op jit(solution)/shard_map/pallas_call | solution.py:48
  484.3 9.9 %shard_map.266 = (bf16[256,512]{1,0:T(8,128)(2,1)S(1)}, f32[512,1024]{1,0:T(8,128)S(1)}, bf16[512,1024]{1,0:T(8,128)(2,1)S(1)}) custom-call(bf16[256,1024]{1,0:T(8,128)(2,1)} %collective-permute-done.61.refs_0_.refs_4_, bf16[1024,256]{1,0:T(8,128)(2,1)S(1)} %bitcast.136, bf16[1024,256]{1,0:T(8,128)(2,1)S(1)} %collective-permute-done.7.refs_8_.refs_2_, ...), custom_call_target="tpu_custom_call" | custom-call | flops 99999997952 | tf_op jit(solution)/shard_map/pallas_call | solution.py:48
  501.4 3.0 shard_map.268
  505.6 3.8 shard_map.269
  510.3 3.1 shard_map.270
  515.9 3.8 shard_map.271
  535.6 6.0 shard_map.274
  557.9 3.0 shard_map.277
  561.1 5.8 reduce-scatter.11.cloned.1.call-done
  573.1 4.5 fusion.5
  586.8 18.0 %all-gather = f32[90112]{0:T(1024)S(1)} all-gather(f32[22528]{0:T(1024)S(1)} %pad_maximum_fusion.1), channel_id=2, replica_groups=mesh['section'=2,'dp'=4,'tensor'=4] {'dp'}, dimensions={0}, use_global_device_ids=true | all-gather | bytes 450560 | tf_op jit(solution)/shard_map/all_gather | solution.py:637
  (921 shorter events, 240.8 us)
Async XLA Ops:
  7.2 538.4 %reduce-scatter.5.cloned.1.call-start = ((), (), s32[]{:S(2)}) async-start(), calls=%async_computation.4 | async-start | bytes 2621440 | tf_op jit(solution)/shard_map/reduce_scatter | solution.py:540
  10.0 18.0 %collective-permute-start = (bf16[1024,768]{1,0:T(8,128)(2,1)}, bf16[1024,768]{1,0:T(8,128)(2,1)}, u32[]{:S(2)}, u32[]{:S(2)}) collective-permute-start(bf16[1024,768]{1,0:T(8,128)(2,1)} %pad_maximum_fusion.own_w_ref.refs_1_.refs_3_), channel_id=1, source_target_pairs={{0,1},{1,0},{2,3},{3,2},{4,5},{5,4},{6,7},{7,6},{8,9},{9,8},{10,11... | collective-permute-start | bytes 4718600 | tf_op jit(solution)/shard_map/ppermute | solution.py:20
  20.3 15.4 %collective-permute-start.2 = (bf16[256,1024]{1,0:T(8,128)(2,1)}, bf16[256,1024]{1,0:T(8,128)(2,1)}, u32[]{:S(2)}, u32[]{:S(2)}) collective-permute-start(bf16[256,1024]{1,0:T(8,128)(2,1)} %shard_map.194.rows_ref.refs_1_), channel_id=1, source_target_pairs={{0,2},{1,3},{2,0},{3,1},{4,6},{5,7},{6,4},{7,5},{8,10},{9,11},{10,... | collective-permute-start | bytes 1572872 | tf_op jit(solution)/shard_map/ppermute | solution.py:20
  22.9 57.7 %collective-permute-start.14 = (bf16[1024,1024]{1,0:T(8,128)(2,1)S(1)}, bf16[1024,1024]{1,0:T(8,128)(2,1)}, u32[]{:S(2)}, u32[]{:S(2)}) collective-permute-start(bf16[1024,1024]{1,0:T(8,128)(2,1)S(1)} %bitcast.86), channel_id=1, source_target_pairs={{0,1},{1,0},{2,3},{3,2},{4,5},{5,4},{6,7},{7,6},{8,9},{9,8},{10,11... | collective-permute-start | bytes 6291464 | tf_op jit(solution)/shard_map/ppermute | solution.py:20
  23.1 57.4 %collective-permute-start.15 = (bf16[1024,1024]{1,0:T(8,128)(2,1)}, bf16[1024,1024]{1,0:T(8,128)(2,1)}, u32[]{:S(2)}, u32[]{:S(2)}) collective-permute-start(bf16[1024,1024]{1,0:T(8,128)(2,1)} %bitcast.103), channel_id=1, source_target_pairs={{0,1},{1,0},{2,3},{3,2},{4,5},{5,4},{6,7},{7,6},{8,9},{9,8},{10,11... | collective-permute-start | bytes 6291464 | tf_op jit(solution)/shard_map/ppermute | solution.py:20
  27.8 11.6 %collective-permute-start.7 = (bf16[1024,256]{1,0:T(8,128)(2,1)S(1)}, bf16[1024,256]{1,0:T(8,128)(2,1)S(1)}, u32[]{:S(2)}, u32[]{:S(2)}) collective-permute-start(bf16[1024,256]{1,0:T(8,128)(2,1)S(1)} %bitcast.120), channel_id=1, source_target_pairs={{0,1},{1,0},{2,3},{3,2},{4,5},{5,4},{6,7},{7,6},{8,9},{9,8},{10,11... | collective-permute-start | bytes 1572872 | tf_op jit(solution)/shard_map/ppermute | solution.py:20
  39.4 13.9 %collective-permute-start.9 = (bf16[256,1024]{1,0:T(8,128)(2,1)S(1)}, bf16[256,1024]{1,0:T(8,128)(2,1)S(1)}, u32[]{:S(2)}, u32[]{:S(2)}) collective-permute-start(bf16[256,1024]{1,0:T(8,128)(2,1)S(1)} %shard_map.196.rows_ref.refs_3_), channel_id=1, source_target_pairs={{0,2},{1,3},{2,0},{3,1},{4,6},{5,7},{6,4},{7,5},{8,10},{9,11},{10,... | collective-permute-start | bytes 1572872 | tf_op jit(solution)/shard_map/ppermute | solution.py:20
  42.7 21.6 %collective-permute-start.10 = (bf16[256,512]{1,0:T(8,128)(2,1)S(1)}, bf16[256,512]{1,0:T(8,128)(2,1)S(1)}, u32[]{:S(2)}, u32[]{:S(2)}) collective-permute-start(bf16[256,512]{1,0:T(8,128)(2,1)S(1)} %get-tuple-element.283), channel_id=1, source_target_pairs={{0,1},{1,0},{2,3},{3,2},{4,5},{5,4},{6,7},{7,6},{8,9},{9,8},{10,11... | collective-permute-start | bytes 786440 | tf_op jit(solution)/shard_map/ppermute | solution.py:20
  43.1 21.4 %collective-permute-start.11 = (bf16[256,512]{1,0:T(8,128)(2,1)S(1)}, bf16[256,512]{1,0:T(8,128)(2,1)S(1)}, u32[]{:S(2)}, u32[]{:S(2)}) collective-permute-start(bf16[256,512]{1,0:T(8,128)(2,1)S(1)} %get-tuple-element.284), channel_id=1, source_target_pairs={{0,1},{1,0},{2,3},{3,2},{4,5},{5,4},{6,7},{7,6},{8,9},{9,8},{10,11... | collective-permute-start | bytes 786440 | tf_op jit(solution)/shard_map/ppermute | solution.py:20
  53.3 24.8 %collective-permute-start.8 = (bf16[256,1024]{1,0:T(8,128)(2,1)S(1)}, bf16[256,1024]{1,0:T(8,128)(2,1)S(1)}, u32[]{:S(2)}, u32[]{:S(2)}) collective-permute-start(bf16[256,1024]{1,0:T(8,128)(2,1)S(1)} %get-tuple-element.279.refs_9_), channel_id=1, source_target_pairs={{0,2},{1,3},{2,0},{3,1},{4,6},{5,7},{6,4},{7,5},{8,10},{9,11},{10,... | collective-permute-start | bytes 1572872 | tf_op jit(solution)/shard_map/ppermute | solution.py:20
  72.3 16.1 %collective-permute-start.17 = (bf16[256,1024]{1,0:T(8,128)(2,1)S(1)}, bf16[256,1024]{1,0:T(8,128)(2,1)S(1)}, u32[]{:S(2)}, u32[]{:S(2)}) collective-permute-start(bf16[256,1024]{1,0:T(8,128)(2,1)S(1)} %get-tuple-element.287.refs_9_), channel_id=1, source_target_pairs={{0,2},{1,3},{2,0},{3,1},{4,6},{5,7},{6,4},{7,5},{8,10},{9,11},{10,... | collective-permute-start | bytes 1572872 | tf_op jit(solution)/shard_map/ppermute | solution.py:20
  78.7 19.6 %collective-permute-start.16 = (bf16[256,1024]{1,0:T(8,128)(2,1)S(1)}, bf16[256,1024]{1,0:T(8,128)(2,1)S(1)}, u32[]{:S(2)}, u32[]{:S(2)}) collective-permute-start(bf16[256,1024]{1,0:T(8,128)(2,1)S(1)} %get-tuple-element.290.rows_ref.refs_1_), channel_id=1, source_target_pairs={{0,2},{1,3},{2,0},{3,1},{4,6},{5,7},{6,4},{7,5},{8,10},{9,11},{10,... | collective-permute-start | bytes 1572872 | tf_op jit(solution)/shard_map/ppermute | solution.py:20
  89.9 19.1 %collective-permute-start.19 = (bf16[256,1024]{1,0:T(8,128)(2,1)S(1)}, bf16[256,1024]{1,0:T(8,128)(2,1)S(1)}, u32[]{:S(2)}, u32[]{:S(2)}) collective-permute-start(bf16[256,1024]{1,0:T(8,128)(2,1)S(1)} %get-tuple-element.293.rows_ref.refs_3_), channel_id=1, source_target_pairs={{0,2},{1,3},{2,0},{3,1},{4,6},{5,7},{6,4},{7,5},{8,10},{9,11},{10,... | collective-permute-start | bytes 1572872 | tf_op jit(solution)/shard_map/ppermute | solution.py:20
  106.2 14.8 %collective-permute-start.18 = (bf16[256,1024]{1,0:T(8,128)(2,1)S(1)}, bf16[256,1024]{1,0:T(8,128)(2,1)S(1)}, u32[]{:S(2)}, u32[]{:S(2)}) collective-permute-start(bf16[256,1024]{1,0:T(8,128)(2,1)S(1)} %get-tuple-element.296.refs_6_), channel_id=1, source_target_pairs={{0,2},{1,3},{2,0},{3,1},{4,6},{5,7},{6,4},{7,5},{8,10},{9,11},{10,... | collective-permute-start | bytes 1572872 | tf_op jit(solution)/shard_map/ppermute | solution.py:20
  116.4 14.8 %collective-permute-start.22 = (bf16[256,1024]{1,0:T(8,128)(2,1)S(1)}, bf16[256,1024]{1,0:T(8,128)(2,1)S(1)}, u32[]{:S(2)}, u32[]{:S(2)}) collective-permute-start(bf16[256,1024]{1,0:T(8,128)(2,1)S(1)} %get-tuple-element.298.refs_5_), channel_id=1, source_target_pairs={{0,2},{1,3},{2,0},{3,1},{4,6},{5,7},{6,4},{7,5},{8,10},{9,11},{10,... | collective-permute-start | bytes 1572872 | tf_op jit(solution)/shard_map/ppermute | solution.py:20
  121.4 14.5 %collective-permute-start.20 = (bf16[256,1024]{1,0:T(8,128)(2,1)S(1)}, bf16[256,1024]{1,0:T(8,128)(2,1)S(1)}, u32[]{:S(2)}, u32[]{:S(2)}) collective-permute-start(bf16[256,1024]{1,0:T(8,128)(2,1)S(1)} %get-tuple-element.301.refs_5_), channel_id=1, source_target_pairs={{0,16},{1,17},{2,18},{3,19},{4,20},{5,21},{6,22},{7,23},{8,24},{9,... | collective-permute-start | bytes 1572872 | tf_op jit(solution)/shard_map/ppermute | solution.py:503
  132.5 13.7 %collective-permute-start.23 = (bf16[256,1024]{1,0:T(8,128)(2,1)S(1)}, bf16[256,1024]{1,0:T(8,128)(2,1)S(1)}, u32[]{:S(2)}, u32[]{:S(2)}) collective-permute-start(bf16[256,1024]{1,0:T(8,128)(2,1)S(1)} %get-tuple-element.305), channel_id=1, source_target_pairs={{0,16},{1,17},{2,18},{3,19},{4,20},{5,21},{6,22},{7,23},{8,24},{9,... | collective-permute-start | bytes 1572872 | tf_op jit(solution)/shard_map/ppermute | solution.py:503
  136.4 14.2 %collective-permute-start.21 = (bf16[256,1024]{1,0:T(8,128)(2,1)S(1)}, bf16[256,1024]{1,0:T(8,128)(2,1)S(1)}, u32[]{:S(2)}, u32[]{:S(2)}) collective-permute-start(bf16[256,1024]{1,0:T(8,128)(2,1)S(1)} %shard_map.211.rows_ref.refs_1_), channel_id=1, source_target_pairs={{0,2},{1,3},{2,0},{3,1},{4,6},{5,7},{6,4},{7,5},{8,10},{9,11},{10,... | collective-permute-start | bytes 1572872 | tf_op jit(solution)/shard_map/ppermute | solution.py:20
  146.6 21.4 %collective-permute-start.29 = (bf16[256,1024]{1,0:T(8,128)(2,1)S(1)}, bf16[256,1024]{1,0:T(8,128)(2,1)S(1)}, u32[]{:S(2)}, u32[]{:S(2)}) collective-permute-start(bf16[256,1024]{1,0:T(8,128)(2,1)S(1)} %shard_map.214.rows_ref.refs_3_), channel_id=1, source_target_pairs={{0,2},{1,3},{2,0},{3,1},{4,6},{5,7},{6,4},{7,5},{8,10},{9,11},{10,... | collective-permute-start | bytes 1572872 | tf_op jit(solution)/shard_map/ppermute | solution.py:20
  154.5 18.8 %collective-permute-start.30 = (bf16[256,512]{1,0:T(8,128)(2,1)S(1)}, bf16[256,512]{1,0:T(8,128)(2,1)S(1)}, u32[]{:S(2)}, u32[]{:S(2)}) collective-permute-start(bf16[256,512]{1,0:T(8,128)(2,1)S(1)} %get-tuple-element.317), channel_id=1, source_target_pairs={{0,1},{1,0},{2,3},{3,2},{4,5},{5,4},{6,7},{7,6},{8,9},{9,8},{10,11... | collective-permute-start | bytes 786440 | tf_op jit(solution)/shard_map/ppermute | solution.py:20
  154.6 18.8 %collective-permute-start.31 = (bf16[256,512]{1,0:T(8,128)(2,1)S(1)}, bf16[256,512]{1,0:T(8,128)(2,1)S(1)}, u32[]{:S(2)}, u32[]{:S(2)}) collective-permute-start(bf16[256,512]{1,0:T(8,128)(2,1)S(1)} %get-tuple-element.318), channel_id=1, source_target_pairs={{0,1},{1,0},{2,3},{3,2},{4,5},{5,4},{6,7},{7,6},{8,9},{9,8},{10,11... | collective-permute-start | bytes 786440 | tf_op jit(solution)/shard_map/ppermute | solution.py:20
  171.8 14.8 %collective-permute-start.28 = (bf16[256,1024]{1,0:T(8,128)(2,1)S(1)}, bf16[256,1024]{1,0:T(8,128)(2,1)S(1)}, u32[]{:S(2)}, u32[]{:S(2)}) collective-permute-start(bf16[256,1024]{1,0:T(8,128)(2,1)S(1)} %get-tuple-element.313.refs_9_), channel_id=1, source_target_pairs={{0,2},{1,3},{2,0},{3,1},{4,6},{5,7},{6,4},{7,5},{8,10},{9,11},{10,... | collective-permute-start | bytes 1572872 | tf_op jit(solution)/shard_map/ppermute | solution.py:20
  179.4 18.4 %collective-permute-start.35 = (bf16[256,1024]{1,0:T(8,128)(2,1)S(1)}, bf16[256,1024]{1,0:T(8,128)(2,1)S(1)}, u32[]{:S(2)}, u32[]{:S(2)}) collective-permute-start(bf16[256,1024]{1,0:T(8,128)(2,1)S(1)} %get-tuple-element.321.refs_9_), channel_id=1, source_target_pairs={{0,2},{1,3},{2,0},{3,1},{4,6},{5,7},{6,4},{7,5},{8,10},{9,11},{10,... | collective-permute-start | bytes 1572872 | tf_op jit(solution)/shard_map/ppermute | solution.py:20
  188.1 20.9 %collective-permute-start.34 = (bf16[256,1024]{1,0:T(8,128)(2,1)S(1)}, bf16[256,1024]{1,0:T(8,128)(2,1)S(1)}, u32[]{:S(2)}, u32[]{:S(2)}) collective-permute-start(bf16[256,1024]{1,0:T(8,128)(2,1)S(1)} %get-tuple-element.324.rows_ref.refs_1_), channel_id=1, source_target_pairs={{0,2},{1,3},{2,0},{3,1},{4,6},{5,7},{6,4},{7,5},{8,10},{9,11},{10,... | collective-permute-start | bytes 1572872 | tf_op jit(solution)/shard_map/ppermute | solution.py:20
  199.3 21.0 %collective-permute-start.37 = (bf16[256,1024]{1,0:T(8,128)(2,1)S(1)}, bf16[256,1024]{1,0:T(8,128)(2,1)S(1)}, u32[]{:S(2)}, u32[]{:S(2)}) collective-permute-start(bf16[256,1024]{1,0:T(8,128)(2,1)S(1)} %get-tuple-element.327.rows_ref.refs_3_), channel_id=1, source_target_pairs={{0,2},{1,3},{2,0},{3,1},{4,6},{5,7},{6,4},{7,5},{8,10},{9,11},{10,... | collective-permute-start | bytes 1572872 | tf_op jit(solution)/shard_map/ppermute | solution.py:20
  215.0 16.5 %collective-permute-start.36 = (bf16[256,1024]{1,0:T(8,128)(2,1)S(1)}, bf16[256,1024]{1,0:T(8,128)(2,1)S(1)}, u32[]{:S(2)}, u32[]{:S(2)}) collective-permute-start(bf16[256,1024]{1,0:T(8,128)(2,1)S(1)} %get-tuple-element.330.refs_6_), channel_id=1, source_target_pairs={{0,2},{1,3},{2,0},{3,1},{4,6},{5,7},{6,4},{7,5},{8,10},{9,11},{10,... | collective-permute-start | bytes 1572872 | tf_op jit(solution)/shard_map/ppermute | solution.py:20
  227.2 15.5 %collective-permute-start.39 = (bf16[256,1024]{1,0:T(8,128)(2,1)S(1)}, bf16[256,1024]{1,0:T(8,128)(2,1)S(1)}, u32[]{:S(2)}, u32[]{:S(2)}) collective-permute-start(bf16[256,1024]{1,0:T(8,128)(2,1)S(1)} %get-tuple-element.332.refs_5_), channel_id=1, source_target_pairs={{0,2},{1,3},{2,0},{3,1},{4,6},{5,7},{6,4},{7,5},{8,10},{9,11},{10,... | collective-permute-start | bytes 1572872 | tf_op jit(solution)/shard_map/ppermute | solution.py:20
  232.6 21.3 %collective-permute-start.38 = (bf16[256,1024]{1,0:T(8,128)(2,1)S(1)}, bf16[256,1024]{1,0:T(8,128)(2,1)S(1)}, u32[]{:S(2)}, u32[]{:S(2)}) collective-permute-start(bf16[256,1024]{1,0:T(8,128)(2,1)S(1)} %get-tuple-element.336.rows_ref.refs_1_), channel_id=1, source_target_pairs={{0,2},{1,3},{2,0},{3,1},{4,6},{5,7},{6,4},{7,5},{8,10},{9,11},{10,... | collective-permute-start | bytes 1572872 | tf_op jit(solution)/shard_map/ppermute | solution.py:20
  243.9 21.3 %collective-permute-start.41 = (bf16[256,1024]{1,0:T(8,128)(2,1)S(1)}, bf16[256,1024]{1,0:T(8,128)(2,1)S(1)}, u32[]{:S(2)}, u32[]{:S(2)}) collective-permute-start(bf16[256,1024]{1,0:T(8,128)(2,1)S(1)} %get-tuple-element.343.rows_ref.refs_3_), channel_id=1, source_target_pairs={{0,2},{1,3},{2,0},{3,1},{4,6},{5,7},{6,4},{7,5},{8,10},{9,11},{10,... | collective-permute-start | bytes 1572872 | tf_op jit(solution)/shard_map/ppermute | solution.py:20
  261.3 22.4 %collective-permute-start.40 = (bf16[256,1024]{1,0:T(8,128)(2,1)}, bf16[256,1024]{1,0:T(8,128)(2,1)}, u32[]{:S(2)}, u32[]{:S(2)}) collective-permute-start(bf16[256,1024]{1,0:T(8,128)(2,1)} %get-tuple-element.348.refs_6_), channel_id=1, source_target_pairs={{0,2},{1,3},{2,0},{3,1},{4,6},{5,7},{6,4},{7,5},{8,10},{9,11},{10,... | collective-permute-start | bytes 1572872 | tf_op jit(solution)/shard_map/ppermute | solution.py:20
  272.5 23.8 %collective-permute-start.43 = (bf16[256,1024]{1,0:T(8,128)(2,1)}, bf16[256,1024]{1,0:T(8,128)(2,1)}, u32[]{:S(2)}, u32[]{:S(2)}) collective-permute-start(bf16[256,1024]{1,0:T(8,128)(2,1)} %get-tuple-element.355.refs_9_), channel_id=1, source_target_pairs={{0,2},{1,3},{2,0},{3,1},{4,6},{5,7},{6,4},{7,5},{8,10},{9,11},{10,... | collective-permute-start | bytes 1572872 | tf_op jit(solution)/shard_map/ppermute | solution.py:20
  287.5 25.9 %collective-permute-start.42 = (bf16[256,1024]{1,0:T(8,128)(2,1)S(1)}, bf16[256,1024]{1,0:T(8,128)(2,1)S(1)}, u32[]{:S(2)}, u32[]{:S(2)}) collective-permute-start(bf16[256,1024]{1,0:T(8,128)(2,1)S(1)} %get-tuple-element.359.refs_0_.refs_1_), channel_id=1, source_target_pairs={{0,2},{1,3},{2,0},{3,1},{4,6},{5,7},{6,4},{7,5},{8,10},{9,11},{10,... | collective-permute-start | bytes 1572872 | tf_op jit(solution)/shard_map/ppermute | solution.py:20
  298.7 23.1 %collective-permute-start.45 = (bf16[256,1024]{1,0:T(8,128)(2,1)S(1)}, bf16[256,1024]{1,0:T(8,128)(2,1)S(1)}, u32[]{:S(2)}, u32[]{:S(2)}) collective-permute-start(bf16[256,1024]{1,0:T(8,128)(2,1)S(1)} %get-tuple-element.369.refs_0_.refs_3_), channel_id=1, source_target_pairs={{0,2},{1,3},{2,0},{3,1},{4,6},{5,7},{6,4},{7,5},{8,10},{9,11},{10,... | collective-permute-start | bytes 1572872 | tf_op jit(solution)/shard_map/ppermute | solution.py:20
  335.0 14.9 %collective-permute-start.46 = (bf16[256,1024]{1,0:T(8,128)(2,1)S(1)}, bf16[256,1024]{1,0:T(8,128)(2,1)S(1)}, u32[]{:S(2)}, u32[]{:S(2)}) collective-permute-start(bf16[256,1024]{1,0:T(8,128)(2,1)S(1)} %get-tuple-element.387.refs_5_), channel_id=1, source_target_pairs={{0,2},{1,3},{2,0},{3,1},{4,6},{5,7},{6,4},{7,5},{8,10},{9,11},{10,... | collective-permute-start | bytes 1572872 | tf_op jit(solution)/shard_map/ppermute | solution.py:20
  341.4 18.8 %collective-permute-start.50 = (bf16[256,1024]{1,0:T(8,128)(2,1)S(1)}, bf16[256,1024]{1,0:T(8,128)(2,1)S(1)}, u32[]{:S(2)}, u32[]{:S(2)}) collective-permute-start(bf16[256,1024]{1,0:T(8,128)(2,1)S(1)} %get-tuple-element.393.refs_5_), channel_id=1, source_target_pairs={{0,2},{1,3},{2,0},{3,1},{4,6},{5,7},{6,4},{7,5},{8,10},{9,11},{10,... | collective-permute-start | bytes 1572872 | tf_op jit(solution)/shard_map/ppermute | solution.py:20
  351.4 23.3 %collective-permute-start.48 = (bf16[256,1024]{1,0:T(8,128)(2,1)S(1)}, bf16[256,1024]{1,0:T(8,128)(2,1)S(1)}, u32[]{:S(2)}, u32[]{:S(2)}) collective-permute-start(bf16[256,1024]{1,0:T(8,128)(2,1)S(1)} %get-tuple-element.400.refs_5_), channel_id=1, source_target_pairs={{16,0},{17,1},{18,2},{19,3},{20,4},{21,5},{22,6},{23,7},{24,8},{25... | collective-permute-start | bytes 1572872 | tf_op jit(solution)/shard_map/ppermute | solution.py:508
  361.1 23.6 %collective-permute-start.51 = (bf16[256,1024]{1,0:T(8,128)(2,1)S(1)}, bf16[256,1024]{1,0:T(8,128)(2,1)S(1)}, u32[]{:S(2)}, u32[]{:S(2)}) collective-permute-start(bf16[256,1024]{1,0:T(8,128)(2,1)S(1)} %get-tuple-element.407), channel_id=1, source_target_pairs={{16,0},{17,1},{18,2},{19,3},{20,4},{21,5},{22,6},{23,7},{24,8},{25... | collective-permute-start | bytes 1572872 | tf_op jit(solution)/shard_map/ppermute | solution.py:508
  375.6 15.4 %collective-permute-start.49 = (bf16[256,1024]{1,0:T(8,128)(2,1)S(1)}, bf16[256,1024]{1,0:T(8,128)(2,1)S(1)}, u32[]{:S(2)}, u32[]{:S(2)}) collective-permute-start(bf16[256,1024]{1,0:T(8,128)(2,1)S(1)} %get-tuple-element.402.rows_ref.refs_1_), channel_id=1, source_target_pairs={{0,2},{1,3},{2,0},{3,1},{4,6},{5,7},{6,4},{7,5},{8,10},{9,11},{10,... | collective-permute-start | bytes 1572872 | tf_op jit(solution)/shard_map/ppermute | solution.py:20
  385.6 13.0 %collective-permute-start.53 = (bf16[256,1024]{1,0:T(8,128)(2,1)S(1)}, bf16[256,1024]{1,0:T(8,128)(2,1)S(1)}, u32[]{:S(2)}, u32[]{:S(2)}) collective-permute-start(bf16[256,1024]{1,0:T(8,128)(2,1)S(1)} %get-tuple-element.409.rows_ref.refs_3_), channel_id=1, source_target_pairs={{0,2},{1,3},{2,0},{3,1},{4,6},{5,7},{6,4},{7,5},{8,10},{9,11},{10,... | collective-permute-start | bytes 1572872 | tf_op jit(solution)/shard_map/ppermute | solution.py:20
  397.1 14.9 %collective-permute-start.52 = (bf16[256,1024]{1,0:T(8,128)(2,1)S(1)}, bf16[256,1024]{1,0:T(8,128)(2,1)S(1)}, u32[]{:S(2)}, u32[]{:S(2)}) collective-permute-start(bf16[256,1024]{1,0:T(8,128)(2,1)S(1)} %get-tuple-element.414.refs_6_), channel_id=1, source_target_pairs={{0,2},{1,3},{2,0},{3,1},{4,6},{5,7},{6,4},{7,5},{8,10},{9,11},{10,... | collective-permute-start | bytes 1572872 | tf_op jit(solution)/shard_map/ppermute | solution.py:20
  404.6 16.2 %collective-permute-start.59 = (bf16[256,1024]{1,0:T(8,128)(2,1)S(1)}, bf16[256,1024]{1,0:T(8,128)(2,1)S(1)}, u32[]{:S(2)}, u32[]{:S(2)}) collective-permute-start(bf16[256,1024]{1,0:T(8,128)(2,1)S(1)} %get-tuple-element.425.refs_14_), channel_id=1, source_target_pairs={{0,2},{1,3},{2,0},{3,1},{4,6},{5,7},{6,4},{7,5},{8,10},{9,11},{10,... | collective-permute-start | bytes 1572872 | tf_op jit(solution)/shard_map/ppermute | solution.py:20
  410.0 26.8 %collective-permute-start.55 = (bf16[256,1024]{1,0:T(8,128)(2,1)S(1)}, bf16[256,1024]{1,0:T(8,128)(2,1)S(1)}, u32[]{:S(2)}, u32[]{:S(2)}) collective-permute-start(bf16[256,1024]{1,0:T(8,128)(2,1)S(1)} %get-tuple-element.441), channel_id=1, source_target_pairs={{0,1},{1,0},{2,3},{3,2},{4,5},{5,4},{6,7},{7,6},{8,9},{9,8},{10,11... | collective-permute-start | bytes 1572872 | tf_op jit(solution)/shard_map/ppermute | solution.py:20
  410.0 38.9 %collective-permute-start.56 = (bf16[256,1024]{1,0:T(8,128)(2,1)S(1)}, bf16[256,1024]{1,0:T(8,128)(2,1)S(1)}, u32[]{:S(2)}, u32[]{:S(2)}) collective-permute-start(bf16[256,1024]{1,0:T(8,128)(2,1)S(1)} %get-tuple-element.442), channel_id=1, source_target_pairs={{0,1},{1,0},{2,3},{3,2},{4,5},{5,4},{6,7},{7,6},{8,9},{9,8},{10,11... | collective-permute-start | bytes 1572872 | tf_op jit(solution)/shard_map/ppermute | solution.py:20
  410.5 38.4 %collective-permute-start.57 = (bf16[256,1024]{1,0:T(8,128)(2,1)S(1)}, bf16[256,1024]{1,0:T(8,128)(2,1)S(1)}, u32[]{:S(2)}, u32[]{:S(2)}) collective-permute-start(bf16[256,1024]{1,0:T(8,128)(2,1)S(1)} %get-tuple-element.443), channel_id=1, source_target_pairs={{0,1},{1,0},{2,3},{3,2},{4,5},{5,4},{6,7},{7,6},{8,9},{9,8},{10,11... | collective-permute-start | bytes 1572872 | tf_op jit(solution)/shard_map/ppermute | solution.py:20
  412.0 37.0 %collective-permute-start.58 = (bf16[256,1024]{1,0:T(8,128)(2,1)S(1)}, bf16[256,1024]{1,0:T(8,128)(2,1)S(1)}, u32[]{:S(2)}, u32[]{:S(2)}) collective-permute-start(bf16[256,1024]{1,0:T(8,128)(2,1)S(1)} %get-tuple-element.444), channel_id=1, source_target_pairs={{0,1},{1,0},{2,3},{3,2},{4,5},{5,4},{6,7},{7,6},{8,9},{9,8},{10,11... | collective-permute-start | bytes 1572872 | tf_op jit(solution)/shard_map/ppermute | solution.py:20
  420.7 52.1 %collective-permute-start.54 = (bf16[256,1024]{1,0:T(8,128)(2,1)}, bf16[256,1024]{1,0:T(8,128)(2,1)}, u32[]{:S(2)}, u32[]{:S(2)}) collective-permute-start(bf16[256,1024]{1,0:T(8,128)(2,1)} %get-tuple-element.429.refs_0_.refs_1_), channel_id=1, source_target_pairs={{0,2},{1,3},{2,0},{3,1},{4,6},{5,7},{6,4},{7,5},{8,10},{9,11},{10,... | collective-permute-start | bytes 1572872 | tf_op jit(solution)/shard_map/ppermute | solution.py:20
  436.8 47.4 %collective-permute-start.61 = (bf16[256,1024]{1,0:T(8,128)(2,1)}, bf16[256,1024]{1,0:T(8,128)(2,1)}, u32[]{:S(2)}, u32[]{:S(2)}) collective-permute-start(bf16[256,1024]{1,0:T(8,128)(2,1)} %get-tuple-element.447.refs_0_.refs_3_), channel_id=1, source_target_pairs={{0,2},{1,3},{2,0},{3,1},{4,6},{5,7},{6,4},{7,5},{8,10},{9,11},{10,... | collective-permute-start | bytes 1572872 | tf_op jit(solution)/shard_map/ppermute | solution.py:20
  451.5 104.3 %reduce-scatter.7.cloned.1.call-start = ((), (), s32[]{:S(2)}) async-start(), calls=%async_computation.5 | async-start | bytes 2621440 | tf_op jit(solution)/shard_map/reduce_scatter | solution.py:540
  472.8 22.0 %collective-permute-start.62 = (bf16[256,1024]{1,0:T(8,128)(2,1)S(1)}, bf16[256,1024]{1,0:T(8,128)(2,1)S(1)}, u32[]{:S(2)}, u32[]{:S(2)}) collective-permute-start(bf16[256,1024]{1,0:T(8,128)(2,1)S(1)} %get-tuple-element.465), channel_id=1, source_target_pairs={{0,1},{1,0},{2,3},{3,2},{4,5},{5,4},{6,7},{7,6},{8,9},{9,8},{10,11... | collective-permute-start | bytes 1572872 | tf_op jit(solution)/shard_map/ppermute | solution.py:20
  472.9 21.9 %collective-permute-start.63 = (bf16[256,1024]{1,0:T(8,128)(2,1)S(1)}, bf16[256,1024]{1,0:T(8,128)(2,1)S(1)}, u32[]{:S(2)}, u32[]{:S(2)}) collective-permute-start(bf16[256,1024]{1,0:T(8,128)(2,1)S(1)} %get-tuple-element.466), channel_id=1, source_target_pairs={{0,1},{1,0},{2,3},{3,2},{4,5},{5,4},{6,7},{7,6},{8,9},{9,8},{10,11... | collective-permute-start | bytes 1572872 | tf_op jit(solution)/shard_map/ppermute | solution.py:20
  473.4 21.4 %collective-permute-start.64 = (bf16[256,1024]{1,0:T(8,128)(2,1)S(1)}, bf16[256,1024]{1,0:T(8,128)(2,1)S(1)}, u32[]{:S(2)}, u32[]{:S(2)}) collective-permute-start(bf16[256,1024]{1,0:T(8,128)(2,1)S(1)} %get-tuple-element.467), channel_id=1, source_target_pairs={{0,1},{1,0},{2,3},{3,2},{4,5},{5,4},{6,7},{7,6},{8,9},{9,8},{10,11... | collective-permute-start | bytes 1572872 | tf_op jit(solution)/shard_map/ppermute | solution.py:20
  473.5 21.4 %collective-permute-start.65 = (bf16[256,1024]{1,0:T(8,128)(2,1)S(1)}, bf16[256,1024]{1,0:T(8,128)(2,1)S(1)}, u32[]{:S(2)}, u32[]{:S(2)}) collective-permute-start(bf16[256,1024]{1,0:T(8,128)(2,1)S(1)} %get-tuple-element.468), channel_id=1, source_target_pairs={{0,1},{1,0},{2,3},{3,2},{4,5},{5,4},{6,7},{7,6},{8,9},{9,8},{10,11... | collective-permute-start | bytes 1572872 | tf_op jit(solution)/shard_map/ppermute | solution.py:20
  499.3 67.6 %reduce-scatter.11.cloned.1.call-start = ((), (), s32[]{:S(2)}) async-start(), calls=%async_computation.7 | async-start | bytes 655360 | tf_op jit(solution)/shard_map/reduce_scatter | solution.py:540
  500.1 14.2 %collective-permute-start.67 = (bf16[512,1024]{1,0:T(8,128)(2,1)}, bf16[512,1024]{1,0:T(8,128)(2,1)S(1)}, u32[]{:S(2)}, u32[]{:S(2)}) collective-permute-start(bf16[512,1024]{1,0:T(8,128)(2,1)} %copy-done.306), channel_id=1, source_target_pairs={{0,1},{1,0},{2,3},{3,2},{4,5},{5,4},{6,7},{7,6},{8,9},{9,8},{10,11... | collective-permute-start | bytes 3145736 | tf_op jit(solution)/shard_map/ppermute | solution.py:20
  504.4 19.2 %collective-permute-start.68 = (bf16[256,256]{1,0:T(8,128)(2,1)S(1)}, bf16[256,256]{1,0:T(8,128)(2,1)S(1)}, u32[]{:S(2)}, u32[]{:S(2)}) collective-permute-start(bf16[256,256]{1,0:T(8,128)(2,1)S(1)} %get-tuple-element.486), channel_id=1, source_target_pairs={{0,1},{1,0},{2,3},{3,2},{4,5},{5,4},{6,7},{7,6},{8,9},{9,8},{10,11... | collective-permute-start | bytes 393224 | tf_op jit(solution)/shard_map/ppermute | solution.py:20
  504.5 19.5 %collective-permute-start.69 = (bf16[256,256]{1,0:T(8,128)(2,1)S(1)}, bf16[256,256]{1,0:T(8,128)(2,1)S(1)}, u32[]{:S(2)}, u32[]{:S(2)}) collective-permute-start(bf16[256,256]{1,0:T(8,128)(2,1)S(1)} %get-tuple-element.487), channel_id=1, source_target_pairs={{0,1},{1,0},{2,3},{3,2},{4,5},{5,4},{6,7},{7,6},{8,9},{9,8},{10,11... | collective-permute-start | bytes 393224 | tf_op jit(solution)/shard_map/ppermute | solution.py:20
  505.0 19.1 %collective-permute-start.70 = (bf16[256,256]{1,0:T(8,128)(2,1)S(1)}, bf16[256,256]{1,0:T(8,128)(2,1)S(1)}, u32[]{:S(2)}, u32[]{:S(2)}) collective-permute-start(bf16[256,256]{1,0:T(8,128)(2,1)S(1)} %get-tuple-element.488), channel_id=1, source_target_pairs={{0,1},{1,0},{2,3},{3,2},{4,5},{5,4},{6,7},{7,6},{8,9},{9,8},{10,11... | collective-permute-start | bytes 393224 | tf_op jit(solution)/shard_map/ppermute | solution.py:20
  505.0 19.0 %collective-permute-start.71 = (bf16[256,256]{1,0:T(8,128)(2,1)S(1)}, bf16[256,256]{1,0:T(8,128)(2,1)S(1)}, u32[]{:S(2)}, u32[]{:S(2)}) collective-permute-start(bf16[256,256]{1,0:T(8,128)(2,1)S(1)} %get-tuple-element.489), channel_id=1, source_target_pairs={{0,1},{1,0},{2,3},{3,2},{4,5},{5,4},{6,7},{7,6},{8,9},{9,8},{10,11... | collective-permute-start | bytes 393224 | tf_op jit(solution)/shard_map/ppermute | solution.py:20
  514.2 30.8 %collective-permute-start.66 = (bf16[256,1024]{1,0:T(8,128)(2,1)}, bf16[256,1024]{1,0:T(8,128)(2,1)}, u32[]{:S(2)}, u32[]{:S(2)}) collective-permute-start(bf16[256,1024]{1,0:T(8,128)(2,1)} %get-tuple-element.473.refs_5_), channel_id=1, source_target_pairs={{0,2},{1,3},{2,0},{3,1},{4,6},{5,7},{6,4},{7,5},{8,10},{9,11},{10,... | collective-permute-start | bytes 1572872 | tf_op jit(solution)/shard_map/ppermute | solution.py:20
  523.6 29.1 %collective-permute-start.72 = (bf16[256,1024]{1,0:T(8,128)(2,1)}, bf16[256,1024]{1,0:T(8,128)(2,1)}, u32[]{:S(2)}, u32[]{:S(2)}) collective-permute-start(bf16[256,1024]{1,0:T(8,128)(2,1)} %get-tuple-element.479.refs_5_), channel_id=1, source_target_pairs={{0,2},{1,3},{2,0},{3,1},{4,6},{5,7},{6,4},{7,5},{8,10},{9,11},{10,... | collective-permute-start | bytes 1572872 | tf_op jit(solution)/shard_map/ppermute | solution.py:20
  543.5 12.3 %collective-permute-start.78 = (bf16[256,768]{1,0:T(8,128)(2,1)}, bf16[256,768]{1,0:T(8,128)(2,1)}, u32[]{:S(2)}, u32[]{:S(2)}) collective-permute-start(bf16[256,768]{1,0:T(8,128)(2,1)} %get-tuple-element.527), channel_id=1, source_target_pairs={{0,1},{1,0},{2,3},{3,2},{4,5},{5,4},{6,7},{7,6},{8,9},{9,8},{10,11... | collective-permute-start | bytes 1179656 | tf_op jit(solution)/shard_map/ppermute | solution.py:20
  543.5 12.3 %collective-permute-start.79 = (bf16[256,768]{1,0:T(8,128)(2,1)}, bf16[256,768]{1,0:T(8,128)(2,1)}, u32[]{:S(2)}, u32[]{:S(2)}) collective-permute-start(bf16[256,768]{1,0:T(8,128)(2,1)} %get-tuple-element.528), channel_id=1, source_target_pairs={{0,1},{1,0},{2,3},{3,2},{4,5},{5,4},{6,7},{7,6},{8,9},{9,8},{10,11... | collective-permute-start | bytes 1179656 | tf_op jit(solution)/shard_map/ppermute | solution.py:20
  544.0 11.8 %collective-permute-start.80 = (bf16[256,768]{1,0:T(8,128)(2,1)}, bf16[256,768]{1,0:T(8,128)(2,1)}, u32[]{:S(2)}, u32[]{:S(2)}) collective-permute-start(bf16[256,768]{1,0:T(8,128)(2,1)} %get-tuple-element.529), channel_id=1, source_target_pairs={{0,1},{1,0},{2,3},{3,2},{4,5},{5,4},{6,7},{7,6},{8,9},{9,8},{10,11... | collective-permute-start | bytes 1179656 | tf_op jit(solution)/shard_map/ppermute | solution.py:20
  544.0 66.9 %reduce-scatter.9.cloned.1.call-start = ((), (), s32[]{:S(2)}) async-start(), calls=%async_computation.6 | async-start | bytes 1966080 | tf_op jit(solution)/shard_map/reduce_scatter | solution.py:540
  (339 other events, 2309.6 us)
Sparse Core Ops, SparseCore 0:
  451.6 44.1 reduce-scatter.4
  499.4 44.1 reduce-scatter.6
  545.9 20.9 reduce-scatter.10
  569.1 39.3 reduce-scatter.8

commit v2 on v1

v2 whole, which is shorter than its diff:
```python
import functools

import jax
import jax.numpy as jnp
from jax import lax
from jax.experimental import pallas as pl
from jax.experimental.pallas import tpu as pltpu
from jax.sharding import PartitionSpec as P

HD = 64
SLAB = 2 * HD
EXPO = HD ** (-0.5) * 1.4426950408889634
BF = jnp.bfloat16
F32 = jnp.float32
precise = lax.Precision.HIGHEST


def swap(block, bit):
    count = lax.axis_size("tensor")
    return lax.ppermute(block, "tensor", [(i, i ^ bit) for i in range(count)])


def tensor_sum(block):
    count = lax.axis_size("tensor")
    bit = 1
    while bit < count:
        block = block + swap(block, bit)
        bit *= 2
    return block


TIMES = {
    "first_norm_kernel": 1,
    "triple_kernel": 3,
    "attend_kernel": 8,
    "middle_kernel": 1,
    "mlp_kernel": 6,
    "layer_end_kernel": 1,
    "grad_feed_kernel": 1,
    "grad_mlp_kernel": 6,
    "grad_middle_kernel": 2,
    "grad_attend_kernel": 11,
    "grad_normed_kernel": 3,
    "grad_rows_kernel": 1,
    "weight_kernel": 6,
    "add_kernel": 1,
    "copy_kernel": 1,
}
SHARE = 1


def over_dp(block):
    count = lax.axis_size("dp")
    if count & (count - 1):
        return lax.all_gather(block, "dp", axis=0, tiled=True)
    bit = 1
    while bit < count:
        other = lax.ppermute(block, "dp", [(i, i ^ bit) for i in range(count)])
        block = jnp.concatenate([block, other], 0)
        bit *= 2
    return block


def line_reduce(block):
    count, place = lax.axis_size("dp"), lax.axis_index("dp")
    size = block.shape[0] // count

    def chunk(owner):
        at = jnp.clip(owner, 0, count - 1) * size
        return lax.dynamic_slice(block, (at, 0), (size, block.shape[1])).astype(F32)

    came = []
    up = down = jnp.zeros((size, block.shape[1]), BF)
    for step in range(1, count):
        up = (chunk(place + count - step) + up.astype(F32)).astype(BF)
        down = (chunk(place - count + step) + down.astype(F32)).astype(BF)
        up, down = lax.optimization_barrier((up, down))
        up = lax.ppermute(up, "dp", [(i, i + 1) for i in range(step)])
        down = lax.ppermute(down, "dp", [(i, i - 1) for i in range(count - step, count)])
        came.append((up, down))
    return chunk(place) + up.astype(F32) + down.astype(F32), came


def call(kernel, ins, outs, scratch=(), token=None, flag=None, flops=0, far_in=(), far_out=()):
    name = getattr(kernel, "func", kernel).__name__
    vmem = pl.BlockSpec(memory_space=pltpu.VMEM)
    anywhere = pl.BlockSpec(memory_space=pl.ANY)
    specs = [anywhere if i in far_in else vmem for i in range(len(ins))]
    if flag is not None:
        ins = (flag, *ins)
        specs = [pl.BlockSpec(memory_space=pltpu.SMEM), *specs]
    body = kernel
    if token is not None:
        token = token if isinstance(token, tuple) else (token,)
        place = len(ins)
        ins = (*ins, *token)
        specs += [anywhere] * len(token)

        def body(*refs):
            kernel(*refs[:place], *refs[len(ins) :])

    shift = 0 if flag is None else 1
    ins = [outside(x) if i - shift in far_in else x for i, x in enumerate(ins)]
    results = pl.pallas_call(
        body,
        in_specs=specs,
        out_specs=[anywhere if i in far_out else vmem for i in range(len(outs))],
        out_shape=list(outs),
        scratch_shapes=list(scratch),
        compiler_params=pltpu.CompilerParams(vmem_limit_bytes=(20 if name == "weight_kernel" else 14) << 20),
        cost_estimate=pl.CostEstimate(flops=flops or int(TIMES[name] * SHARE * 1.15e9), bytes_accessed=0, transcendentals=0),
    )(*ins)
    return [outside(x) if i in far_out else x for i, x in enumerate(results)]


def outside(block):
    return pltpu.with_memory_space_constraint(block, pltpu.HBM)


def like(rows, cols, kind):
    return jax.ShapeDtypeStruct((rows, cols), kind)


def dot_nn(left, right):
    return jnp.dot(left, right, preferred_element_type=F32)


def dot_nt(left, right):
    return lax.dot_general(left, right, (((1,), (1,)), ((), ())), preferred_element_type=F32)


def unit_rows(rows):
    center = rows - jnp.mean(rows, axis=-1, keepdims=True)
    spread = jnp.mean(center * center, axis=-1, keepdims=True)
    inverse = lax.rsqrt(spread + 1e-06)
    return center * inverse, inverse


def norm_back(unit, inverse, grad, factor):
    grad_unit = grad * (1.0 + factor)
    return inverse * (
        grad_unit
        - jnp.mean(grad_unit, axis=-1, keepdims=True)
        - unit * jnp.mean(grad_unit * unit, axis=-1, keepdims=True)
    )


def gelu_both(u):
    root = 0.7978845608028654
    square = u * u
    inner = root * (1.0 + 0.044715 * square)
    tanh = jnp.tanh(u * inner)
    half = 0.5 * (1.0 + tanh)
    slope = half + (0.5 * u) * (1.0 - tanh * tanh) * (root + (3.0 * 0.044715 * root) * square)
    return u * half, slope


def total(ref):
    return jnp.sum(ref, axis=0, keepdims=True)


def first_norm_kernel(rows_ref, mod_ref, out_ref):
    unit, _ = unit_rows(rows_ref[...].astype(F32))
    out_ref[...] = (unit * (1.0 + mod_ref[1:2]) + mod_ref[0:1]).astype(BF)


def triple_kernel(rows_ref, own_w_ref, other_w_ref, bias_ref, triple_ref, *send_refs):
    width = own_w_ref.shape[1]
    third = width // 3
    for group, w_ref in enumerate((own_w_ref, other_w_ref)):
        cols = slice(group * width, (group + 1) * width)
        part = (dot_nn(rows_ref[...], w_ref[...]) + bias_ref[:, cols]).astype(BF)
        triple_ref[:, cols] = part
        send_refs[1 - group][...] = part[:, third:]


def slabs(width):
    return [(group, first) for group in range(2) for first in range(0, width, SLAB)]


def tokens_of(near_ref, far_ref, away_near_ref, away_far_ref, group, first, width, which):
    here = group * 3 * width + which * width + first
    away = (which - 1) * width + first
    return jnp.concatenate(
        [ref[:, here : here + SLAB] for ref in (near_ref, far_ref)]
        + [refs[group][:, away : away + SLAB] for refs in (away_near_ref, away_far_ref)],
        0,
    )


def queries_of(near_ref, far_ref, group, first, width):
    start = group * 3 * width + first
    return jnp.concatenate([ref[:, start : start + SLAB] for ref in (near_ref, far_ref)], 0)


def attend_kernel(
    near_ref, far_ref, an0_ref, an1_ref, af0_ref, af1_ref, own_w_ref, other_w_ref, mixed_ref, log_ref, keep_ref, send_ref
):
    block = mixed_ref.shape[0]
    width = mixed_ref.shape[1] // 2
    size = keep_ref.shape[0]
    upper = lax.broadcasted_iota(jnp.int32, (SLAB, block), 0) >= HD
    for group, first in slabs(width):
        tokens = (near_ref, far_ref, (an0_ref, an1_ref), (af0_ref, af1_ref), group, first, width)
        queries = queries_of(near_ref, far_ref, group, first, width).T
        keys = tokens_of(*tokens, 1)
        values = tokens_of(*tokens, 2).T
        outs = []
        for h in range(2):
            scores = dot_nn(keys, jnp.where(upper == (h == 1), queries, jnp.zeros_like(queries)))
            peak = jnp.max(scores, axis=0, keepdims=True)
            expo = jnp.exp2((scores - peak) * EXPO)
            weight = total(expo)
            out = dot_nn(values[h * HD : (h + 1) * HD], expo.astype(BF))
            outs.append(out * (1.0 / weight))
            head = (group * width + first) // HD + h
            log_ref[head : head + 1, :] = peak * EXPO + jnp.log2(weight)
        at = group * width + first
        mixed_ref[:, at : at + SLAB] = jnp.concatenate(outs, 0).T.astype(BF)
    for rows, out_ref in ((slice(size, 2 * size), send_ref), (slice(0, size), keep_ref)):
        branch = dot_nt(mixed_ref[rows, :width], own_w_ref[...])
        branch = branch + dot_nt(mixed_ref[rows, width:], other_w_ref[...])
        out_ref[...] = branch.astype(out_ref.dtype)


def middle_kernel(keep_ref, far_ref, bias_ref, rows_ref, mod_ref, branch_ref, middle_ref, second_ref):
    branch = keep_ref[...] + far_ref[...].astype(F32) + bias_ref[...]
    middle = rows_ref[...].astype(F32) + mod_ref[2:3] * branch
    unit, _ = unit_rows(middle)
    branch_ref[...] = branch.astype(BF)
    middle_ref[...] = middle
    second_ref[...] = (unit * (1.0 + mod_ref[4:5]) + mod_ref[3:4]).astype(BF)


def mlp_kernel(
    rows_ref, own_w1_ref, other_w1_ref, bias_ref, own_w2_ref, other_w2_ref, act_out, slope_out, out_ref, act_ref, slope_ref, sems
):
    width = own_w1_ref.shape[1]
    tile = 256
    copies = []
    for group, w1_ref in enumerate((own_w1_ref, other_w1_ref)):
        for first in range(0, width, tile):
            cols = slice(group * width + first, group * width + first + tile)
            value, slope = gelu_both(dot_nn(rows_ref[...], w1_ref[:, first : first + tile]) + bias_ref[:, cols])
            act_ref[:, cols] = value.astype(BF)
            slope_ref[:, cols] = slope.astype(BF)
        cols = slice(group * width, (group + 1) * width)
        for i, (ref, out) in enumerate(((act_ref, act_out), (slope_ref, slope_out))):
            copies.append(pltpu.make_async_copy(ref.at[:, cols], out.at[:, cols], sems.at[group, i]))
            copies[-1].start()
    feed = dot_nt(act_ref[:, :width], own_w2_ref[...]) + dot_nt(act_ref[:, width:], other_w2_ref[...])
    out_ref[...] = feed.astype(out_ref.dtype)
    for copy in copies:
        copy.wait()


def layer_end_kernel(keep_ref, far_ref, bias_ref, middle_ref, mod_ref, feed_ref, out_ref):
    feed = keep_ref[...] + far_ref[...].astype(F32) + bias_ref[...]
    feed_ref[...] = feed.astype(BF)
    out_ref[...] = (middle_ref[...] + mod_ref[5:6] * feed).astype(BF)


def grad_feed_kernel(grad_ref, feed_ref, mod_ref, out_ref, sums_ref):
    grad = grad_ref[...].astype(F32)
    out = (mod_ref[5:6] * grad).astype(BF)
    out_ref[...] = out
    sums_ref[0:1] = total(grad * feed_ref[...].astype(F32))
    sums_ref[1:2] = total(out.astype(F32))


def grad_mlp_kernel(
    rows_ref, own_w2_ref, other_w2_ref, slope_in, own_w1_ref, other_w1_ref, hidden_out, sums_ref, out_ref, hidden_ref, slope_ref, sems
):
    width = own_w2_ref.shape[1]
    tile = 256
    halves = [slice(group * width, (group + 1) * width) for group in range(2)]
    slopes = [
        pltpu.make_async_copy(slope_in.at[:, cols], slope_ref.at[:, cols], sems.at[0, group])
        for group, cols in enumerate(halves)
    ]
    hiddens = [
        pltpu.make_async_copy(hidden_ref.at[:, cols], hidden_out.at[:, cols], sems.at[1, group])
        for group, cols in enumerate(halves)
    ]
    for copy in slopes:
        copy.start()
    for group, w2_ref in enumerate((own_w2_ref, other_w2_ref)):
        for first in range(0, width, tile):
            cols = slice(group * width + first, group * width + first + tile)
            grad = dot_nn(rows_ref[...], w2_ref[:, first : first + tile])
            if first == 0:
                slopes[group].wait()
            grad = (grad * slope_ref[:, cols].astype(F32)).astype(BF)
            hidden_ref[:, cols] = grad
            sums_ref[:, cols] = total(grad.astype(F32))
        hiddens[group].start()
    second = dot_nt(hidden_ref[:, :width], own_w1_ref[...]) + dot_nt(hidden_ref[:, width:], other_w1_ref[...])
    out_ref[...] = second.astype(out_ref.dtype)
    for copy in hiddens:
        copy.wait()


def grad_middle_kernel(keep_ref, far_ref, middle_ref, branch_ref, grad_ref, mod_ref, out_ref, rows_ref, sums_ref):
    grad = keep_ref[...] + far_ref[...].astype(F32)
    unit, inverse = unit_rows(middle_ref[...])
    sums_ref[0:1] = total(grad)
    sums_ref[1:2] = total(grad * unit)
    grad = norm_back(unit, inverse, grad, mod_ref[4:5]) + grad_ref[...].astype(F32)
    out_ref[...] = grad
    sums_ref[2:3] = total(grad * branch_ref[...].astype(F32))
    rows = (mod_ref[2:3] * grad).astype(BF)
    rows_ref[...] = rows
    sums_ref[3:4] = total(rows.astype(F32))


def grad_attend_kernel(
    rows_near_ref,
    rows_far_ref,
    own_w_ref,
    other_w_ref,
    near_ref,
    far_ref,
    an0_ref,
    an1_ref,
    af0_ref,
    af1_ref,
    mixed_ref,
    log_ref,
    out_ref,
    keep_ref,
    send_ref,
    grad_ref,
):
    block = mixed_ref.shape[0]
    width = mixed_ref.shape[1] // 2
    size = rows_near_ref.shape[0]
    scale = HD ** (-0.5)
    for part, rows_ref in enumerate((rows_near_ref, rows_far_ref)):
        for group, w_ref in enumerate((own_w_ref, other_w_ref)):
            grad_ref[part * size : (part + 1) * size, group * width : (group + 1) * width] = dot_nn(
                rows_ref[...], w_ref[...]
            ).astype(BF)
    upper = lax.broadcasted_iota(jnp.int32, (SLAB, block), 0) >= HD
    right = lax.broadcasted_iota(jnp.int32, (block, SLAB), 1) >= HD
    for group, first in slabs(width):
        at = group * width + first
        tokens = (near_ref, far_ref, (an0_ref, an1_ref), (af0_ref, af1_ref), group, first, width)
        queries = queries_of(near_ref, far_ref, group, first, width)
        grad = grad_ref[:, at : at + SLAB]
        keys, values = tokens_of(*tokens, 1), tokens_of(*tokens, 2)
        queries_t, grad_t, keys_t = queries.T, grad.T, keys.T
        inner = grad_t.astype(F32) * mixed_ref[:, at : at + SLAB].T.astype(F32)
        none = jnp.zeros_like(queries_t)
        none_r = jnp.zeros_like(queries)
        outs, key_sum, value_sum = [], None, None
        for h in range(2):
            head = at // HD + h
            delta = total(inner[h * HD : (h + 1) * HD])
            scores = dot_nn(keys, jnp.where(upper == (h == 1), queries_t, none))
            probs = jnp.exp2(scores * EXPO - log_ref[head : head + 1, :])
            grad_w = dot_nn(values, jnp.where(upper == (h == 1), grad_t, none))
            grad_s = (probs * (grad_w - delta)).astype(BF)
            value_part = dot_nn(probs.astype(BF), jnp.where(right == (h == 1), grad, none_r))
            key_part = dot_nn(grad_s, jnp.where(right == (h == 1), queries, none_r))
            key_sum = key_part if h == 0 else key_sum + key_part
            value_sum = value_part if h == 0 else value_sum + value_part
            outs.append(dot_nn(keys_t[h * HD : (h + 1) * HD], grad_s))
        out_ref[:, at : at + SLAB] = (jnp.concatenate(outs, 0).T * scale).astype(BF)
        for which, term in enumerate((key_sum * scale, value_sum)):
            cols = group * 2 * width + which * width + first
            turned = (1 - group) * 2 * width + which * width + first
            keep_ref[:, cols : cols + SLAB] = term[:block]
            send_ref[:, turned : turned + SLAB] = term[block:].astype(BF)


def grad_normed_kernel(part, query_ref, keep_ref, got_ref, own_w_ref, other_w_ref, triple_ref, out_ref, sums_ref):
    size, width = triple_ref.shape[0], query_ref.shape[1] // 2
    rows = slice(part * size, (part + 1) * size)
    for group in range(2):
        at = group * 3 * width
        cols = slice(group * 2 * width, (group + 1) * 2 * width)
        triple_ref[:, at : at + width] = query_ref[rows, group * width : (group + 1) * width]
        triple_ref[:, at + width : at + 3 * width] = (
            keep_ref[rows, cols] + got_ref[rows, cols].astype(F32)
        ).astype(BF)
    out = dot_nt(triple_ref[:, : 3 * width], own_w_ref[...]) + dot_nt(triple_ref[:, 3 * width :], other_w_ref[...])
    out_ref[...] = out.astype(out_ref.dtype)
    sums_ref[...] = total(triple_ref[...].astype(F32))


def grad_rows_kernel(keep_ref, far_ref, rows_ref, middle_ref, mod_ref, out_ref, sums_ref):
    grad = keep_ref[...] + far_ref[...].astype(F32)
    unit, inverse = unit_rows(rows_ref[...].astype(F32))
    sums_ref[0:1] = total(grad)
    sums_ref[1:2] = total(grad * unit)
    out_ref[...] = (norm_back(unit, inverse, grad, mod_ref[1:2]) + middle_ref[...]).astype(BF)


CHUNKS = 4


def weight_kernel(lefts, rights, flag_ref, *refs):
    count = lefts + rights
    out_refs = refs[2 * count : -7]
    left_rows, left_all, right_all, keep_all, send_all, sems, out_sems = refs[-7:]

    for section in range(2):
        here = refs[section * count : (section + 1) * count]

        @pl.when(flag_ref[0] == section)
        def _():
            copies = []
            for some, to in ((here[:lefts], left_rows), (here[lefts:], right_all)):
                at = 0
                for ref in some:
                    rows = slice(at, at + ref.shape[0])
                    copies.append((pltpu.make_async_copy(ref, to.at[rows], sems.at[len(copies)]), rows))
                    copies[-1][0].start()
                    at += ref.shape[0]
            for copy, rows in copies[:lefts]:
                copy.wait()
                left_all[:, rows] = left_rows[rows].T
            for copy, _ in copies[lefts:]:
                copy.wait()

    rows, width = keep_all.shape
    tile = rows // CHUNKS
    copies = []
    for i in range(CHUNKS):
        part = slice(i * tile, (i + 1) * tile)
        keep_all[part] = dot_nn(left_all[part], right_all[:, :width]).astype(BF)
        send_all[part] = dot_nn(left_all[part], right_all[:, width:]).astype(BF)
        copies.append(pltpu.make_async_copy(keep_all.at[part], out_refs[0].at[part], out_sems.at[0, i]))
        copies.append(pltpu.make_async_copy(send_all.at[part], out_refs[i + 1], out_sems.at[1, i]))
        copies[-2].start()
        copies[-1].start()
    for copy in copies:
        copy.wait()


def weight_grad(first, second, section, token):
    lefts, rights = first
    tokens = sum(x.shape[0] for x in lefts)
    rows, cols = lefts[0].shape[1], rights[0].shape[1]
    ins = (*lefts, *rights, *second[0], *second[1])
    return call(
        functools.partial(weight_kernel, len(lefts), len(rights)),
        ins,
        [like(rows, cols // 2, BF)] + [like(rows // CHUNKS, cols // 2, BF)] * CHUNKS,
        scratch=[
            pltpu.VMEM((tokens, rows), BF),
            pltpu.VMEM((rows, tokens), BF),
            pltpu.VMEM((tokens, cols), BF),
            pltpu.VMEM((rows, cols // 2), BF),
            pltpu.VMEM((rows, cols // 2), BF),
            pltpu.SemaphoreType.DMA((len(lefts) + len(rights),)),
            pltpu.SemaphoreType.DMA((2, CHUNKS)),
        ],
        token=token,
        flag=section,
        far_in=range(len(ins)),
        far_out=range(1 + CHUNKS),
    )


def add_kernel(count, *refs):
    out_ref, one_all, two_all, sems = refs[-4:]
    size = out_ref.shape[0] // CHUNKS
    first, copies = 0, []
    for one_ref, *got in (refs[i * (1 + CHUNKS) : (i + 1) * (1 + CHUNKS)] for i in range(count)):
        cols = slice(first, first + one_ref.shape[1])
        first = cols.stop
        copies.append(pltpu.make_async_copy(one_ref, one_all.at[:, cols], sems.at[len(copies)]))
        for i, two_ref in enumerate(got):
            rows = slice(i * size, (i + 1) * size)
            copies.append(pltpu.make_async_copy(two_ref, two_all.at[rows, cols], sems.at[len(copies)]))
    for copy in copies:
        copy.start()
    for copy in copies:
        copy.wait()
    for i in range(CHUNKS):
        rows = slice(i * size, (i + 1) * size)
        out_ref[rows] = (one_all[rows].astype(F32) + two_all[rows].astype(F32)).astype(BF)


def copy_kernel(from_ref, out_ref):
    out_ref[...] = from_ref[...]


def tied(block, token):
    if token is None:
        return block
    token = token if isinstance(token, tuple) else (token,)
    return lax.optimization_barrier((block, *token))[0]


def forward_steps(rows, mod, weights):
    w_qkv, b_qkv, w_out, b_out, w_fc1, b_fc1, w_fc2 = weights
    size, width = rows.shape
    local = w_out[0].shape[1]
    hidden = w_fc1[0].shape[1]
    token = yield None, ()
    (normed,) = call(first_norm_kernel, (rows, mod), [like(size, width, BF)], token=token)
    normed_far = swap(normed, 2)
    triple_outs = [like(size, 6 * local, BF), like(size, 2 * local, BF), like(size, 2 * local, BF)]
    triple, *sends = call(triple_kernel, (normed, *w_qkv, b_qkv), triple_outs)
    away = [swap(send, 1) for send in sends]
    token = yield triple, ()
    normed_far = tied(normed_far, token)
    triple_far, *sends = call(triple_kernel, (normed_far, *w_qkv, b_qkv), triple_outs, token=token)
    tokens = (triple, triple_far, *away, *(swap(send, 1) for send in sends))
    mixed, log, keep, send = call(
        attend_kernel,
        (*tokens, *w_out),
        [
            like(2 * size, 2 * local, BF),
            like(2 * local // HD, 2 * size, F32),
            like(size, width, F32),
            like(size, width, BF),
        ],
        token=token,
    )
    far = swap(send, 2)
    token = yield keep, ()
    branch, middle, second = call(
        middle_kernel,
        (keep, tied(far, token), b_out[0:1], rows, mod),
        [like(size, width, BF), like(size, width, F32), like(size, width, BF)],
        token=token,
    )
    second_far = swap(second, 2)
    outs = [like(size, 2 * hidden, BF), like(size, 2 * hidden, BF)]
    scratch = [
        pltpu.VMEM((size, 2 * hidden), BF),
        pltpu.VMEM((size, 2 * hidden), BF),
        pltpu.SemaphoreType.DMA((2, 2)),
    ]
    act, slope, keep = call(
        mlp_kernel,
        (second, *w_fc1, b_fc1, *w_fc2),
        [*outs, like(size, width, F32)],
        scratch=scratch,
        far_out=(0, 1),
    )
    token = yield keep, ()
    second_far = tied(second_far, token)
    act_far, slope_far, send = call(
        mlp_kernel,
        (second_far, *w_fc1, b_fc1, *w_fc2),
        [*outs, like(size, width, BF)],
        scratch=scratch,
        token=token,
        far_out=(0, 1),
    )
    far = swap(send, 2)
    token = yield send, ()
    feed, result = call(
        layer_end_kernel,
        (keep, tied(far, token), b_out[1:2], middle, mod),
        [like(size, width, BF), like(size, width, BF)],
        token=token,
    )
    state = (
        rows, (normed, normed_far), tokens, mixed, log, branch, middle,
        (second, second_far), (act, act_far), (slope, slope_far), feed,
    )
    return result, state


def backward_steps(grad, mod, weights, state, flops=0):
    w_qkv, b_qkv, w_out, b_out, w_fc1, b_fc1, w_fc2 = weights
    rows, normed, tokens, mixed, log, branch, middle, second, acts, slopes, feed = state
    size, width = rows.shape
    local = w_out[0].shape[1]
    hidden = w_fc1[0].shape[1]
    token = yield None, ()
    feed_rows, sums_feed = call(
        grad_feed_kernel, (grad, feed, mod), [like(size, width, BF), like(2, width, F32)], token=token
    )
    feed_far = swap(feed_rows, 2)
    outs = [like(size, 2 * hidden, BF), like(1, 2 * hidden, F32)]
    scratch = [
        pltpu.VMEM((size, 2 * hidden), BF),
        pltpu.VMEM((size, 2 * hidden), BF),
        pltpu.SemaphoreType.DMA((2, 2)),
    ]
    hidden_near, sums_near, keep = call(
        grad_mlp_kernel,
        (feed_rows, *w_fc2, slopes[0], *w_fc1),
        [*outs, like(size, width, F32)],
        scratch=scratch,
        far_in=(3,),
        far_out=(0,),
    )
    token = yield keep, ()
    feed_far = tied(feed_far, token)
    hidden_far, sums_far, send = call(
        grad_mlp_kernel,
        (feed_far, *w_fc2, slopes[1], *w_fc1),
        [*outs, like(size, width, BF)],
        scratch=scratch,
        token=token,
        far_in=(3,),
        far_out=(0,),
    )
    far = swap(send, 2)
    token = yield send, ((3, (feed_rows, feed_far), acts),)
    grad_middle, branch_rows, sums_middle = call(
        grad_middle_kernel,
        (keep, tied(far, token), middle, branch, grad, mod),
        [like(size, width, F32), like(size, width, BF), like(4, width, F32)],
        token=token,
    )
    branch_far = swap(branch_rows, 2)
    token = yield branch_rows, ((2, second, (hidden_near, hidden_far)),)
    branch_far = tied(branch_far, token)
    queries, kept, send = call(
        grad_attend_kernel,
        (branch_rows, branch_far, *w_out, *tokens, mixed, log),
        [
            like(2 * size, 2 * local, BF),
            like(2 * size, 4 * local, F32),
            like(2 * size, 4 * local, BF),
        ],
        scratch=[pltpu.VMEM((2 * size, 2 * local), BF)],
        token=token,
        flops=flops,
    )
    got = swap(send, 1)
    token = yield kept, ((1, (branch_rows, branch_far), (mixed,)),)
    outs = [like(size, 6 * local, BF), like(size, width, BF), like(1, 6 * local, F32)]
    triple_far, send, sums_triple_far = call(
        functools.partial(grad_normed_kernel, 1), (queries, kept, got, *w_qkv), outs, token=token
    )
    far = swap(send, 2)
    outs[1] = like(size, width, F32)
    triple_near, keep, sums_triple = call(
        functools.partial(grad_normed_kernel, 0), (queries, kept, got, *w_qkv), outs, token=send
    )
    token = yield keep, ((0, normed, (triple_near, triple_far)),)
    grad_rows, sums_rows = call(
        grad_rows_kernel,
        (keep, tied(far, token), rows, grad_middle, mod),
        [like(size, width, BF), like(2, width, F32)],
        token=token,
    )
    return grad_rows, (sums_rows, sums_middle, sums_feed, sums_triple, sums_triple_far, sums_near, sums_far)


def small_sums(raw):
    sums_rows, sums_middle, sums_feed, sums_triple, sums_triple_far, sums_near, sums_far = raw
    grad_mod = jnp.concatenate(
        [sums_rows, sums_middle[2:3], sums_middle[0:2], sums_feed[0:1]], 0
    ).reshape(1, -1)
    return grad_mod, (
        (sums_triple + sums_triple_far)[0],
        (sums_near + sums_far)[0],
        jnp.concatenate([sums_middle[3:4], sums_feed[1:2]], 0),
    )


def chain_steps(ends, mod, weights, flops):
    sent, state_one = yield from forward_steps(ends, mod, weights)
    arrived = lax.ppermute(sent, "section", [(0, 1)])
    yield sent, ()
    out, state_two = yield from forward_steps(arrived, mod, weights)
    yield out, ()
    back_two = yield from backward_steps(ends, mod, weights, state_two)
    arrived = lax.ppermute(back_two[0], "section", [(1, 0)])
    yield back_two[0], ()
    back_one = yield from backward_steps(arrived, mod, weights, state_one, flops)
    yield back_one[0], ()
    return out, back_two, back_one


def side_by_side(chains, section):
    results = [None] * len(chains)
    products, sums, pending, begun = {}, {}, [], [None, None]
    after = {0: 2}
    for chain in chains:
        next(chain)
    token = None
    while pending or any(result is None for result in results):
        ready = {}
        if any(which == 0 for which, _, _ in pending):
            token = (token, sums[3])
        for i, chain in enumerate(chains):
            try:
                token, made = chain.send(token)
            except StopIteration as stop:
                results[i] = stop.value
                continue
            for which, lefts, rights in made:
                both = ready.setdefault(which, ([], []))
                both[0].extend(lefts)
                both[1].extend(rights)
        for which, keep, got in pending:
            parts = (keep, *got)
            if which == 1:
                waiting = parts
                continue
            if which in after:
                token = (token, sums[after[which]])
                parts = (*parts, *waiting)
            rows, cols = keep.shape[0], sum(x.shape[1] for x in parts[:: 1 + CHUNKS])
            count = len(parts) // (1 + CHUNKS)
            (token,) = call(
                functools.partial(add_kernel, count),
                parts,
                [like(rows, cols, BF)],
                scratch=[
                    pltpu.VMEM((rows, cols), BF),
                    pltpu.VMEM((rows, cols), BF),
                    pltpu.SemaphoreType.DMA((len(parts),)),
                ],
                token=token,
                far_in=range(len(parts)),
            )
            if which in after and lax.axis_size("dp") <= 4:
                sums[which], begun = line_reduce(token)
            else:
                sums[which] = lax.psum_scatter(token, "dp", scatter_dimension=0, tiled=True)
        pending = []
        for which, operands in ready.items():
            if which not in products:
                products[which] = operands
                continue
            keep, *sends = weight_grad(operands, products[which], section, token)
            token = keep
            pending.append((which, keep, [swap(send, 1) for send in sends]))
    return results, sums, token, begun


def body(
    boundary,
    conditioning,
    query_key_value_weight,
    query_value_bias,
    attention_output_weight,
    output_biases,
    first_mlp_weight,
    first_mlp_bias,
    second_mlp_weight,
    w_ada,
    ada_bias,
):
    leading = lax.axis_index("section") == 0
    ends = boundary[0]
    width, _, local = query_key_value_weight.shape[1:]
    tensor_no = lax.axis_index("tensor")
    dp_no = lax.axis_index("dp")
    tensor_count = lax.axis_size("tensor")
    dp_count = lax.axis_size("dp")
    w_qkv = jnp.concatenate([query_key_value_weight[0, :, i] for i in range(3)], 1)
    qv = query_value_bias[0].astype(F32)
    b_qkv = jnp.concatenate([qv[0], jnp.zeros_like(qv[0]), qv[1]])[None]
    w_out, w_fc1, w_fc2 = attention_output_weight[0], first_mlp_weight[0], second_mlp_weight[0]
    hidden = w_fc1.shape[1]
    vectors = jnp.concatenate([b_qkv, first_mlp_bias.astype(F32)], 1)
    other = swap(vectors, 1)
    weights = (
        (w_qkv, swap(w_qkv, 1)),
        jnp.concatenate([b_qkv, other[:, : 3 * local]], 1),
        (w_out, swap(w_out, 1)),
        output_biases[0].astype(F32),
        (w_fc1, swap(w_fc1, 1)),
        jnp.concatenate([vectors[:, 3 * local :], other[:, 3 * local :]], 1),
        (w_fc2, swap(w_fc2, 1)),
    )
    ada_weight = w_ada[0]
    cond_vals = conditioning.astype(F32)
    cond_act = jax.nn.silu(cond_vals).astype(BF)
    mods = (dot_nn(cond_act, ada_weight) + ada_bias[0].astype(F32)).reshape(2, 6, width)

    section = lax.axis_index("section").astype(jnp.int32).reshape(1)
    chains, sums, token, begun = side_by_side(
        [chain_steps(ends[b], mods[b], weights, b * 10**11) for b in range(ends.shape[0])], section
    )
    outs = [chain[0] for chain in chains]
    raw = [(chain[1][1], chain[2][1]) for chain in chains]
    leaves, kind = jax.tree.flatten(raw)
    raw = jax.tree.unflatten(kind, lax.optimization_barrier((*leaves, token))[:-1])
    backs_two = [(chain[1][0], *small_sums(two)) for chain, (two, _) in zip(chains, raw)]
    backs_one = [(chain[2][0], *small_sums(one)) for chain, (_, one) in zip(chains, raw)]

    g_both, g_fc1, g_fc2 = (sums[i].astype(F32) for i in (0, 2, 3))
    g_qkv, g_proj = g_both[:, : 3 * local], g_both[:, 3 * local :]
    g_qkv = jnp.stack([g_qkv[:, i * local : (i + 1) * local] for i in range(3)], 1)

    pick = lambda one, two: jnp.where(leading, one, two)
    grad_mods = jnp.concatenate(
        [pick(one[1], two[1]) for one, two in zip(backs_one, backs_two)], 0
    )
    owned_triple, owned_hidden, partial = (
        pick(
            backs_one[0][2][i] + backs_one[1][2][i],
            backs_two[0][2][i] + backs_two[1][2][i],
        )
        for i in range(3)
    )
    def placed(vector):
        size = vector.shape[0] // 2
        full = jnp.zeros((tensor_count * size,), F32)
        for part, where in ((vector[:size], tensor_no), (vector[size:], tensor_no ^ 1)):
            full = lax.dynamic_update_slice(full, part, (where * size,))
        return full

    span = 3 * local
    queries = jnp.concatenate([owned_triple[:local], owned_triple[span : span + local]])
    values = jnp.concatenate([owned_triple[2 * local : span], owned_triple[span + 2 * local :]])
    flat = jnp.concatenate(
        [
            grad_mods.reshape(-1),
            placed(queries),
            placed(values),
            placed(owned_hidden),
            partial.reshape(-1),
        ]
    )
    (flat,) = call(
        copy_kernel, (flat.reshape(-1, width),), [like(flat.size // width, width, F32)], token=token, flops=10**11
    )
    flat = tied(tensor_sum(flat), begun[0]).reshape(-1)
    grad_mods = flat[: 12 * width].reshape(2, 6 * width)
    biases = flat[12 * width :]
    everything = over_dp(
        jnp.concatenate([grad_mods.reshape(-1), biases, cond_act.astype(F32).reshape(-1)])[None]
    )
    mods_end = 12 * width
    all_mods = everything[:, :mods_end].reshape(2 * dp_count, 6 * width)
    all_acts = everything[:, -2 * width :].reshape(2 * dp_count, width)
    biases = jnp.sum(everything[:, mods_end : -2 * width], axis=0)
    place = dp_no * tensor_count + tensor_no
    shares = dp_count * tensor_count

    def own_share(vector):
        size = vector.shape[0] // shares
        return lax.dynamic_slice(vector, (place * size,), (size,))[None]

    hidden_all = biases.shape[0] - 4 * width
    g_qv_bias = own_share(biases[: 2 * width])
    g_fc1_bias = own_share(biases[2 * width : 2 * width + hidden_all])
    g_out_bias = own_share(biases[2 * width + hidden_all :])
    g_ada_bias = own_share(jnp.sum(all_mods, axis=0))
    share = width // shares
    act_share = lax.dynamic_slice(all_acts, (0, place * share), (all_acts.shape[0], share))
    g_ada = lax.dot_general(
        act_share, all_mods, (((0,), (0,)), ((), ())), precision=precise, preferred_element_type=F32
    )

    cut = 6 * width // tensor_count
    mods_cut = lax.dynamic_slice(grad_mods, (0, tensor_no * cut), (2, cut))
    ada_cut = lax.dynamic_slice(ada_weight, (0, tensor_no * cut), (width, cut))
    back_cond = lax.dot_general(
        mods_cut,
        ada_cut.astype(F32),
        (((1,), (1,)), ((), ())),
        precision=precise,
        preferred_element_type=F32,
    )
    back_cond = tied(back_cond, (everything, *(begun[1] or ())))
    back_cond = back_cond + lax.ppermute(back_cond, "section", [(0, 1), (1, 0)])
    cond_total = tensor_sum(back_cond)
    sig = jax.nn.sigmoid(cond_vals)
    cond_grad = cond_total * sig * (1.0 + cond_vals * (1.0 - sig))

    rows_out = jnp.stack([pick(back[0], out) for back, out in zip(backs_one, outs)])[None]
    return (
        rows_out,
        cond_grad,
        g_qkv[None],
        g_qv_bias,
        g_proj[None],
        g_out_bias,
        g_fc1[None],
        g_fc1_bias,
        g_fc2[None],
        g_ada[None],
        g_ada_bias,
    )


def solution(mesh):
    in_specs = (
        P("section", "dp", "tensor", None),
        P("dp", None),
        P("section", None, None, "tensor"),
        P("section", None, "tensor"),
        P("section", None, "tensor"),
        P("section", None, None),
        P("section", None, "tensor"),
        P("section", "tensor"),
        P("section", None, "tensor"),
        P("section", None, None),
        P("section", None),
    )
    out_specs = (
        P("section", "dp", "tensor", None),
        P("dp", None),
        P("section", "dp", None, "tensor"),
        P("section", ("dp", "tensor")),
        P("section", "dp", "tensor"),
        P("section", ("dp", "tensor")),
        P("section", "dp", "tensor"),
        P("section", ("dp", "tensor")),
        P("section", "dp", "tensor"),
        P("section", ("dp", "tensor"), None),
        P("section", ("dp", "tensor")),
    )
    return jax.shard_map(body, mesh=mesh, in_specs=in_specs, out_specs=out_specs, check_vma=False)
```

time: 631 us -> 591 us (0.937)
  local copies, waits for them, and re-layouts: 97.6 us -> 55 us
  Pallas kernels: 302 us -> 271 us
  starting transfers between devices: 64 us -> 91.3 us
  waiting for transfers between devices: 97.7 us -> 120 us
  blocking collectives: 18 us -> 0 us
    unnamed x642 -> x382, local copies, waits for them, and re-layouts: 89.9 us -> 47 us
    ppermute x77, waiting for transfers between devices: 68.4 us -> 101 us  [swap(): return lax.ppermute(block, 'tensor', [(i, i ^ bit) for i in range(count)])]
    pallas_call x84 -> x72, Pallas kernels: 302 us -> 271 us  [call(): pl.pallas_call(body, in_specs=specs, out_specs=[anywhere if i in far_out...]
    ppermute x0 -> x8, starting transfers between devices: none -> 21.1 us  [the longest x3 11.9 us: line_reduce(): up = lax.ppermute(up, 'dp', [(i, i + 1) for i in range(step)])]
    all_gather x1 -> x0, blocking collectives: 18 us -> none  [body(): lax.all_gather(jnp.concatenate([grad_mods.reshape(-1), biases, cond_act.a...]
    ppermute x2, waiting for transfers between devices: 15 us -> 2.91 us  [chain_steps(): arrived = lax.ppermute(back_two[0], 'section', [(1, 0)])]
    ppermute x0 -> x8, waiting for transfers between devices: none -> 9.59 us  [the longest x3 8.16 us: line_reduce(): up = lax.ppermute(up, 'dp', [(i, i + 1) for i in range(step)])]
  transfers between devices with their start and end apart: 86 -> 92, of which waited for: 33 -> 35; matrix products, arithmetic and copies ran while one was open for 4% -> 5% of each run, Pallas kernels for 49% -> 46%
where the time goes in v2:
time: 591 us; the launch traced here: 580 us
  Pallas kernels  271 us (46%)
  waiting for transfers between devices  120 us (20%)
  starting transfers between devices  91.3 us (15%)
  local copies, waits for them, and re-layouts  55 us (9%)
  between operations  17.2 us (3%)
  matrix products  13.4 us (2%)
  other arithmetic  12.5 us (2%)
    pallas_call x72, Pallas kernels, call(): pl.pallas_call(body, in_specs=specs, out_specs=[anywhere if i in far_out...  271 us
    ppermute x77, waiting for transfers between devices, swap(): return lax.ppermute(block, 'tensor', [(i, i ^ bit) for i in range(count)])  101 us
    ppermute x77, starting transfers between devices, swap(): return lax.ppermute(block, 'tensor', [(i, i ^ bit) for i in range(count)])  58.4 us
    unnamed x382, local copies, waits for them, and re-layouts  47 us
    ppermute x3, starting transfers between devices, line_reduce(): up = lax.ppermute(up, 'dp', [(i, i + 1) for i in range(step)])  11.9 us
  transfers between devices with their start and end apart: 92, of which 35 were waited for; matrix products, arithmetic and copies ran while one was open for 5% of the time, Pallas kernels for 46%

profile of v2, /device:TPU:0, one launch (start us, length us, event | category | flops | bytes accessed | tf_op | source)
XLA Modules:
  0.0 580.4 jit_solution(16351431681186702147)
XLA Ops:
  10.0 6.3 %fusion.2 = f32[2,6144]{1,0:T(2,128)S(1)} fusion(bf16[1,1024,6144]{2,1,0:T(8,128)(2,1)} %param.20, f32[6144]{0:T(1024)S(1)} %bitcast.130, bf16[2,1024]{1,0:T(2,128)(2,1)S(1)} %copy-done.180), kind=kOutput, calls=%fused_computation.3 | convolution fusion | flops 25190400 | bytes 12660736 | tf_op jit(solution)/shard_map/dot_general | solution.py:125
  27.3 7.1 %collective-permute-done.2.refs_0_.refs_2_ = bf16[256,1024]{1,0:T(8,128)(2,1)} collective-permute-done((bf16[256,1024]{1,0:T(8,128)(2,1)}, bf16[256,1024]{1,0:T(8,128)(2,1)}, u32[]{:S(2)}, u32[]{:S(2)}) %collective-permute-start.2) | collective-permute-done | bytes 524320 | tf_op jit(solution)/shard_map/ppermute | solution.py:20
  34.9 2.8 shard_map.198
  41.3 9.9 %shard_map.199 = (bf16[512,512]{1,0:T(8,128)(2,1)S(1)}, f32[8,512]{1,0:T(8,128)S(1)}, f32[256,1024]{1,0:T(8,128)S(1)}, bf16[256,1024]{1,0:T(8,128)(2,1)S(1)}) custom-call(bf16[256,1536]{1,0:T(8,128)(2,1)S(1)} %get-tuple-element.271.refs_2_.refs_0_.refs_4_, bf16[256,1536]{1,0:T(8,128)(2,1)S(1)} %get-tuple-element.274.refs_1_.refs_5_, ...), custom_call_target="tpu_custom_call" | custom-call | flops 9200000000 | tf_op jit(solution)/shard_map/pallas_call | solution.py:104
  58.0 9.9 %shard_map.201 = (bf16[512,512]{1,0:T(8,128)(2,1)S(1)}, f32[8,512]{1,0:T(8,128)S(1)}, f32[256,1024]{1,0:T(8,128)S(1)}, bf16[256,1024]{1,0:T(8,128)(2,1)S(1)}) custom-call(bf16[256,1536]{1,0:T(8,128)(2,1)S(1)} %get-tuple-element.272.refs_4_.refs_8_.refs_0_, bf16[256,1536]{1,0:T(8,128)(2,1)S(1)} %get-tuple-element.282.refs_1_.refs_5_, ...), custom_call_target="tpu_custom_call" | custom-call | flops 9200000000 | tf_op jit(solution)/shard_map/pallas_call | solution.py:104
  73.3 13.8 %shard_map.203 = (bf16[256,2048]{1,0:T(8,128)(2,1)S(1)}, bf16[256,2048]{1,0:T(8,128)(2,1)S(1)}, f32[256,1024]{1,0:T(8,128)S(1)}) custom-call(bf16[256,1024]{1,0:T(8,128)(2,1)S(1)} %get-tuple-element.289.rows_ref.refs_1_, bf16[1024,1024]{1,0:T(8,128)(2,1)S(1)} %bitcast.92, bf16[1024,1024]{1,0:T(8,128)(2,1)S(1)} %collective-permute-done.14.other_w1_ref.refs_2_.refs_5_, ...), custom_call_target="tpu_custom_call" | custom-call | flops 6899999744 | tf_op jit(solution)/shard_map/pallas_call | solution.py:104
  89.4 4.0 shard_map.205
  94.8 4.0 shard_map.206
  102.1 3.9 collective-permute-done.19.refs_0_.refs_4_
  106.1 4.0 shard_map.207
  111.3 6.0 %collective-permute-done.18.refs_1_ = bf16[256,1024]{1,0:T(8,128)(2,1)S(1)} collective-permute-done((bf16[256,1024]{1,0:T(8,128)(2,1)S(1)}, bf16[256,1024]{1,0:T(8,128)(2,1)S(1)}, u32[]{:S(2)}, u32[]{:S(2)}) %collective-permute-start.18) | collective-permute-done | bytes 524320 | tf_op jit(solution)/shard_map/ppermute | solution.py:20
  117.7 3.4 collective-permute-start.20
  121.1 6.3 %collective-permute-done.22.refs_1_ = bf16[256,1024]{1,0:T(8,128)(2,1)S(1)} collective-permute-done((bf16[256,1024]{1,0:T(8,128)(2,1)S(1)}, bf16[256,1024]{1,0:T(8,128)(2,1)S(1)}, u32[]{:S(2)}, u32[]{:S(2)}) %collective-permute-start.22) | collective-permute-done | bytes 524320 | tf_op jit(solution)/shard_map/ppermute | solution.py:20
  128.5 3.6 collective-permute-start.23
  137.1 5.0 collective-permute-done.23.refs_0_.refs_3_.refs_2_
  150.8 9.7 %shard_map.215 = (bf16[512,512]{1,0:T(8,128)(2,1)S(1)}, f32[8,512]{1,0:T(8,128)S(1)}, f32[256,1024]{1,0:T(8,128)S(1)}, bf16[256,1024]{1,0:T(8,128)(2,1)S(1)}) custom-call(bf16[256,1536]{1,0:T(8,128)(2,1)S(1)} %get-tuple-element.302.refs_2_.refs_0_.refs_4_, bf16[256,1536]{1,0:T(8,128)(2,1)S(1)} %get-tuple-element.308.refs_1_.refs_5_, ...), custom_call_target="tpu_custom_call" | custom-call | flops 9200000000 | tf_op jit(solution)/shard_map/pallas_call | solution.py:104
  167.7 9.7 %shard_map.217 = (bf16[512,512]{1,0:T(8,128)(2,1)S(1)}, f32[8,512]{1,0:T(8,128)S(1)}, f32[256,1024]{1,0:T(8,128)S(1)}, bf16[256,1024]{1,0:T(8,128)(2,1)S(1)}) custom-call(bf16[256,1536]{1,0:T(8,128)(2,1)S(1)} %get-tuple-element.306.refs_4_.refs_8_.refs_0_, bf16[256,1536]{1,0:T(8,128)(2,1)S(1)} %get-tuple-element.316.refs_1_.refs_5_, ...), custom_call_target="tpu_custom_call" | custom-call | flops 9200000000 | tf_op jit(solution)/shard_map/pallas_call | solution.py:104
  182.3 4.2 shard_map.219
  186.5 5.9 %collective-permute-done.35.refs_1_ = bf16[256,1024]{1,0:T(8,128)(2,1)S(1)} collective-permute-done((bf16[256,1024]{1,0:T(8,128)(2,1)S(1)}, bf16[256,1024]{1,0:T(8,128)(2,1)S(1)}, u32[]{:S(2)}, u32[]{:S(2)}) %collective-permute-start.35) | collective-permute-done | bytes 524320 | tf_op jit(solution)/shard_map/ppermute | solution.py:20
  194.3 4.0 shard_map.221
  200.3 3.3 collective-permute-done.34.refs_0_.refs_10_
  203.6 4.1 shard_map.222
  211.0 3.8 collective-permute-done.37.refs_0_.refs_12_
  214.8 4.3 shard_map.223
  220.6 5.5 collective-permute-done.36.refs_1_
  228.0 4.5 shard_map.226
  232.6 4.7 collective-permute-done.39.refs_1_
  240.0 4.5 shard_map.229
  244.5 4.0 collective-permute-done.38.refs_0_.refs_10_
  248.5 4.7 shard_map.230
  255.6 4.2 collective-permute-done.41.refs_0_.refs_12_
  259.8 5.1 shard_map.231
  266.3 4.7 collective-permute-done.40.refs_1_
  273.5 8.7 %collective-permute-done.43.refs_1_ = bf16[256,1024]{1,0:T(8,128)(2,1)S(1)} collective-permute-done((bf16[256,1024]{1,0:T(8,128)(2,1)S(1)}, bf16[256,1024]{1,0:T(8,128)(2,1)S(1)}, u32[]{:S(2)}, u32[]{:S(2)}) %collective-permute-start.43) | collective-permute-done | bytes 524320 | tf_op jit(solution)/shard_map/ppermute | solution.py:20
  285.7 7.8 %collective-permute-done.42.refs_1_.refs_8_ = bf16[256,1024]{1,0:T(8,128)(2,1)S(1)} collective-permute-done((bf16[256,1024]{1,0:T(8,128)(2,1)S(1)}, bf16[256,1024]{1,0:T(8,128)(2,1)S(1)}, u32[]{:S(2)}, u32[]{:S(2)}) %collective-permute-start.42) | collective-permute-done | bytes 524320 | tf_op jit(solution)/shard_map/ppermute | solution.py:20
  293.5 12.7 %shard_map.234 = (bf16[512,512]{1,0:T(8,128)(2,1)S(1)}, f32[512,1024]{1,0:T(8,128)S(1)}, bf16[512,1024]{1,0:T(8,128)(2,1)S(1)}) custom-call(bf16[256,1024]{1,0:T(8,128)(2,1)S(1)} %get-tuple-element.354.refs_6_.refs_0_.refs_7_, bf16[256,1024]{1,0:T(8,128)(2,1)S(1)} %collective-permute-done.42.refs_1_.refs_8_, bf16[1024,256]{1,0:T(8,128)(2,1)} %bitcast.9.refs_6_.refs_2_, ...), custom_call_target="tpu_custom_call" | custom-call | flops 12650000384 | tf_op jit(solution)/shard_map/pallas_call | solution.py:104
  306.4 12.5 %shard_map.235 = (bf16[512,512]{1,0:T(8,128)(2,1)S(1)}, f32[512,1024]{1,0:T(8,128)S(1)}, bf16[512,1024]{1,0:T(8,128)(2,1)S(1)}) custom-call(bf16[256,1024]{1,0:T(8,128)(2,1)S(1)} %get-tuple-element.357.refs_12_.refs_0_.refs_9_, bf16[256,1024]{1,0:T(8,128)(2,1)S(1)} %collective-permute-done.45.refs_1_.refs_10_, bf16[1024,256]{1,0:T(8,128)(2,1)} %bitcast.9.refs_6_.refs_2_, ...), custom_call_target="tpu_custom_call" | custom-call | flops 12650000384 | tf_op jit(solution)/shard_map/pallas_call | solution.py:104
  319.4 2.8 shard_map.236
  326.1 3.5 shard_map.238
  332.8 4.3 collective-permute-done.46.refs_1_
  339.3 8.1 %collective-permute-done.50.refs_1_ = bf16[256,1024]{1,0:T(8,128)(2,1)S(1)} collective-permute-done((bf16[256,1024]{1,0:T(8,128)(2,1)}, bf16[256,1024]{1,0:T(8,128)(2,1)S(1)}, u32[]{:S(2)}, u32[]{:S(2)}) %collective-permute-start.50) | collective-permute-done | bytes 524320 | tf_op jit(solution)/shard_map/ppermute | solution.py:20
  357.6 4.5 shard_map.242
  363.1 2.9 collective-permute-done.51.refs_0_.refs_4_
  367.6 4.5 shard_map.245
  372.2 4.9 shard_map.246
  377.9 3.2 collective-permute-done.53.refs_0_.refs_4_
  381.2 4.7 shard_map.247
  388.2 8.5 %shard_map.248 = (bf16[1024,1024]{1,0:T(8,128)(2,1)S(1)}, bf16[256,1024]{1,0:T(8,128)(2,1)S(1)}, bf16[256,1024]{1,0:T(8,128)(2,1)S(1)}, bf16[256,1024]{1,0:T(8,128)(2,1)S(1)}, bf16[256,1024]{1,0:T(8,128)(2,1)S(1)}) custom-call(s32[1]{0:T(128)} %bitcast.14.refs_0_, bf16[256,1024]{1,0:T(8,128)(2,1)} %copy-done.64, bf16[256,1024]{1,0:T(8,128)(2,1)} %copy-done.65, ...), custom_call_target="tpu_custom_call" | custom-call | flops 6899999744 | tf_op jit(solution)/shard_map/pallas_call | solution.py:104
  408.1 4.0 shard_map.251.refs_17_
  412.3 8.8 %shard_map.252 = (bf16[1024,1024]{1,0:T(8,128)(2,1)S(1)}, bf16[256,1024]{1,0:T(8,128)(2,1)S(1)}, bf16[256,1024]{1,0:T(8,128)(2,1)S(1)}, bf16[256,1024]{1,0:T(8,128)(2,1)S(1)}, bf16[256,1024]{1,0:T(8,128)(2,1)S(1)}) custom-call(s32[1]{0:T(128)} %bitcast.14.refs_0_, bf16[256,1024]{1,0:T(8,128)(2,1)} %copy-done.41, bf16[256,1024]{1,0:T(8,128)(2,1)} %copy-done.42, ...), custom_call_target="tpu_custom_call" | custom-call | flops 6899999744 | tf_op jit(solution)/shard_map/pallas_call | solution.py:104
  423.7 12.7 %shard_map.253 = (bf16[512,512]{1,0:T(8,128)(2,1)S(1)}, f32[512,1024]{1,0:T(8,128)S(1)}, bf16[512,1024]{1,0:T(8,128)(2,1)S(1)}) custom-call(bf16[256,1024]{1,0:T(8,128)(2,1)S(1)} %get-tuple-element.405.refs_6_.refs_0_.refs_1_, bf16[256,1024]{1,0:T(8,128)(2,1)S(1)} %collective-permute-done.54.refs_1_.refs_2_, bf16[1024,256]{1,0:T(8,128)(2,1)} %bitcast.9.refs_6_.refs_2_, ...), custom_call_target="tpu_custom_call" | custom-call | flops 12650000384 | tf_op jit(solution)/shard_map/pallas_call | solution.py:104
  438.2 12.8 %shard_map.254 = (bf16[512,512]{1,0:T(8,128)(2,1)S(1)}, f32[512,1024]{1,0:T(8,128)S(1)}, bf16[512,1024]{1,0:T(8,128)(2,1)S(1)}) custom-call(bf16[256,1024]{1,0:T(8,128)(2,1)S(1)} %get-tuple-element.420.refs_5_.refs_0_.refs_3_, bf16[256,1024]{1,0:T(8,128)(2,1)} %collective-permute-done.61.refs_1_.refs_4_, bf16[1024,256]{1,0:T(8,128)(2,1)} %bitcast.9.refs_6_.refs_2_, ...), custom_call_target="tpu_custom_call" | custom-call | flops 99999997952 | tf_op jit(solution)/shard_map/pallas_call | solution.py:104
  454.2 4.1 shard_map.255.refs_13_
  459.2 4.7 shard_map.256
  465.8 3.0 shard_map.257
  471.2 2.8 shard_map.258
  474.8 3.7 shard_map.259
  482.4 8.6 %shard_map.261 = (bf16[1024,768]{1,0:T(8,128)(2,1)S(1)}, bf16[256,768]{1,0:T(8,128)(2,1)}, bf16[256,768]{1,0:T(8,128)(2,1)S(1)}, bf16[256,768]{1,0:T(8,128)(2,1)S(1)}, bf16[256,768]{1,0:T(8,128)(2,1)S(1)}) custom-call(s32[1]{0:T(128)} %bitcast.14.refs_0_, bf16[256,1024]{1,0:T(8,128)(2,1)} %shard_map.194.rows_ref.refs_1_, ...), custom_call_target="tpu_custom_call" | custom-call | flops 6899999744 | tf_op jit(solution)/shard_map/pallas_call | solution.py:104
  505.5 2.7 shard_map.264.refs_1_
  519.6 4.4 collective-permute-done.79
  531.0 3.2 collective-permute-start.82
  539.1 4.4 fusion.5
  544.9 3.7 collective-permute-done.83
  554.0 7.8 %collective-permute-start.88 = (bf16[256,1024]{1,0:T(8,128)(2,1)S(1)}, bf16[256,1024]{1,0:T(8,128)(2,1)}, u32[]{:S(2)}, u32[]{:S(2)}) collective-permute-start(bf16[256,1024]{1,0:T(8,128)(2,1)S(1)} %get-tuple-element.529), channel_id=1, source_target_pairs={{0,4},{4,8},{8,12},{1,5},{5,9},{9,13},{2,6},{6,10},{10,14},{3,7},{... | collective-permute-start | bytes 1572872 | tf_op jit(solution)/shard_map/ppermute | solution.py:78
  (664 shorter events, 196.6 us)
Async XLA Ops:
  7.2 487.2 %reduce-scatter.3.cloned.1.call-start = ((), (), s32[]{:S(2)}) async-start(), calls=%async_computation.2 | async-start | bytes 2621440 | tf_op jit(solution)/shard_map/reduce_scatter | solution.py:722
  8.9 12.9 %collective-permute-start = (bf16[1024,768]{1,0:T(8,128)(2,1)S(1)}, bf16[1024,768]{1,0:T(8,128)(2,1)}, u32[]{:S(2)}, u32[]{:S(2)}) collective-permute-start(bf16[1024,768]{1,0:T(8,128)(2,1)S(1)} %pad_maximum_fusion.own_w_ref.refs_1_.refs_3_), channel_id=1, source_target_pairs={{0,1},{1,0},{2,3},{3,2},{4,5},{5,4},{6,7},{7,6},{8,9},{9,8},{10,11... | collective-permute-start | bytes 4718600 | tf_op jit(solution)/shard_map/ppermute | solution.py:20
  18.9 15.4 %collective-permute-start.2 = (bf16[256,1024]{1,0:T(8,128)(2,1)}, bf16[256,1024]{1,0:T(8,128)(2,1)}, u32[]{:S(2)}, u32[]{:S(2)}) collective-permute-start(bf16[256,1024]{1,0:T(8,128)(2,1)} %shard_map.194.rows_ref.refs_1_), channel_id=1, source_target_pairs={{0,2},{1,3},{2,0},{3,1},{4,6},{5,7},{6,4},{7,5},{8,10},{9,11},{10,... | collective-permute-start | bytes 1572872 | tf_op jit(solution)/shard_map/ppermute | solution.py:20
  21.5 16.8 %collective-permute-start.7 = (bf16[1024,256]{1,0:T(8,128)(2,1)}, bf16[1024,256]{1,0:T(8,128)(2,1)}, u32[]{:S(2)}, u32[]{:S(2)}) collective-permute-start(bf16[1024,256]{1,0:T(8,128)(2,1)} %bitcast.9.refs_6_.refs_2_), channel_id=1, source_target_pairs={{0,1},{1,0},{2,3},{3,2},{4,5},{5,4},{6,7},{7,6},{8,9},{9,8},{10,11... | collective-permute-start | bytes 1572872 | tf_op jit(solution)/shard_map/ppermute | solution.py:20
  38.3 34.9 %collective-permute-start.14 = (bf16[1024,1024]{1,0:T(8,128)(2,1)S(1)}, bf16[1024,1024]{1,0:T(8,128)(2,1)S(1)}, u32[]{:S(2)}, u32[]{:S(2)}) collective-permute-start(bf16[1024,1024]{1,0:T(8,128)(2,1)S(1)} %bitcast.91), channel_id=1, source_target_pairs={{0,1},{1,0},{2,3},{3,2},{4,5},{5,4},{6,7},{7,6},{8,9},{9,8},{10,11... | collective-permute-start | bytes 6291464 | tf_op jit(solution)/shard_map/ppermute | solution.py:20
  38.5 34.8 %collective-permute-start.15 = (bf16[1024,1024]{1,0:T(8,128)(2,1)S(1)}, bf16[1024,1024]{1,0:T(8,128)(2,1)S(1)}, u32[]{:S(2)}, u32[]{:S(2)}) collective-permute-start(bf16[1024,1024]{1,0:T(8,128)(2,1)S(1)} %bitcast.108), channel_id=1, source_target_pairs={{0,1},{1,0},{2,3},{3,2},{4,5},{5,4},{6,7},{7,6},{8,9},{9,8},{10,11... | collective-permute-start | bytes 6291464 | tf_op jit(solution)/shard_map/ppermute | solution.py:20
  39.0 14.0 %collective-permute-start.9 = (bf16[256,1024]{1,0:T(8,128)(2,1)S(1)}, bf16[256,1024]{1,0:T(8,128)(2,1)S(1)}, u32[]{:S(2)}, u32[]{:S(2)}) collective-permute-start(bf16[256,1024]{1,0:T(8,128)(2,1)S(1)} %shard_map.196.rows_ref.refs_3_), channel_id=1, source_target_pairs={{0,2},{1,3},{2,0},{3,1},{4,6},{5,7},{6,4},{7,5},{8,10},{9,11},{10,... | collective-permute-start | bytes 1572872 | tf_op jit(solution)/shard_map/ppermute | solution.py:20
  40.8 14.8 %collective-permute-start.10 = (bf16[256,512]{1,0:T(8,128)(2,1)S(1)}, bf16[256,512]{1,0:T(8,128)(2,1)S(1)}, u32[]{:S(2)}, u32[]{:S(2)}) collective-permute-start(bf16[256,512]{1,0:T(8,128)(2,1)S(1)} %get-tuple-element.283), channel_id=1, source_target_pairs={{0,1},{1,0},{2,3},{3,2},{4,5},{5,4},{6,7},{7,6},{8,9},{9,8},{10,11... | collective-permute-start | bytes 786440 | tf_op jit(solution)/shard_map/ppermute | solution.py:20
  40.8 15.4 %collective-permute-start.11 = (bf16[256,512]{1,0:T(8,128)(2,1)S(1)}, bf16[256,512]{1,0:T(8,128)(2,1)S(1)}, u32[]{:S(2)}, u32[]{:S(2)}) collective-permute-start(bf16[256,512]{1,0:T(8,128)(2,1)S(1)} %get-tuple-element.284), channel_id=1, source_target_pairs={{0,1},{1,0},{2,3},{3,2},{4,5},{5,4},{6,7},{7,6},{8,9},{9,8},{10,11... | collective-permute-start | bytes 786440 | tf_op jit(solution)/shard_map/ppermute | solution.py:20
  56.2 14.0 %collective-permute-start.8 = (bf16[256,1024]{1,0:T(8,128)(2,1)S(1)}, bf16[256,1024]{1,0:T(8,128)(2,1)S(1)}, u32[]{:S(2)}, u32[]{:S(2)}) collective-permute-start(bf16[256,1024]{1,0:T(8,128)(2,1)S(1)} %get-tuple-element.280), channel_id=1, source_target_pairs={{0,2},{1,3},{2,0},{3,1},{4,6},{5,7},{6,4},{7,5},{8,10},{9,11},{10,... | collective-permute-start | bytes 1572872 | tf_op jit(solution)/shard_map/ppermute | solution.py:20
  68.8 19.3 %collective-permute-start.17 = (bf16[256,1024]{1,0:T(8,128)(2,1)S(1)}, bf16[256,1024]{1,0:T(8,128)(2,1)S(1)}, u32[]{:S(2)}, u32[]{:S(2)}) collective-permute-start(bf16[256,1024]{1,0:T(8,128)(2,1)S(1)} %get-tuple-element.291), channel_id=1, source_target_pairs={{0,2},{1,3},{2,0},{3,1},{4,6},{5,7},{6,4},{7,5},{8,10},{9,11},{10,... | collective-permute-start | bytes 1572872 | tf_op jit(solution)/shard_map/ppermute | solution.py:20
  71.5 23.3 %collective-permute-start.16 = (bf16[256,1024]{1,0:T(8,128)(2,1)S(1)}, bf16[256,1024]{1,0:T(8,128)(2,1)S(1)}, u32[]{:S(2)}, u32[]{:S(2)}) collective-permute-start(bf16[256,1024]{1,0:T(8,128)(2,1)S(1)} %get-tuple-element.289.rows_ref.refs_1_), channel_id=1, source_target_pairs={{0,2},{1,3},{2,0},{3,1},{4,6},{5,7},{6,4},{7,5},{8,10},{9,11},{10,... | collective-permute-start | bytes 1572872 | tf_op jit(solution)/shard_map/ppermute | solution.py:20
  89.1 17.0 %collective-permute-start.19 = (bf16[256,1024]{1,0:T(8,128)(2,1)S(1)}, bf16[256,1024]{1,0:T(8,128)(2,1)S(1)}, u32[]{:S(2)}, u32[]{:S(2)}) collective-permute-start(bf16[256,1024]{1,0:T(8,128)(2,1)S(1)} %get-tuple-element.293.rows_ref.refs_3_), channel_id=1, source_target_pairs={{0,2},{1,3},{2,0},{3,1},{4,6},{5,7},{6,4},{7,5},{8,10},{9,11},{10,... | collective-permute-start | bytes 1572872 | tf_op jit(solution)/shard_map/ppermute | solution.py:20
  100.8 16.5 %collective-permute-start.18 = (bf16[256,1024]{1,0:T(8,128)(2,1)S(1)}, bf16[256,1024]{1,0:T(8,128)(2,1)S(1)}, u32[]{:S(2)}, u32[]{:S(2)}) collective-permute-start(bf16[256,1024]{1,0:T(8,128)(2,1)S(1)} %get-tuple-element.296.refs_6_), channel_id=1, source_target_pairs={{0,2},{1,3},{2,0},{3,1},{4,6},{5,7},{6,4},{7,5},{8,10},{9,11},{10,... | collective-permute-start | bytes 1572872 | tf_op jit(solution)/shard_map/ppermute | solution.py:20
  110.1 17.2 %collective-permute-start.22 = (bf16[256,1024]{1,0:T(8,128)(2,1)S(1)}, bf16[256,1024]{1,0:T(8,128)(2,1)S(1)}, u32[]{:S(2)}, u32[]{:S(2)}) collective-permute-start(bf16[256,1024]{1,0:T(8,128)(2,1)S(1)} %get-tuple-element.298.refs_5_), channel_id=1, source_target_pairs={{0,2},{1,3},{2,0},{3,1},{4,6},{5,7},{6,4},{7,5},{8,10},{9,11},{10,... | collective-permute-start | bytes 1572872 | tf_op jit(solution)/shard_map/ppermute | solution.py:20
  117.7 14.5 %collective-permute-start.20 = (bf16[256,1024]{1,0:T(8,128)(2,1)S(1)}, bf16[256,1024]{1,0:T(8,128)(2,1)S(1)}, u32[]{:S(2)}, u32[]{:S(2)}) collective-permute-start(bf16[256,1024]{1,0:T(8,128)(2,1)S(1)} %get-tuple-element.301.refs_5_), channel_id=1, source_target_pairs={{0,16},{1,17},{2,18},{3,19},{4,20},{5,21},{6,22},{7,23},{8,24},{9,... | collective-permute-start | bytes 1572872 | tf_op jit(solution)/shard_map/ppermute | solution.py:664
  128.5 13.6 %collective-permute-start.23 = (bf16[256,1024]{1,0:T(8,128)(2,1)S(1)}, bf16[256,1024]{1,0:T(8,128)(2,1)S(1)}, u32[]{:S(2)}, u32[]{:S(2)}) collective-permute-start(bf16[256,1024]{1,0:T(8,128)(2,1)S(1)} %get-tuple-element.305), channel_id=1, source_target_pairs={{0,16},{1,17},{2,18},{3,19},{4,20},{5,21},{6,22},{7,23},{8,24},{9,... | collective-permute-start | bytes 1572872 | tf_op jit(solution)/shard_map/ppermute | solution.py:664
  132.6 12.7 %collective-permute-start.21 = (bf16[256,1024]{1,0:T(8,128)(2,1)S(1)}, bf16[256,1024]{1,0:T(8,128)(2,1)S(1)}, u32[]{:S(2)}, u32[]{:S(2)}) collective-permute-start(bf16[256,1024]{1,0:T(8,128)(2,1)S(1)} %shard_map.209.rows_ref.refs_9_), channel_id=1, source_target_pairs={{0,2},{1,3},{2,0},{3,1},{4,6},{5,7},{6,4},{7,5},{8,10},{9,11},{10,... | collective-permute-start | bytes 1572872 | tf_op jit(solution)/shard_map/ppermute | solution.py:20
  136.5 13.7 %collective-permute-start.24 = (bf16[256,512]{1,0:T(8,128)(2,1)S(1)}, bf16[256,512]{1,0:T(8,128)(2,1)S(1)}, u32[]{:S(2)}, u32[]{:S(2)}) collective-permute-start(bf16[256,512]{1,0:T(8,128)(2,1)S(1)} %get-tuple-element.309), channel_id=1, source_target_pairs={{0,1},{1,0},{2,3},{3,2},{4,5},{5,4},{6,7},{7,6},{8,9},{9,8},{10,11... | collective-permute-start | bytes 786440 | tf_op jit(solution)/shard_map/ppermute | solution.py:20
  136.6 13.6 %collective-permute-start.25 = (bf16[256,512]{1,0:T(8,128)(2,1)S(1)}, bf16[256,512]{1,0:T(8,128)(2,1)S(1)}, u32[]{:S(2)}, u32[]{:S(2)}) collective-permute-start(bf16[256,512]{1,0:T(8,128)(2,1)S(1)} %get-tuple-element.310), channel_id=1, source_target_pairs={{0,1},{1,0},{2,3},{3,2},{4,5},{5,4},{6,7},{7,6},{8,9},{9,8},{10,11... | collective-permute-start | bytes 786440 | tf_op jit(solution)/shard_map/ppermute | solution.py:20
  148.4 14.0 %collective-permute-start.29 = (bf16[256,1024]{1,0:T(8,128)(2,1)S(1)}, bf16[256,1024]{1,0:T(8,128)(2,1)S(1)}, u32[]{:S(2)}, u32[]{:S(2)}) collective-permute-start(bf16[256,1024]{1,0:T(8,128)(2,1)S(1)} %shard_map.212.rows_ref.refs_11_), channel_id=1, source_target_pairs={{0,2},{1,3},{2,0},{3,1},{4,6},{5,7},{6,4},{7,5},{8,10},{9,11},{10,... | collective-permute-start | bytes 1572872 | tf_op jit(solution)/shard_map/ppermute | solution.py:20
  150.2 17.5 %collective-permute-start.30 = (bf16[256,512]{1,0:T(8,128)(2,1)S(1)}, bf16[256,512]{1,0:T(8,128)(2,1)S(1)}, u32[]{:S(2)}, u32[]{:S(2)}) collective-permute-start(bf16[256,512]{1,0:T(8,128)(2,1)S(1)} %get-tuple-element.317), channel_id=1, source_target_pairs={{0,1},{1,0},{2,3},{3,2},{4,5},{5,4},{6,7},{7,6},{8,9},{9,8},{10,11... | collective-permute-start | bytes 786440 | tf_op jit(solution)/shard_map/ppermute | solution.py:20
  150.3 17.5 %collective-permute-start.31 = (bf16[256,512]{1,0:T(8,128)(2,1)S(1)}, bf16[256,512]{1,0:T(8,128)(2,1)S(1)}, u32[]{:S(2)}, u32[]{:S(2)}) collective-permute-start(bf16[256,512]{1,0:T(8,128)(2,1)S(1)} %get-tuple-element.318), channel_id=1, source_target_pairs={{0,1},{1,0},{2,3},{3,2},{4,5},{5,4},{6,7},{7,6},{8,9},{9,8},{10,11... | collective-permute-start | bytes 786440 | tf_op jit(solution)/shard_map/ppermute | solution.py:20
  166.0 13.9 %collective-permute-start.28 = (bf16[256,1024]{1,0:T(8,128)(2,1)S(1)}, bf16[256,1024]{1,0:T(8,128)(2,1)S(1)}, u32[]{:S(2)}, u32[]{:S(2)}) collective-permute-start(bf16[256,1024]{1,0:T(8,128)(2,1)S(1)} %get-tuple-element.314), channel_id=1, source_target_pairs={{0,2},{1,3},{2,0},{3,1},{4,6},{5,7},{6,4},{7,5},{8,10},{9,11},{10,... | collective-permute-start | bytes 1572872 | tf_op jit(solution)/shard_map/ppermute | solution.py:20
  177.5 14.9 %collective-permute-start.35 = (bf16[256,1024]{1,0:T(8,128)(2,1)S(1)}, bf16[256,1024]{1,0:T(8,128)(2,1)S(1)}, u32[]{:S(2)}, u32[]{:S(2)}) collective-permute-start(bf16[256,1024]{1,0:T(8,128)(2,1)S(1)} %get-tuple-element.325), channel_id=1, source_target_pairs={{0,2},{1,3},{2,0},{3,1},{4,6},{5,7},{6,4},{7,5},{8,10},{9,11},{10,... | collective-permute-start | bytes 1572872 | tf_op jit(solution)/shard_map/ppermute | solution.py:20
  180.4 23.1 %collective-permute-start.34 = (bf16[256,1024]{1,0:T(8,128)(2,1)S(1)}, bf16[256,1024]{1,0:T(8,128)(2,1)S(1)}, u32[]{:S(2)}, u32[]{:S(2)}) collective-permute-start(bf16[256,1024]{1,0:T(8,128)(2,1)S(1)} %get-tuple-element.323.rows_ref.refs_9_), channel_id=1, source_target_pairs={{0,2},{1,3},{2,0},{3,1},{4,6},{5,7},{6,4},{7,5},{8,10},{9,11},{10,... | collective-permute-start | bytes 1572872 | tf_op jit(solution)/shard_map/ppermute | solution.py:20
  192.9 21.9 %collective-permute-start.37 = (bf16[256,1024]{1,0:T(8,128)(2,1)S(1)}, bf16[256,1024]{1,0:T(8,128)(2,1)S(1)}, u32[]{:S(2)}, u32[]{:S(2)}) collective-permute-start(bf16[256,1024]{1,0:T(8,128)(2,1)S(1)} %get-tuple-element.327.rows_ref.refs_11_), channel_id=1, source_target_pairs={{0,2},{1,3},{2,0},{3,1},{4,6},{5,7},{6,4},{7,5},{8,10},{9,11},{10,... | collective-permute-start | bytes 1572872 | tf_op jit(solution)/shard_map/ppermute | solution.py:20
  209.7 16.4 %collective-permute-start.36 = (bf16[256,1024]{1,0:T(8,128)(2,1)S(1)}, bf16[256,1024]{1,0:T(8,128)(2,1)S(1)}, u32[]{:S(2)}, u32[]{:S(2)}) collective-permute-start(bf16[256,1024]{1,0:T(8,128)(2,1)S(1)} %get-tuple-element.330.refs_6_), channel_id=1, source_target_pairs={{0,2},{1,3},{2,0},{3,1},{4,6},{5,7},{6,4},{7,5},{8,10},{9,11},{10,... | collective-permute-start | bytes 1572872 | tf_op jit(solution)/shard_map/ppermute | solution.py:20
  219.2 18.1 %collective-permute-start.39 = (bf16[256,1024]{1,0:T(8,128)(2,1)S(1)}, bf16[256,1024]{1,0:T(8,128)(2,1)S(1)}, u32[]{:S(2)}, u32[]{:S(2)}) collective-permute-start(bf16[256,1024]{1,0:T(8,128)(2,1)S(1)} %get-tuple-element.332.refs_5_), channel_id=1, source_target_pairs={{0,2},{1,3},{2,0},{3,1},{4,6},{5,7},{6,4},{7,5},{8,10},{9,11},{10,... | collective-permute-start | bytes 1572872 | tf_op jit(solution)/shard_map/ppermute | solution.py:20
  226.6 21.9 %collective-permute-start.38 = (bf16[256,1024]{1,0:T(8,128)(2,1)S(1)}, bf16[256,1024]{1,0:T(8,128)(2,1)S(1)}, u32[]{:S(2)}, u32[]{:S(2)}) collective-permute-start(bf16[256,1024]{1,0:T(8,128)(2,1)S(1)} %get-tuple-element.336.rows_ref.refs_9_), channel_id=1, source_target_pairs={{0,2},{1,3},{2,0},{3,1},{4,6},{5,7},{6,4},{7,5},{8,10},{9,11},{10,... | collective-permute-start | bytes 1572872 | tf_op jit(solution)/shard_map/ppermute | solution.py:20
  238.6 21.2 %collective-permute-start.41 = (bf16[256,1024]{1,0:T(8,128)(2,1)S(1)}, bf16[256,1024]{1,0:T(8,128)(2,1)S(1)}, u32[]{:S(2)}, u32[]{:S(2)}) collective-permute-start(bf16[256,1024]{1,0:T(8,128)(2,1)S(1)} %get-tuple-element.343.rows_ref.refs_11_), channel_id=1, source_target_pairs={{0,2},{1,3},{2,0},{3,1},{4,6},{5,7},{6,4},{7,5},{8,10},{9,11},{10,... | collective-permute-start | bytes 1572872 | tf_op jit(solution)/shard_map/ppermute | solution.py:20
  254.3 16.8 %collective-permute-start.40 = (bf16[256,1024]{1,0:T(8,128)(2,1)S(1)}, bf16[256,1024]{1,0:T(8,128)(2,1)S(1)}, u32[]{:S(2)}, u32[]{:S(2)}) collective-permute-start(bf16[256,1024]{1,0:T(8,128)(2,1)S(1)} %get-tuple-element.348.refs_6_), channel_id=1, source_target_pairs={{0,2},{1,3},{2,0},{3,1},{4,6},{5,7},{6,4},{7,5},{8,10},{9,11},{10,... | collective-permute-start | bytes 1572872 | tf_op jit(solution)/shard_map/ppermute | solution.py:20
  264.9 17.4 %collective-permute-start.43 = (bf16[256,1024]{1,0:T(8,128)(2,1)S(1)}, bf16[256,1024]{1,0:T(8,128)(2,1)S(1)}, u32[]{:S(2)}, u32[]{:S(2)}) collective-permute-start(bf16[256,1024]{1,0:T(8,128)(2,1)S(1)} %get-tuple-element.351.refs_6_), channel_id=1, source_target_pairs={{0,2},{1,3},{2,0},{3,1},{4,6},{5,7},{6,4},{7,5},{8,10},{9,11},{10,... | collective-permute-start | bytes 1572872 | tf_op jit(solution)/shard_map/ppermute | solution.py:20
  272.1 21.3 %collective-permute-start.42 = (bf16[256,1024]{1,0:T(8,128)(2,1)S(1)}, bf16[256,1024]{1,0:T(8,128)(2,1)S(1)}, u32[]{:S(2)}, u32[]{:S(2)}) collective-permute-start(bf16[256,1024]{1,0:T(8,128)(2,1)S(1)} %get-tuple-element.354.refs_6_.refs_0_.refs_7_), channel_id=1, source_target_pairs={{0,2},{1,3},{2,0},{3,1},{4,6},{5,7},{6,4},{7,5},{8,10},{9,11},{10,... | collective-permute-start | bytes 1572872 | tf_op jit(solution)/shard_map/ppermute | solution.py:20
  284.3 22.0 %collective-permute-start.45 = (bf16[256,1024]{1,0:T(8,128)(2,1)S(1)}, bf16[256,1024]{1,0:T(8,128)(2,1)S(1)}, u32[]{:S(2)}, u32[]{:S(2)}) collective-permute-start(bf16[256,1024]{1,0:T(8,128)(2,1)S(1)} %get-tuple-element.357.refs_12_.refs_0_.refs_9_), channel_id=1, source_target_pairs={{0,2},{1,3},{2,0},{3,1},{4,6},{5,7},{6,4},{7,5},{8,10},{9,11},{10,... | collective-permute-start | bytes 1572872 | tf_op jit(solution)/shard_map/ppermute | solution.py:20
  306.2 13.2 %collective-permute-start.44 = (bf16[512,1024]{1,0:T(8,128)(2,1)S(1)}, bf16[512,1024]{1,0:T(8,128)(2,1)S(1)}, u32[]{:S(2)}, u32[]{:S(2)}) collective-permute-start(bf16[512,1024]{1,0:T(8,128)(2,1)S(1)} %get-tuple-element.363), channel_id=1, source_target_pairs={{0,1},{1,0},{2,3},{3,2},{4,5},{5,4},{6,7},{7,6},{8,9},{9,8},{10,11... | collective-permute-start | bytes 3145736 | tf_op jit(solution)/shard_map/ppermute | solution.py:20
  322.3 14.8 %collective-permute-start.46 = (bf16[256,1024]{1,0:T(8,128)(2,1)S(1)}, bf16[256,1024]{1,0:T(8,128)(2,1)S(1)}, u32[]{:S(2)}, u32[]{:S(2)}) collective-permute-start(bf16[256,1024]{1,0:T(8,128)(2,1)S(1)} %get-tuple-element.368.refs_5_), channel_id=1, source_target_pairs={{0,2},{1,3},{2,0},{3,1},{4,6},{5,7},{6,4},{7,5},{8,10},{9,11},{10,... | collective-permute-start | bytes 1572872 | tf_op jit(solution)/shard_map/ppermute | solution.py:20
  329.7 17.8 %collective-permute-start.50 = (bf16[256,1024]{1,0:T(8,128)(2,1)}, bf16[256,1024]{1,0:T(8,128)(2,1)S(1)}, u32[]{:S(2)}, u32[]{:S(2)}) collective-permute-start(bf16[256,1024]{1,0:T(8,128)(2,1)} %get-tuple-element.372.refs_5_), channel_id=1, source_target_pairs={{0,2},{1,3},{2,0},{3,1},{4,6},{5,7},{6,4},{7,5},{8,10},{9,11},{10,... | collective-permute-start | bytes 1572872 | tf_op jit(solution)/shard_map/ppermute | solution.py:20
  338.0 14.2 %collective-permute-start.48 = (bf16[256,1024]{1,0:T(8,128)(2,1)S(1)}, bf16[256,1024]{1,0:T(8,128)(2,1)S(1)}, u32[]{:S(2)}, u32[]{:S(2)}) collective-permute-start(bf16[256,1024]{1,0:T(8,128)(2,1)S(1)} %get-tuple-element.376.refs_5_), channel_id=1, source_target_pairs={{16,0},{17,1},{18,2},{19,3},{20,4},{21,5},{22,6},{23,7},{24,8},{25... | collective-permute-start | bytes 1572872 | tf_op jit(solution)/shard_map/ppermute | solution.py:669
  350.8 15.2 %collective-permute-start.51 = (bf16[256,1024]{1,0:T(8,128)(2,1)S(1)}, bf16[256,1024]{1,0:T(8,128)(2,1)S(1)}, u32[]{:S(2)}, u32[]{:S(2)}) collective-permute-start(bf16[256,1024]{1,0:T(8,128)(2,1)S(1)} %get-tuple-element.383), channel_id=1, source_target_pairs={{16,0},{17,1},{18,2},{19,3},{20,4},{21,5},{22,6},{23,7},{24,8},{25... | collective-permute-start | bytes 1572872 | tf_op jit(solution)/shard_map/ppermute | solution.py:669
  355.4 16.8 %collective-permute-start.49 = (bf16[256,1024]{1,0:T(8,128)(2,1)S(1)}, bf16[256,1024]{1,0:T(8,128)(2,1)S(1)}, u32[]{:S(2)}, u32[]{:S(2)}) collective-permute-start(bf16[256,1024]{1,0:T(8,128)(2,1)S(1)} %get-tuple-element.378.rows_ref.refs_1_), channel_id=1, source_target_pairs={{0,2},{1,3},{2,0},{3,1},{4,6},{5,7},{6,4},{7,5},{8,10},{9,11},{10,... | collective-permute-start | bytes 1572872 | tf_op jit(solution)/shard_map/ppermute | solution.py:20
  366.2 14.9 %collective-permute-start.53 = (bf16[256,1024]{1,0:T(8,128)(2,1)S(1)}, bf16[256,1024]{1,0:T(8,128)(2,1)S(1)}, u32[]{:S(2)}, u32[]{:S(2)}) collective-permute-start(bf16[256,1024]{1,0:T(8,128)(2,1)S(1)} %get-tuple-element.385.rows_ref.refs_3_), channel_id=1, source_target_pairs={{0,2},{1,3},{2,0},{3,1},{4,6},{5,7},{6,4},{7,5},{8,10},{9,11},{10,... | collective-permute-start | bytes 1572872 | tf_op jit(solution)/shard_map/ppermute | solution.py:20
  377.2 21.5 %collective-permute-start.52 = (bf16[256,1024]{1,0:T(8,128)(2,1)S(1)}, bf16[256,1024]{1,0:T(8,128)(2,1)S(1)}, u32[]{:S(2)}, u32[]{:S(2)}) collective-permute-start(bf16[256,1024]{1,0:T(8,128)(2,1)S(1)} %get-tuple-element.390.refs_6_), channel_id=1, source_target_pairs={{0,2},{1,3},{2,0},{3,1},{4,6},{5,7},{6,4},{7,5},{8,10},{9,11},{10,... | collective-permute-start | bytes 1572872 | tf_op jit(solution)/shard_map/ppermute | solution.py:20
  386.9 15.3 %collective-permute-start.59 = (bf16[256,1024]{1,0:T(8,128)(2,1)S(1)}, bf16[256,1024]{1,0:T(8,128)(2,1)S(1)}, u32[]{:S(2)}, u32[]{:S(2)}) collective-permute-start(bf16[256,1024]{1,0:T(8,128)(2,1)S(1)} %get-tuple-element.401.refs_17_), channel_id=1, source_target_pairs={{0,2},{1,3},{2,0},{3,1},{4,6},{5,7},{6,4},{7,5},{8,10},{9,11},{10,... | collective-permute-start | bytes 1572872 | tf_op jit(solution)/shard_map/ppermute | solution.py:20
  402.2 20.4 %collective-permute-start.54 = (bf16[256,1024]{1,0:T(8,128)(2,1)S(1)}, bf16[256,1024]{1,0:T(8,128)(2,1)S(1)}, u32[]{:S(2)}, u32[]{:S(2)}) collective-permute-start(bf16[256,1024]{1,0:T(8,128)(2,1)S(1)} %get-tuple-element.405.refs_6_.refs_0_.refs_1_), channel_id=1, source_target_pairs={{0,2},{1,3},{2,0},{3,1},{4,6},{5,7},{6,4},{7,5},{8,10},{9,11},{10,... | collective-permute-start | bytes 1572872 | tf_op jit(solution)/shard_map/ppermute | solution.py:20
  405.6 31.6 %collective-permute-start.61 = (bf16[256,1024]{1,0:T(8,128)(2,1)S(1)}, bf16[256,1024]{1,0:T(8,128)(2,1)}, u32[]{:S(2)}, u32[]{:S(2)}) collective-permute-start(bf16[256,1024]{1,0:T(8,128)(2,1)S(1)} %get-tuple-element.420.refs_5_.refs_0_.refs_3_), channel_id=1, source_target_pairs={{0,2},{1,3},{2,0},{3,1},{4,6},{5,7},{6,4},{7,5},{8,10},{9,11},{10,... | collective-permute-start | bytes 1572872 | tf_op jit(solution)/shard_map/ppermute | solution.py:20
  412.2 92.3 %reduce-scatter.5.cloned.1.call-start = ((), (), s32[]{:S(2)}) async-start(), calls=%async_computation.3 | async-start | bytes 2621440 | tf_op jit(solution)/shard_map/reduce_scatter | solution.py:722
  422.5 30.3 %collective-permute-start.62 = (bf16[256,1024]{1,0:T(8,128)(2,1)S(1)}, bf16[256,1024]{1,0:T(8,128)(2,1)S(1)}, u32[]{:S(2)}, u32[]{:S(2)}) collective-permute-start(bf16[256,1024]{1,0:T(8,128)(2,1)S(1)} %get-tuple-element.430), channel_id=1, source_target_pairs={{0,1},{1,0},{2,3},{3,2},{4,5},{5,4},{6,7},{7,6},{8,9},{9,8},{10,11... | collective-permute-start | bytes 1572872 | tf_op jit(solution)/shard_map/ppermute | solution.py:20
  422.5 30.3 %collective-permute-start.63 = (bf16[256,1024]{1,0:T(8,128)(2,1)S(1)}, bf16[256,1024]{1,0:T(8,128)(2,1)S(1)}, u32[]{:S(2)}, u32[]{:S(2)}) collective-permute-start(bf16[256,1024]{1,0:T(8,128)(2,1)S(1)} %get-tuple-element.431), channel_id=1, source_target_pairs={{0,1},{1,0},{2,3},{3,2},{4,5},{5,4},{6,7},{7,6},{8,9},{9,8},{10,11... | collective-permute-start | bytes 1572872 | tf_op jit(solution)/shard_map/ppermute | solution.py:20
  423.0 29.8 %collective-permute-start.64 = (bf16[256,1024]{1,0:T(8,128)(2,1)S(1)}, bf16[256,1024]{1,0:T(8,128)(2,1)S(1)}, u32[]{:S(2)}, u32[]{:S(2)}) collective-permute-start(bf16[256,1024]{1,0:T(8,128)(2,1)S(1)} %get-tuple-element.432), channel_id=1, source_target_pairs={{0,1},{1,0},{2,3},{3,2},{4,5},{5,4},{6,7},{7,6},{8,9},{9,8},{10,11... | collective-permute-start | bytes 1572872 | tf_op jit(solution)/shard_map/ppermute | solution.py:20
  423.1 29.8 %collective-permute-start.65 = (bf16[256,1024]{1,0:T(8,128)(2,1)S(1)}, bf16[256,1024]{1,0:T(8,128)(2,1)S(1)}, u32[]{:S(2)}, u32[]{:S(2)}) collective-permute-start(bf16[256,1024]{1,0:T(8,128)(2,1)S(1)} %get-tuple-element.433), channel_id=1, source_target_pairs={{0,1},{1,0},{2,3},{3,2},{4,5},{5,4},{6,7},{7,6},{8,9},{9,8},{10,11... | collective-permute-start | bytes 1572872 | tf_op jit(solution)/shard_map/ppermute | solution.py:20
  459.1 15.8 %collective-permute-start.67 = (bf16[512,1024]{1,0:T(8,128)(2,1)}, bf16[512,1024]{1,0:T(8,128)(2,1)S(1)}, u32[]{:S(2)}, u32[]{:S(2)}) collective-permute-start(bf16[512,1024]{1,0:T(8,128)(2,1)} %copy-done.33), channel_id=1, source_target_pairs={{0,1},{1,0},{2,3},{3,2},{4,5},{5,4},{6,7},{7,6},{8,9},{9,8},{10,11... | collective-permute-start | bytes 3145736 | tf_op jit(solution)/shard_map/ppermute | solution.py:20
  464.7 31.7 %collective-permute-start.73 = (bf16[256,256]{1,0:T(8,128)(2,1)}, bf16[256,256]{1,0:T(8,128)(2,1)}, u32[]{:S(2)}, u32[]{:S(2)}) collective-permute-start(bf16[256,256]{1,0:T(8,128)(2,1)} %get-tuple-element.491), channel_id=1, source_target_pairs={{0,1},{1,0},{2,3},{3,2},{4,5},{5,4},{6,7},{7,6},{8,9},{9,8},{10,11... | collective-permute-start | bytes 393224 | tf_op jit(solution)/shard_map/ppermute | solution.py:20
  465.3 31.7 %collective-permute-start.74 = (bf16[256,256]{1,0:T(8,128)(2,1)}, bf16[256,256]{1,0:T(8,128)(2,1)}, u32[]{:S(2)}, u32[]{:S(2)}) collective-permute-start(bf16[256,256]{1,0:T(8,128)(2,1)} %get-tuple-element.492), channel_id=1, source_target_pairs={{0,1},{1,0},{2,3},{3,2},{4,5},{5,4},{6,7},{7,6},{8,9},{9,8},{10,11... | collective-permute-start | bytes 393224 | tf_op jit(solution)/shard_map/ppermute | solution.py:20
  465.3 34.4 %collective-permute-start.75 = (bf16[256,256]{1,0:T(8,128)(2,1)}, bf16[256,256]{1,0:T(8,128)(2,1)}, u32[]{:S(2)}, u32[]{:S(2)}) collective-permute-start(bf16[256,256]{1,0:T(8,128)(2,1)} %get-tuple-element.493), channel_id=1, source_target_pairs={{0,1},{1,0},{2,3},{3,2},{4,5},{5,4},{6,7},{7,6},{8,9},{9,8},{10,11... | collective-permute-start | bytes 393224 | tf_op jit(solution)/shard_map/ppermute | solution.py:20
  469.8 24.6 %collective-permute-start.66 = (bf16[256,1024]{1,0:T(8,128)(2,1)S(1)}, bf16[256,1024]{1,0:T(8,128)(2,1)S(1)}, u32[]{:S(2)}, u32[]{:S(2)}) collective-permute-start(bf16[256,1024]{1,0:T(8,128)(2,1)S(1)} %get-tuple-element.437.refs_5_), channel_id=1, source_target_pairs={{0,2},{1,3},{2,0},{3,1},{4,6},{5,7},{6,4},{7,5},{8,10},{9,11},{10,... | collective-permute-start | bytes 1572872 | tf_op jit(solution)/shard_map/ppermute | solution.py:20
  478.5 18.6 %collective-permute-start.68 = (bf16[256,1024]{1,0:T(8,128)(2,1)}, bf16[256,1024]{1,0:T(8,128)(2,1)}, u32[]{:S(2)}, u32[]{:S(2)}) collective-permute-start(bf16[256,1024]{1,0:T(8,128)(2,1)} %get-tuple-element.443.refs_5_), channel_id=1, source_target_pairs={{0,2},{1,3},{2,0},{3,1},{4,6},{5,7},{6,4},{7,5},{8,10},{9,11},{10,... | collective-permute-start | bytes 1572872 | tf_op jit(solution)/shard_map/ppermute | solution.py:20
  510.3 13.8 %collective-permute-start.79 = (bf16[256,1024]{1,0:T(8,128)(2,1)S(1)}, bf16[256,1024]{1,0:T(8,128)(2,1)S(1)}, u32[]{:S(2)}, u32[]{:S(2)}) collective-permute-start(bf16[256,1024]{1,0:T(8,128)(2,1)S(1)} %get-tuple-element.523), channel_id=1, source_target_pairs={{0,4},{1,5},{2,6},{3,7},{16,20},{17,21},{18,22},{19,23}} | collective-permute-start | bytes 1572872 | tf_op jit(solution)/shard_map/ppermute | solution.py:78
  512.4 12.4 %collective-permute-start.80 = (bf16[256,1024]{1,0:T(8,128)(2,1)S(1)}, bf16[256,1024]{1,0:T(8,128)(2,1)S(1)}, u32[]{:S(2)}, u32[]{:S(2)}) collective-permute-start(bf16[256,1024]{1,0:T(8,128)(2,1)S(1)} %get-tuple-element.524), channel_id=1, source_target_pairs={{12,8},{13,9},{14,10},{15,11},{28,24},{29,25},{30,26},{31,27}} | collective-permute-start | bytes 1572872 | tf_op jit(solution)/shard_map/ppermute | solution.py:79
  531.0 12.5 %collective-permute-start.82 = (f32[2,22528]{1,0:T(2,128)S(1)}, f32[2,22528]{1,0:T(2,128)}, u32[]{:S(2)}, u32[]{:S(2)}) collective-permute-start(f32[2,22528]{1,0:T(2,128)S(1)} %pad_maximum_fusion.2), channel_id=1, source_target_pairs={{0,8},{4,12},{8,0},{12,4},{1,9},{5,13},{9,1},{13,5},{2,10},{6,14},... | collective-permute-start | bytes 540680 | tf_op jit(solution)/shard_map/ppermute | solution.py:58
  535.6 12.9 %collective-permute-start.83 = (bf16[256,1024]{1,0:T(8,128)(2,1)}, bf16[256,1024]{1,0:T(8,128)(2,1)S(1)}, u32[]{:S(2)}, u32[]{:S(2)}) collective-permute-start(bf16[256,1024]{1,0:T(8,128)(2,1)} %get-tuple-element.526), channel_id=1, source_target_pairs={{0,4},{4,8},{1,5},{5,9},{2,6},{6,10},{3,7},{7,11},{16,20},{20,24},... | collective-permute-start | bytes 1572872 | tf_op jit(solution)/shard_map/ppermute | solution.py:78
  548.6 16.0 %collective-permute-start.85 = (f32[2,1024]{1,0:T(2,128)S(1)}, f32[2,1024]{1,0:T(2,128)S(1)}, u32[]{:S(2)}, u32[]{:S(2)}) collective-permute-start(f32[2,1024]{1,0:T(2,128)S(1)} %fusion.5), channel_id=1, source_target_pairs={{0,16},{16,0},{1,17},{17,1},{2,18},{18,2},{3,19},{19,3},{4,20},{20... | collective-permute-start | bytes 24584 | tf_op jit(solution)/shard_map/ppermute | solution.py:862
  552.8 17.3 %collective-permute-start.89 = (bf16[256,1024]{1,0:T(8,128)(2,1)}, bf16[256,1024]{1,0:T(8,128)(2,1)S(1)}, u32[]{:S(2)}, u32[]{:S(2)}) collective-permute-start(bf16[256,1024]{1,0:T(8,128)(2,1)} %get-tuple-element.530), channel_id=1, source_target_pairs={{4,0},{8,4},{12,8},{5,1},{9,5},{13,9},{6,2},{10,6},{14,10},{7,3},{... | collective-permute-start | bytes 1572872 | tf_op jit(solution)/shard_map/ppermute | solution.py:79
  554.0 16.1 %collective-permute-start.88 = (bf16[256,1024]{1,0:T(8,128)(2,1)S(1)}, bf16[256,1024]{1,0:T(8,128)(2,1)}, u32[]{:S(2)}, u32[]{:S(2)}) collective-permute-start(bf16[256,1024]{1,0:T(8,128)(2,1)S(1)} %get-tuple-element.529), channel_id=1, source_target_pairs={{0,4},{4,8},{8,12},{1,5},{5,9},{9,13},{2,6},{6,10},{10,14},{3,7},{... | collective-permute-start | bytes 1572872 | tf_op jit(solution)/shard_map/ppermute | solution.py:78
  (214 other events, 3289.7 us)
Sparse Core Ops, SparseCore 0:
  412.3 45.9 reduce-scatter.2
  460.7 43.6 reduce-scatter.4

commit v3 on v2

--- a/solution.py
+++ b/solution.py
@@ -49,12 +49,13 @@
 SHARE = 1
 
 
-def over_dp(block):
+def over_dp(block, begun):
     count = lax.axis_size("dp")
     if count & (count - 1):
         return lax.all_gather(block, "dp", axis=0, tiled=True)
     bit = 1
     while bit < count:
+        block = tied(block, begun.pop(0) if begun else None)
         other = lax.ppermute(block, "dp", [(i, i ^ bit) for i in range(count)])
         block = jnp.concatenate([block, other], 0)
         bit *= 2
@@ -233,25 +234,19 @@
 
 
 def mlp_kernel(
-    rows_ref, own_w1_ref, other_w1_ref, bias_ref, own_w2_ref, other_w2_ref, act_out, slope_out, out_ref, act_ref, slope_ref, sems
+    rows_ref, own_w1_ref, other_w1_ref, bias_ref, own_w2_ref, other_w2_ref, act_out, slope_out, out_ref, act_ref
 ):
     width = own_w1_ref.shape[1]
     tile = 256
-    copies = []
     for group, w1_ref in enumerate((own_w1_ref, other_w1_ref)):
         for first in range(0, width, tile):
             cols = slice(group * width + first, group * width + first + tile)
             value, slope = gelu_both(dot_nn(rows_ref[...], w1_ref[:, first : first + tile]) + bias_ref[:, cols])
             act_ref[:, cols] = value.astype(BF)
-            slope_ref[:, cols] = slope.astype(BF)
-        cols = slice(group * width, (group + 1) * width)
-        for i, (ref, out) in enumerate(((act_ref, act_out), (slope_ref, slope_out))):
-            copies.append(pltpu.make_async_copy(ref.at[:, cols], out.at[:, cols], sems.at[group, i]))
-            copies[-1].start()
+            act_out[:, cols] = value.astype(BF)
+            slope_out[:, cols] = slope.astype(BF)
     feed = dot_nt(act_ref[:, :width], own_w2_ref[...]) + dot_nt(act_ref[:, width:], other_w2_ref[...])
     out_ref[...] = feed.astype(out_ref.dtype)
-    for copy in copies:
-        copy.wait()
 
 
 def layer_end_kernel(keep_ref, far_ref, bias_ref, middle_ref, mod_ref, feed_ref, out_ref):
@@ -470,15 +465,17 @@
     for one_ref, *got in (refs[i * (1 + CHUNKS) : (i + 1) * (1 + CHUNKS)] for i in range(count)):
         cols = slice(first, first + one_ref.shape[1])
         first = cols.stop
-        copies.append(pltpu.make_async_copy(one_ref, one_all.at[:, cols], sems.at[len(copies)]))
         for i, two_ref in enumerate(got):
             rows = slice(i * size, (i + 1) * size)
-            copies.append(pltpu.make_async_copy(two_ref, two_all.at[rows, cols], sems.at[len(copies)]))
-    for copy in copies:
+            for ref, to in ((one_ref.at[rows], one_all), (two_ref, two_all)):
+                copies.append((i, pltpu.make_async_copy(ref, to.at[rows, cols], sems.at[len(copies)])))
+    copies.sort(key=lambda pair: pair[0])
+    for _, copy in copies:
         copy.start()
-    for copy in copies:
-        copy.wait()
     for i in range(CHUNKS):
+        for where, copy in copies:
+            if where == i:
+                copy.wait()
         rows = slice(i * size, (i + 1) * size)
         out_ref[rows] = (one_all[rows].astype(F32) + two_all[rows].astype(F32)).astype(BF)
 
@@ -500,7 +497,8 @@
     local = w_out[0].shape[1]
     hidden = w_fc1[0].shape[1]
     token = yield None, ()
-    (normed,) = call(first_norm_kernel, (rows, mod), [like(size, width, BF)], token=token)
+    early, mod = mod
+    (normed,) = call(first_norm_kernel, (rows, early), [like(size, width, BF)], token=token)
     normed_far = swap(normed, 2)
     triple_outs = [like(size, 6 * local, BF), like(size, 2 * local, BF), like(size, 2 * local, BF)]
     triple, *sends = call(triple_kernel, (normed, *w_qkv, b_qkv), triple_outs)
@@ -530,17 +528,12 @@
     )
     second_far = swap(second, 2)
     outs = [like(size, 2 * hidden, BF), like(size, 2 * hidden, BF)]
-    scratch = [
-        pltpu.VMEM((size, 2 * hidden), BF),
-        pltpu.VMEM((size, 2 * hidden), BF),
-        pltpu.SemaphoreType.DMA((2, 2)),
-    ]
+    scratch = [pltpu.VMEM((size, 2 * hidden), BF)]
     act, slope, keep = call(
         mlp_kernel,
         (second, *w_fc1, b_fc1, *w_fc2),
         [*outs, like(size, width, F32)],
         scratch=scratch,
-        far_out=(0, 1),
     )
     token = yield keep, ()
     second_far = tied(second_far, token)
@@ -550,7 +543,6 @@
         [*outs, like(size, width, BF)],
         scratch=scratch,
         token=token,
-        far_out=(0, 1),
     )
     far = swap(send, 2)
     token = yield send, ()
@@ -570,6 +562,7 @@
 def backward_steps(grad, mod, weights, state, flops=0):
     w_qkv, b_qkv, w_out, b_out, w_fc1, b_fc1, w_fc2 = weights
     rows, normed, tokens, mixed, log, branch, middle, second, acts, slopes, feed = state
+    mod = mod[1]
     size, width = rows.shape
     local = w_out[0].shape[1]
     hidden = w_fc1[0].shape[1]
@@ -711,7 +704,7 @@
                 scratch=[
                     pltpu.VMEM((rows, cols), BF),
                     pltpu.VMEM((rows, cols), BF),
-                    pltpu.SemaphoreType.DMA((len(parts),)),
+                    pltpu.SemaphoreType.DMA((2 * CHUNKS * count,)),
                 ],
                 token=token,
                 far_in=range(len(parts)),
@@ -770,7 +763,12 @@
     ada_weight = w_ada[0]
     cond_vals = conditioning.astype(F32)
     cond_act = jax.nn.silu(cond_vals).astype(BF)
-    mods = (dot_nn(cond_act, ada_weight) + ada_bias[0].astype(F32)).reshape(2, 6, width)
+    shift = ada_bias[0].astype(F32)
+    mods = [
+        (dot_nn(cond_act, ada_weight[:, part]) + shift[part]).reshape(2, -1, width)
+        for part in (slice(0, 2 * width), slice(2 * width, 6 * width))
+    ]
+    mods = [(mods[0][b], jnp.concatenate([mods[0][b], mods[1][b]], 0)) for b in range(2)]
 
     section = lax.axis_index("section").astype(jnp.int32).reshape(1)
     chains, sums, token, begun = side_by_side(
@@ -820,11 +818,19 @@
     (flat,) = call(
         copy_kernel, (flat.reshape(-1, width),), [like(flat.size // width, width, F32)], token=token, flops=10**11
     )
-    flat = tied(tensor_sum(flat), begun[0]).reshape(-1)
+    flat = tensor_sum(flat).reshape(-1)
     grad_mods = flat[: 12 * width].reshape(2, 6 * width)
     biases = flat[12 * width :]
+    rest, terms = grad_mods, []
+    for _ in range(3):
+        terms.append(lax.reduce_precision(rest, 8, 7))
+        rest = rest - terms[-1]
+    back_cond = dot_nt(jnp.concatenate(terms, 0).astype(BF), ada_weight)
+    back_cond = tied(back_cond.reshape(3, 2, width).sum(0), begun[0])
+    cond_total = back_cond + lax.ppermute(back_cond, "section", [(0, 1), (1, 0)])
+    begun = [begun[0], (cond_total, *(begun[1] or ()))]
     everything = over_dp(
-        jnp.concatenate([grad_mods.reshape(-1), biases, cond_act.astype(F32).reshape(-1)])[None]
+        jnp.concatenate([grad_mods.reshape(-1), biases, cond_act.astype(F32).reshape(-1)])[None], begun[:2]
     )
     mods_end = 12 * width
     all_mods = everything[:, :mods_end].reshape(2 * dp_count, 6 * width)
@@ -848,19 +854,6 @@
         act_share, all_mods, (((0,), (0,)), ((), ())), precision=precise, preferred_element_type=F32
     )
 
-    cut = 6 * width // tensor_count
-    mods_cut = lax.dynamic_slice(grad_mods, (0, tensor_no * cut), (2, cut))
-    ada_cut = lax.dynamic_slice(ada_weight, (0, tensor_no * cut), (width, cut))
-    back_cond = lax.dot_general(
-        mods_cut,
-        ada_cut.astype(F32),
-        (((1,), (1,)), ((), ())),
-        precision=precise,
-        preferred_element_type=F32,
-    )
-    back_cond = tied(back_cond, (everything, *(begun[1] or ())))
-    back_cond = back_cond + lax.ppermute(back_cond, "section", [(0, 1), (1, 0)])
-    cond_total = tensor_sum(back_cond)
     sig = jax.nn.sigmoid(cond_vals)
     cond_grad = cond_total * sig * (1.0 + cond_vals * (1.0 - sig))
 

time: 591 us -> 590 us (level)
  waiting for transfers between devices: 120 us -> 135 us
  Pallas kernels: 271 us -> 257 us
  starting transfers between devices: 91.3 us -> 84.4 us
    pallas_call x72, Pallas kernels: 271 us -> 257 us  [call(): pl.pallas_call(body, in_specs=specs, out_specs=[anywhere if i in far_out...]
    ppermute x77 -> x75, waiting for transfers between devices: 101 us -> 112 us  [swap(): return lax.ppermute(block, 'tensor', [(i, i ^ bit) for i in range(count)])]
    ppermute x77 -> x75, starting transfers between devices: 58.4 us -> 47.3 us  [swap(): return lax.ppermute(block, 'tensor', [(i, i ^ bit) for i in range(count)])]
    unnamed x382 -> x362, local copies, waits for them, and re-layouts: 47 us -> 48.6 us
  transfers between devices with their start and end apart: 92 -> 90, of which waited for: 35 -> 30; matrix products, arithmetic and copies ran while one was open for 5% -> 5% of each run, Pallas kernels for 46% -> 44%
where the time goes in v3:
time: 590 us; the launch traced here: 579 us
  Pallas kernels  257 us (44%)
  waiting for transfers between devices  135 us (23%)
  starting transfers between devices  84.4 us (14%)
  local copies, waits for them, and re-layouts  57.6 us (10%)
  matrix products  18.1 us (3%)
  between operations  17.2 us (3%)
  other arithmetic  10.1 us (2%)
    pallas_call x72, Pallas kernels, call(): pl.pallas_call(body, in_specs=specs, out_specs=[anywhere if i in far_out...  257 us
    ppermute x75, waiting for transfers between devices, swap(): return lax.ppermute(block, 'tensor', [(i, i ^ bit) for i in range(count)])  112 us
    unnamed x362, local copies, waits for them, and re-layouts  48.6 us
    ppermute x75, starting transfers between devices, swap(): return lax.ppermute(block, 'tensor', [(i, i ^ bit) for i in range(count)])  47.3 us
    ppermute x3, starting transfers between devices, line_reduce(): up = lax.ppermute(up, 'dp', [(i, i + 1) for i in range(step)])  13.7 us
  transfers between devices with their start and end apart: 90, of which 30 were waited for; matrix products, arithmetic and copies ran while one was open for 5% of the time, Pallas kernels for 44%

profile of v3, /device:TPU:0, one launch (start us, length us, event | category | flops | bytes accessed | tf_op | source)
XLA Modules:
  0.0 579.5 jit_solution(10195128411535972373)
XLA Ops:
  10.0 2.8 fusion.9
  18.2 4.6 fusion.4
  22.9 3.3 shard_map.195
  32.0 3.3 shard_map.198
  42.3 10.2 %shard_map.199 = (bf16[512,512]{1,0:T(8,128)(2,1)S(1)}, f32[8,512]{1,0:T(8,128)S(1)}, f32[256,1024]{1,0:T(8,128)S(1)}, bf16[256,1024]{1,0:T(8,128)(2,1)S(1)}) custom-call(bf16[256,1536]{1,0:T(8,128)(2,1)S(1)} %copy-done.104, bf16[256,1536]{1,0:T(8,128)(2,1)S(1)} %copy-done.127, bf16[256,512]{1,0:T(8,128)(2,1)} %collective-permute-done.3.refs_2_.refs_6_, ...), custom_call_target="tpu_custom_call" | custom-call | flops 9200000000 | tf_op jit(solution)/shard_map/pallas_call | solution.py:105
  57.4 9.6 %shard_map.201 = (bf16[512,512]{1,0:T(8,128)(2,1)S(1)}, f32[8,512]{1,0:T(8,128)S(1)}, f32[256,1024]{1,0:T(8,128)S(1)}, bf16[256,1024]{1,0:T(8,128)(2,1)S(1)}) custom-call(bf16[256,1536]{1,0:T(8,128)(2,1)S(1)} %copy-done.124, bf16[256,1536]{1,0:T(8,128)(2,1)S(1)} %get-tuple-element.283.refs_1_.refs_5_, ...), custom_call_target="tpu_custom_call" | custom-call | flops 9200000000 | tf_op jit(solution)/shard_map/pallas_call | solution.py:105
  73.9 3.3 shard_map.203
  78.2 3.7 collective-permute-done.17.refs_1_
  84.2 3.1 shard_map.205
  88.4 4.8 collective-permute-done.16.refs_0_.refs_2_
  93.2 3.1 shard_map.206
  98.3 6.1 %collective-permute-done.19.refs_0_.refs_4_ = bf16[256,1024]{1,0:T(8,128)(2,1)S(1)} collective-permute-done((bf16[256,1024]{1,0:T(8,128)(2,1)S(1)}, bf16[256,1024]{1,0:T(8,128)(2,1)S(1)}, u32[]{:S(2)}, u32[]{:S(2)}) %collective-permute-start.19) | collective-permute-done | bytes 524320 | tf_op jit(solution)/shard_map/ppermute | solution.py:20
  104.4 3.1 shard_map.207
  108.6 7.0 %collective-permute-done.18.refs_1_ = bf16[256,1024]{1,0:T(8,128)(2,1)S(1)} collective-permute-done((bf16[256,1024]{1,0:T(8,128)(2,1)S(1)}, bf16[256,1024]{1,0:T(8,128)(2,1)S(1)}, u32[]{:S(2)}, u32[]{:S(2)}) %collective-permute-start.18) | collective-permute-done | bytes 524320 | tf_op jit(solution)/shard_map/ppermute | solution.py:20
  115.9 3.4 collective-permute-start.20
  119.4 6.8 %collective-permute-done.22.refs_1_ = bf16[256,1024]{1,0:T(8,128)(2,1)S(1)} collective-permute-done((bf16[256,1024]{1,0:T(8,128)(2,1)S(1)}, bf16[256,1024]{1,0:T(8,128)(2,1)S(1)}, u32[]{:S(2)}, u32[]{:S(2)}) %collective-permute-start.22) | collective-permute-done | bytes 524320 | tf_op jit(solution)/shard_map/ppermute | solution.py:20
  126.5 3.6 collective-permute-start.23
  134.6 6.1 %collective-permute-done.23.refs_0_.refs_3_.refs_2_ = bf16[256,1024]{1,0:T(8,128)(2,1)S(1)} collective-permute-done((bf16[256,1024]{1,0:T(8,128)(2,1)S(1)}, bf16[256,1024]{1,0:T(8,128)(2,1)S(1)}, u32[]{:S(2)}, u32[]{:S(2)}) %collective-permute-start.23) | collective-permute-done | bytes 524320 | tf_op jit(solution)/shard_map/ppermute | solution.py:657
  148.5 9.6 %shard_map.215 = (bf16[512,512]{1,0:T(8,128)(2,1)S(1)}, f32[8,512]{1,0:T(8,128)S(1)}, f32[256,1024]{1,0:T(8,128)S(1)}, bf16[256,1024]{1,0:T(8,128)(2,1)S(1)}) custom-call(bf16[256,1536]{1,0:T(8,128)(2,1)S(1)} %get-tuple-element.303.refs_2_.refs_0_.refs_4_, bf16[256,1536]{1,0:T(8,128)(2,1)S(1)} %get-tuple-element.309.refs_1_.refs_5_, ...), custom_call_target="tpu_custom_call" | custom-call | flops 9200000000 | tf_op jit(solution)/shard_map/pallas_call | solution.py:105
  165.9 9.6 %shard_map.217 = (bf16[512,512]{1,0:T(8,128)(2,1)S(1)}, f32[8,512]{1,0:T(8,128)S(1)}, f32[256,1024]{1,0:T(8,128)S(1)}, bf16[256,1024]{1,0:T(8,128)(2,1)S(1)}) custom-call(bf16[256,1536]{1,0:T(8,128)(2,1)S(1)} %get-tuple-element.307.refs_4_.refs_8_.refs_0_, bf16[256,1536]{1,0:T(8,128)(2,1)S(1)} %get-tuple-element.317.refs_1_.refs_5_, ...), custom_call_target="tpu_custom_call" | custom-call | flops 9200000000 | tf_op jit(solution)/shard_map/pallas_call | solution.py:105
  180.1 3.1 shard_map.219
  184.2 6.1 %collective-permute-done.35.refs_1_ = bf16[256,1024]{1,0:T(8,128)(2,1)S(1)} collective-permute-done((bf16[256,1024]{1,0:T(8,128)(2,1)S(1)}, bf16[256,1024]{1,0:T(8,128)(2,1)S(1)}, u32[]{:S(2)}, u32[]{:S(2)}) %collective-permute-start.35) | collective-permute-done | bytes 524320 | tf_op jit(solution)/shard_map/ppermute | solution.py:20
  191.9 3.3 shard_map.221
  195.2 6.3 %collective-permute-done.34.refs_0_.refs_10_ = bf16[256,1024]{1,0:T(8,128)(2,1)S(1)} collective-permute-done((bf16[256,1024]{1,0:T(8,128)(2,1)S(1)}, bf16[256,1024]{1,0:T(8,128)(2,1)S(1)}, u32[]{:S(2)}, u32[]{:S(2)}) %collective-permute-start.34) | collective-permute-done | bytes 524320 | tf_op jit(solution)/shard_map/ppermute | solution.py:20
  201.5 3.1 shard_map.222
  207.7 5.1 collective-permute-done.37.refs_0_.refs_12_
  212.8 3.1 shard_map.223
  218.8 5.1 collective-permute-done.36.refs_1_
  225.5 4.7 shard_map.226
  230.3 4.9 collective-permute-done.39.refs_1_
  237.6 4.5 shard_map.229
  242.1 4.4 collective-permute-done.38.refs_0_.refs_10_
  246.5 4.6 shard_map.230
  252.2 5.5 collective-permute-done.41.refs_0_.refs_12_
  257.7 5.1 shard_map.231
  263.8 5.1 collective-permute-done.40.refs_1_
  271.1 9.1 %collective-permute-done.43.refs_1_ = bf16[256,1024]{1,0:T(8,128)(2,1)S(1)} collective-permute-done((bf16[256,1024]{1,0:T(8,128)(2,1)S(1)}, bf16[256,1024]{1,0:T(8,128)(2,1)S(1)}, u32[]{:S(2)}, u32[]{:S(2)}) %collective-permute-start.43) | collective-permute-done | bytes 524320 | tf_op jit(solution)/shard_map/ppermute | solution.py:20
  282.3 9.1 %collective-permute-done.42.refs_1_.refs_8_ = bf16[256,1024]{1,0:T(8,128)(2,1)S(1)} collective-permute-done((bf16[256,1024]{1,0:T(8,128)(2,1)S(1)}, bf16[256,1024]{1,0:T(8,128)(2,1)S(1)}, u32[]{:S(2)}, u32[]{:S(2)}) %collective-permute-start.42) | collective-permute-done | bytes 524320 | tf_op jit(solution)/shard_map/ppermute | solution.py:20
  291.4 12.6 %shard_map.234 = (bf16[512,512]{1,0:T(8,128)(2,1)S(1)}, f32[512,1024]{1,0:T(8,128)S(1)}, bf16[512,1024]{1,0:T(8,128)(2,1)S(1)}) custom-call(bf16[256,1024]{1,0:T(8,128)(2,1)S(1)} %get-tuple-element.355.refs_6_.refs_0_.refs_7_, bf16[256,1024]{1,0:T(8,128)(2,1)S(1)} %collective-permute-done.42.refs_1_.refs_8_, bf16[1024,256]{1,0:T(8,128)(2,1)S(1)} %bitcast.130, ...), custom_call_target="tpu_custom_call" | custom-call | flops 12650000384 | tf_op jit(solution)/shard_map/pallas_call | solution.py:105
  304.1 12.4 %shard_map.235 = (bf16[512,512]{1,0:T(8,128)(2,1)S(1)}, f32[512,1024]{1,0:T(8,128)S(1)}, bf16[512,1024]{1,0:T(8,128)(2,1)S(1)}) custom-call(bf16[256,1024]{1,0:T(8,128)(2,1)S(1)} %get-tuple-element.358.refs_12_.refs_0_.refs_9_, bf16[256,1024]{1,0:T(8,128)(2,1)S(1)} %collective-permute-done.45.refs_1_.refs_10_, bf16[1024,256]{1,0:T(8,128)(2,1)S(1)} %bitcast.131, ...), custom_call_target="tpu_custom_call" | custom-call | flops 12650000384 | tf_op jit(solution)/shard_map/pallas_call | solution.py:105
  317.1 2.9 shard_map.236
  323.5 3.5 shard_map.238
  331.5 3.3 collective-permute-done.46.refs_1_
  337.1 8.2 %collective-permute-done.50.refs_1_ = bf16[256,1024]{1,0:T(8,128)(2,1)} collective-permute-done((bf16[256,1024]{1,0:T(8,128)(2,1)}, bf16[256,1024]{1,0:T(8,128)(2,1)}, u32[]{:S(2)}, u32[]{:S(2)}) %collective-permute-start.50) | collective-permute-done | bytes 524320 | tf_op jit(solution)/shard_map/ppermute | solution.py:20
  353.3 4.6 shard_map.242
  357.9 5.6 collective-permute-done.51.refs_0_.refs_4_
  364.8 4.6 shard_map.245
  369.4 4.9 shard_map.246
  376.4 4.7 shard_map.247
  383.1 8.5 %shard_map.248 = (bf16[1024,1024]{1,0:T(8,128)(2,1)S(1)}, bf16[256,1024]{1,0:T(8,128)(2,1)S(1)}, bf16[256,1024]{1,0:T(8,128)(2,1)S(1)}, bf16[256,1024]{1,0:T(8,128)(2,1)S(1)}, bf16[256,1024]{1,0:T(8,128)(2,1)S(1)}) custom-call(s32[1]{0:T(128)} %bitcast.15.refs_0_, bf16[256,1024]{1,0:T(8,128)(2,1)} %copy-done.61, bf16[256,1024]{1,0:T(8,128)(2,1)} %copy-done.62, ...), custom_call_target="tpu_custom_call" | custom-call | flops 6899999744 | tf_op jit(solution)/shard_map/pallas_call | solution.py:105
  404.5 3.7 shard_map.251.refs_17_
  408.3 8.8 %shard_map.252 = (bf16[1024,1024]{1,0:T(8,128)(2,1)S(1)}, bf16[256,1024]{1,0:T(8,128)(2,1)S(1)}, bf16[256,1024]{1,0:T(8,128)(2,1)S(1)}, bf16[256,1024]{1,0:T(8,128)(2,1)S(1)}, bf16[256,1024]{1,0:T(8,128)(2,1)S(1)}) custom-call(s32[1]{0:T(128)} %bitcast.15.refs_0_, bf16[256,1024]{1,0:T(8,128)(2,1)} %copy-done.43, bf16[256,1024]{1,0:T(8,128)(2,1)} %copy-done.44, ...), custom_call_target="tpu_custom_call" | custom-call | flops 6899999744 | tf_op jit(solution)/shard_map/pallas_call | solution.py:105
  419.6 13.0 %shard_map.253 = (bf16[512,512]{1,0:T(8,128)(2,1)S(1)}, f32[512,1024]{1,0:T(8,128)S(1)}, bf16[512,1024]{1,0:T(8,128)(2,1)S(1)}) custom-call(bf16[256,1024]{1,0:T(8,128)(2,1)} %get-tuple-element.406.refs_6_.refs_0_.refs_1_, bf16[256,1024]{1,0:T(8,128)(2,1)} %collective-permute-done.54.refs_1_.refs_2_, bf16[1024,256]{1,0:T(8,128)(2,1)S(1)} %bitcast.132, ...), custom_call_target="tpu_custom_call" | custom-call | flops 12650000384 | tf_op jit(solution)/shard_map/pallas_call | solution.py:105
  434.5 13.3 %shard_map.254 = (bf16[512,512]{1,0:T(8,128)(2,1)S(1)}, f32[512,1024]{1,0:T(8,128)S(1)}, bf16[512,1024]{1,0:T(8,128)(2,1)S(1)}) custom-call(bf16[256,1024]{1,0:T(8,128)(2,1)S(1)} %get-tuple-element.421.refs_5_.refs_0_.refs_3_, bf16[256,1024]{1,0:T(8,128)(2,1)} %collective-permute-done.61.refs_1_.refs_4_, bf16[1024,256]{1,0:T(8,128)(2,1)S(1)} %bitcast.133, ...), custom_call_target="tpu_custom_call" | custom-call | flops 99999997952 | tf_op jit(solution)/shard_map/pallas_call | solution.py:105
  450.9 3.8 shard_map.255.refs_13_
  455.3 4.8 shard_map.256
  470.9 3.7 shard_map.259
  478.7 8.6 %shard_map.261 = (bf16[1024,768]{1,0:T(8,128)(2,1)S(1)}, bf16[256,768]{1,0:T(8,128)(2,1)}, bf16[256,768]{1,0:T(8,128)(2,1)S(1)}, bf16[256,768]{1,0:T(8,128)(2,1)S(1)}, bf16[256,768]{1,0:T(8,128)(2,1)S(1)}) custom-call(s32[1]{0:T(128)} %bitcast.15.refs_0_, bf16[256,1024]{1,0:T(8,128)(2,1)} %shard_map.194.rows_ref.refs_1_, ...), custom_call_target="tpu_custom_call" | custom-call | flops 6899999744 | tf_op jit(solution)/shard_map/pallas_call | solution.py:105
  508.3 3.6 collective-permute-start.79
  518.4 8.0 %fusion.12 = f32[2,1024]{1,0:T(2,128)S(1)} fusion(bf16[3,2,6144]{2,1,0:T(2,128)(2,1)S(1)} %convert_element_type.93, bf16[1,1024,6144]{2,1,0:T(8,128)(2,1)} %param.20), kind=kOutput, calls=%fused_computation.10 | convolution fusion | flops 75501568 | bytes 12664832 | tf_op jit(solution)/shard_map/dot_general | solution.py:130
  533.0 4.8 collective-permute-start.82
  538.0 8.7 %collective-permute-done.82 = bf16[256,1024]{1,0:T(8,128)(2,1)S(1)} collective-permute-done((bf16[256,1024]{1,0:T(8,128)(2,1)S(1)}, bf16[256,1024]{1,0:T(8,128)(2,1)S(1)}, u32[]{:S(2)}, u32[]{:S(2)}) %collective-permute-start.82) | collective-permute-done | bytes 524320 | tf_op jit(solution)/shard_map/ppermute | solution.py:79
  546.7 8.1 %collective-permute-start.87 = (f32[2,22528]{1,0:T(2,128)S(1)}, f32[2,22528]{1,0:T(2,128)S(1)}, u32[]{:S(2)}, u32[]{:S(2)}) collective-permute-start(f32[2,22528]{1,0:T(2,128)S(1)} %pad_maximum_fusion.2), channel_id=1, source_target_pairs={{0,8},{4,12},{8,0},{12,4},{1,9},{5,13},{9,1},{13,5},{2,10},{6,14},... | collective-permute-start | bytes 540680 | tf_op jit(solution)/shard_map/ppermute | solution.py:59
  557.5 5.4 collective-permute-start.84
  (646 shorter events, 188.6 us)
Async XLA Ops:
  7.2 483.5 %reduce-scatter.3.cloned.1.call-start = ((), (), s32[]{:S(2)}) async-start(), calls=%async_computation.2 | async-start | bytes 2621440 | tf_op jit(solution)/shard_map/reduce_scatter | solution.py:715
  8.9 14.0 %collective-permute-start = (bf16[1024,768]{1,0:T(8,128)(2,1)S(1)}, bf16[1024,768]{1,0:T(8,128)(2,1)}, u32[]{:S(2)}, u32[]{:S(2)}) collective-permute-start(bf16[1024,768]{1,0:T(8,128)(2,1)S(1)} %pad_maximum_fusion.own_w_ref.refs_1_.refs_3_), channel_id=1, source_target_pairs={{0,1},{1,0},{2,3},{3,2},{4,5},{5,4},{6,7},{7,6},{8,9},{9,8},{10,11... | collective-permute-start | bytes 4718600 | tf_op jit(solution)/shard_map/ppermute | solution.py:20
  9.5 13.4 %collective-permute-start.1 = (f32[1,1792]{1,0:T(1,128)S(1)}, f32[1,1792]{1,0:T(1,128)S(1)}, u32[]{:S(2)}, u32[]{:S(2)}) collective-permute-start(f32[1,1792]{1,0:T(1,128)S(1)} %pad_maximum_fusion.8), channel_id=1, source_target_pairs={{0,1},{1,0},{2,3},{3,2},{4,5},{5,4},{6,7},{7,6},{8,9},{9,8},{10,11... | collective-permute-start | bytes 21512 | tf_op jit(solution)/shard_map/ppermute | solution.py:20
  15.4 16.1 %collective-permute-start.2 = (bf16[256,1024]{1,0:T(8,128)(2,1)}, bf16[256,1024]{1,0:T(8,128)(2,1)}, u32[]{:S(2)}, u32[]{:S(2)}) collective-permute-start(bf16[256,1024]{1,0:T(8,128)(2,1)} %shard_map.194.rows_ref.refs_1_), channel_id=1, source_target_pairs={{0,2},{1,3},{2,0},{3,1},{4,6},{5,7},{6,4},{7,5},{8,10},{9,11},{10,... | collective-permute-start | bytes 1572872 | tf_op jit(solution)/shard_map/ppermute | solution.py:20
  18.0 18.8 %collective-permute-start.7 = (bf16[1024,256]{1,0:T(8,128)(2,1)S(1)}, bf16[1024,256]{1,0:T(8,128)(2,1)}, u32[]{:S(2)}, u32[]{:S(2)}) collective-permute-start(bf16[1024,256]{1,0:T(8,128)(2,1)S(1)} %bitcast.125), channel_id=1, source_target_pairs={{0,1},{1,0},{2,3},{3,2},{4,5},{5,4},{6,7},{7,6},{8,9},{9,8},{10,11... | collective-permute-start | bytes 1572872 | tf_op jit(solution)/shard_map/ppermute | solution.py:20
  36.7 35.0 %collective-permute-start.14 = (bf16[1024,1024]{1,0:T(8,128)(2,1)}, bf16[1024,1024]{1,0:T(8,128)(2,1)S(1)}, u32[]{:S(2)}, u32[]{:S(2)}) collective-permute-start(bf16[1024,1024]{1,0:T(8,128)(2,1)} %bitcast.91), channel_id=1, source_target_pairs={{0,1},{1,0},{2,3},{3,2},{4,5},{5,4},{6,7},{7,6},{8,9},{9,8},{10,11... | collective-permute-start | bytes 6291464 | tf_op jit(solution)/shard_map/ppermute | solution.py:20
  37.2 34.6 %collective-permute-start.15 = (bf16[1024,1024]{1,0:T(8,128)(2,1)}, bf16[1024,1024]{1,0:T(8,128)(2,1)S(1)}, u32[]{:S(2)}, u32[]{:S(2)}) collective-permute-start(bf16[1024,1024]{1,0:T(8,128)(2,1)} %bitcast.108), channel_id=1, source_target_pairs={{0,1},{1,0},{2,3},{3,2},{4,5},{5,4},{6,7},{7,6},{8,9},{9,8},{10,11... | collective-permute-start | bytes 6291464 | tf_op jit(solution)/shard_map/ppermute | solution.py:20
  37.3 15.2 %collective-permute-start.9 = (bf16[256,1024]{1,0:T(8,128)(2,1)}, bf16[256,1024]{1,0:T(8,128)(2,1)S(1)}, u32[]{:S(2)}, u32[]{:S(2)}) collective-permute-start(bf16[256,1024]{1,0:T(8,128)(2,1)} %copy-done.37), channel_id=1, source_target_pairs={{0,2},{1,3},{2,0},{3,1},{4,6},{5,7},{6,4},{7,5},{8,10},{9,11},{10,... | collective-permute-start | bytes 1572872 | tf_op jit(solution)/shard_map/ppermute | solution.py:20
  38.4 17.1 %collective-permute-start.10 = (bf16[256,512]{1,0:T(8,128)(2,1)}, bf16[256,512]{1,0:T(8,128)(2,1)S(1)}, u32[]{:S(2)}, u32[]{:S(2)}) collective-permute-start(bf16[256,512]{1,0:T(8,128)(2,1)} %copy-done.80), channel_id=1, source_target_pairs={{0,1},{1,0},{2,3},{3,2},{4,5},{5,4},{6,7},{7,6},{8,9},{9,8},{10,11... | collective-permute-start | bytes 786440 | tf_op jit(solution)/shard_map/ppermute | solution.py:20
  38.4 17.6 %collective-permute-start.11 = (bf16[256,512]{1,0:T(8,128)(2,1)}, bf16[256,512]{1,0:T(8,128)(2,1)S(1)}, u32[]{:S(2)}, u32[]{:S(2)}) collective-permute-start(bf16[256,512]{1,0:T(8,128)(2,1)} %copy-done.79), channel_id=1, source_target_pairs={{0,1},{1,0},{2,3},{3,2},{4,5},{5,4},{6,7},{7,6},{8,9},{9,8},{10,11... | collective-permute-start | bytes 786440 | tf_op jit(solution)/shard_map/ppermute | solution.py:20
  56.0 14.1 %collective-permute-start.8 = (bf16[256,1024]{1,0:T(8,128)(2,1)S(1)}, bf16[256,1024]{1,0:T(8,128)(2,1)S(1)}, u32[]{:S(2)}, u32[]{:S(2)}) collective-permute-start(bf16[256,1024]{1,0:T(8,128)(2,1)S(1)} %get-tuple-element.281), channel_id=1, source_target_pairs={{0,2},{1,3},{2,0},{3,1},{4,6},{5,7},{6,4},{7,5},{8,10},{9,11},{10,... | collective-permute-start | bytes 1572872 | tf_op jit(solution)/shard_map/ppermute | solution.py:20
  67.1 14.8 %collective-permute-start.17 = (bf16[256,1024]{1,0:T(8,128)(2,1)S(1)}, bf16[256,1024]{1,0:T(8,128)(2,1)S(1)}, u32[]{:S(2)}, u32[]{:S(2)}) collective-permute-start(bf16[256,1024]{1,0:T(8,128)(2,1)S(1)} %get-tuple-element.292), channel_id=1, source_target_pairs={{0,2},{1,3},{2,0},{3,1},{4,6},{5,7},{6,4},{7,5},{8,10},{9,11},{10,... | collective-permute-start | bytes 1572872 | tf_op jit(solution)/shard_map/ppermute | solution.py:20
  70.7 22.4 %collective-permute-start.16 = (bf16[256,1024]{1,0:T(8,128)(2,1)S(1)}, bf16[256,1024]{1,0:T(8,128)(2,1)S(1)}, u32[]{:S(2)}, u32[]{:S(2)}) collective-permute-start(bf16[256,1024]{1,0:T(8,128)(2,1)S(1)} %get-tuple-element.290.rows_ref.refs_1_), channel_id=1, source_target_pairs={{0,2},{1,3},{2,0},{3,1},{4,6},{5,7},{6,4},{7,5},{8,10},{9,11},{10,... | collective-permute-start | bytes 1572872 | tf_op jit(solution)/shard_map/ppermute | solution.py:20
  83.3 21.1 %collective-permute-start.19 = (bf16[256,1024]{1,0:T(8,128)(2,1)S(1)}, bf16[256,1024]{1,0:T(8,128)(2,1)S(1)}, u32[]{:S(2)}, u32[]{:S(2)}) collective-permute-start(bf16[256,1024]{1,0:T(8,128)(2,1)S(1)} %get-tuple-element.294.rows_ref.refs_3_), channel_id=1, source_target_pairs={{0,2},{1,3},{2,0},{3,1},{4,6},{5,7},{6,4},{7,5},{8,10},{9,11},{10,... | collective-permute-start | bytes 1572872 | tf_op jit(solution)/shard_map/ppermute | solution.py:20
  97.3 18.3 %collective-permute-start.18 = (bf16[256,1024]{1,0:T(8,128)(2,1)S(1)}, bf16[256,1024]{1,0:T(8,128)(2,1)S(1)}, u32[]{:S(2)}, u32[]{:S(2)}) collective-permute-start(bf16[256,1024]{1,0:T(8,128)(2,1)S(1)} %get-tuple-element.297.refs_6_), channel_id=1, source_target_pairs={{0,2},{1,3},{2,0},{3,1},{4,6},{5,7},{6,4},{7,5},{8,10},{9,11},{10,... | collective-permute-start | bytes 1572872 | tf_op jit(solution)/shard_map/ppermute | solution.py:20
  107.6 18.6 %collective-permute-start.22 = (bf16[256,1024]{1,0:T(8,128)(2,1)S(1)}, bf16[256,1024]{1,0:T(8,128)(2,1)S(1)}, u32[]{:S(2)}, u32[]{:S(2)}) collective-permute-start(bf16[256,1024]{1,0:T(8,128)(2,1)S(1)} %get-tuple-element.299.refs_5_), channel_id=1, source_target_pairs={{0,2},{1,3},{2,0},{3,1},{4,6},{5,7},{6,4},{7,5},{8,10},{9,11},{10,... | collective-permute-start | bytes 1572872 | tf_op jit(solution)/shard_map/ppermute | solution.py:20
  115.9 14.2 %collective-permute-start.20 = (bf16[256,1024]{1,0:T(8,128)(2,1)S(1)}, bf16[256,1024]{1,0:T(8,128)(2,1)S(1)}, u32[]{:S(2)}, u32[]{:S(2)}) collective-permute-start(bf16[256,1024]{1,0:T(8,128)(2,1)S(1)} %get-tuple-element.302.refs_5_), channel_id=1, source_target_pairs={{0,16},{1,17},{2,18},{3,19},{4,20},{5,21},{6,22},{7,23},{8,24},{9,... | collective-permute-start | bytes 1572872 | tf_op jit(solution)/shard_map/ppermute | solution.py:657
  126.5 14.2 %collective-permute-start.23 = (bf16[256,1024]{1,0:T(8,128)(2,1)S(1)}, bf16[256,1024]{1,0:T(8,128)(2,1)S(1)}, u32[]{:S(2)}, u32[]{:S(2)}) collective-permute-start(bf16[256,1024]{1,0:T(8,128)(2,1)S(1)} %get-tuple-element.306), channel_id=1, source_target_pairs={{0,16},{1,17},{2,18},{3,19},{4,20},{5,21},{6,22},{7,23},{8,24},{9,... | collective-permute-start | bytes 1572872 | tf_op jit(solution)/shard_map/ppermute | solution.py:657
  130.6 13.2 %collective-permute-start.21 = (bf16[256,1024]{1,0:T(8,128)(2,1)S(1)}, bf16[256,1024]{1,0:T(8,128)(2,1)S(1)}, u32[]{:S(2)}, u32[]{:S(2)}) collective-permute-start(bf16[256,1024]{1,0:T(8,128)(2,1)S(1)} %shard_map.209.rows_ref.refs_9_), channel_id=1, source_target_pairs={{0,2},{1,3},{2,0},{3,1},{4,6},{5,7},{6,4},{7,5},{8,10},{9,11},{10,... | collective-permute-start | bytes 1572872 | tf_op jit(solution)/shard_map/ppermute | solution.py:20
  134.0 13.9 %collective-permute-start.24 = (bf16[256,512]{1,0:T(8,128)(2,1)S(1)}, bf16[256,512]{1,0:T(8,128)(2,1)S(1)}, u32[]{:S(2)}, u32[]{:S(2)}) collective-permute-start(bf16[256,512]{1,0:T(8,128)(2,1)S(1)} %get-tuple-element.310), channel_id=1, source_target_pairs={{0,1},{1,0},{2,3},{3,2},{4,5},{5,4},{6,7},{7,6},{8,9},{9,8},{10,11... | collective-permute-start | bytes 786440 | tf_op jit(solution)/shard_map/ppermute | solution.py:20
  134.1 13.8 %collective-permute-start.25 = (bf16[256,512]{1,0:T(8,128)(2,1)S(1)}, bf16[256,512]{1,0:T(8,128)(2,1)S(1)}, u32[]{:S(2)}, u32[]{:S(2)}) collective-permute-start(bf16[256,512]{1,0:T(8,128)(2,1)S(1)} %get-tuple-element.311), channel_id=1, source_target_pairs={{0,1},{1,0},{2,3},{3,2},{4,5},{5,4},{6,7},{7,6},{8,9},{9,8},{10,11... | collective-permute-start | bytes 786440 | tf_op jit(solution)/shard_map/ppermute | solution.py:20
  147.0 13.9 %collective-permute-start.29 = (bf16[256,1024]{1,0:T(8,128)(2,1)S(1)}, bf16[256,1024]{1,0:T(8,128)(2,1)S(1)}, u32[]{:S(2)}, u32[]{:S(2)}) collective-permute-start(bf16[256,1024]{1,0:T(8,128)(2,1)S(1)} %shard_map.212.rows_ref.refs_11_), channel_id=1, source_target_pairs={{0,2},{1,3},{2,0},{3,1},{4,6},{5,7},{6,4},{7,5},{8,10},{9,11},{10,... | collective-permute-start | bytes 1572872 | tf_op jit(solution)/shard_map/ppermute | solution.py:20
  147.9 17.5 %collective-permute-start.30 = (bf16[256,512]{1,0:T(8,128)(2,1)S(1)}, bf16[256,512]{1,0:T(8,128)(2,1)S(1)}, u32[]{:S(2)}, u32[]{:S(2)}) collective-permute-start(bf16[256,512]{1,0:T(8,128)(2,1)S(1)} %get-tuple-element.318), channel_id=1, source_target_pairs={{0,1},{1,0},{2,3},{3,2},{4,5},{5,4},{6,7},{7,6},{8,9},{9,8},{10,11... | collective-permute-start | bytes 786440 | tf_op jit(solution)/shard_map/ppermute | solution.py:20
  148.0 17.5 %collective-permute-start.31 = (bf16[256,512]{1,0:T(8,128)(2,1)S(1)}, bf16[256,512]{1,0:T(8,128)(2,1)S(1)}, u32[]{:S(2)}, u32[]{:S(2)}) collective-permute-start(bf16[256,512]{1,0:T(8,128)(2,1)S(1)} %get-tuple-element.319), channel_id=1, source_target_pairs={{0,1},{1,0},{2,3},{3,2},{4,5},{5,4},{6,7},{7,6},{8,9},{9,8},{10,11... | collective-permute-start | bytes 786440 | tf_op jit(solution)/shard_map/ppermute | solution.py:20
  164.5 14.0 %collective-permute-start.28 = (bf16[256,1024]{1,0:T(8,128)(2,1)S(1)}, bf16[256,1024]{1,0:T(8,128)(2,1)S(1)}, u32[]{:S(2)}, u32[]{:S(2)}) collective-permute-start(bf16[256,1024]{1,0:T(8,128)(2,1)S(1)} %get-tuple-element.315), channel_id=1, source_target_pairs={{0,2},{1,3},{2,0},{3,1},{4,6},{5,7},{6,4},{7,5},{8,10},{9,11},{10,... | collective-permute-start | bytes 1572872 | tf_op jit(solution)/shard_map/ppermute | solution.py:20
  175.4 14.8 %collective-permute-start.35 = (bf16[256,1024]{1,0:T(8,128)(2,1)S(1)}, bf16[256,1024]{1,0:T(8,128)(2,1)S(1)}, u32[]{:S(2)}, u32[]{:S(2)}) collective-permute-start(bf16[256,1024]{1,0:T(8,128)(2,1)S(1)} %get-tuple-element.326), channel_id=1, source_target_pairs={{0,2},{1,3},{2,0},{3,1},{4,6},{5,7},{6,4},{7,5},{8,10},{9,11},{10,... | collective-permute-start | bytes 1572872 | tf_op jit(solution)/shard_map/ppermute | solution.py:20
  179.0 22.5 %collective-permute-start.34 = (bf16[256,1024]{1,0:T(8,128)(2,1)S(1)}, bf16[256,1024]{1,0:T(8,128)(2,1)S(1)}, u32[]{:S(2)}, u32[]{:S(2)}) collective-permute-start(bf16[256,1024]{1,0:T(8,128)(2,1)S(1)} %get-tuple-element.324.rows_ref.refs_9_), channel_id=1, source_target_pairs={{0,2},{1,3},{2,0},{3,1},{4,6},{5,7},{6,4},{7,5},{8,10},{9,11},{10,... | collective-permute-start | bytes 1572872 | tf_op jit(solution)/shard_map/ppermute | solution.py:20
  190.8 21.9 %collective-permute-start.37 = (bf16[256,1024]{1,0:T(8,128)(2,1)S(1)}, bf16[256,1024]{1,0:T(8,128)(2,1)S(1)}, u32[]{:S(2)}, u32[]{:S(2)}) collective-permute-start(bf16[256,1024]{1,0:T(8,128)(2,1)S(1)} %get-tuple-element.328.rows_ref.refs_11_), channel_id=1, source_target_pairs={{0,2},{1,3},{2,0},{3,1},{4,6},{5,7},{6,4},{7,5},{8,10},{9,11},{10,... | collective-permute-start | bytes 1572872 | tf_op jit(solution)/shard_map/ppermute | solution.py:20
  206.7 17.3 %collective-permute-start.36 = (bf16[256,1024]{1,0:T(8,128)(2,1)S(1)}, bf16[256,1024]{1,0:T(8,128)(2,1)S(1)}, u32[]{:S(2)}, u32[]{:S(2)}) collective-permute-start(bf16[256,1024]{1,0:T(8,128)(2,1)S(1)} %get-tuple-element.331.refs_6_), channel_id=1, source_target_pairs={{0,2},{1,3},{2,0},{3,1},{4,6},{5,7},{6,4},{7,5},{8,10},{9,11},{10,... | collective-permute-start | bytes 1572872 | tf_op jit(solution)/shard_map/ppermute | solution.py:20
  217.9 17.3 %collective-permute-start.39 = (bf16[256,1024]{1,0:T(8,128)(2,1)S(1)}, bf16[256,1024]{1,0:T(8,128)(2,1)S(1)}, u32[]{:S(2)}, u32[]{:S(2)}) collective-permute-start(bf16[256,1024]{1,0:T(8,128)(2,1)S(1)} %get-tuple-element.333.refs_5_), channel_id=1, source_target_pairs={{0,2},{1,3},{2,0},{3,1},{4,6},{5,7},{6,4},{7,5},{8,10},{9,11},{10,... | collective-permute-start | bytes 1572872 | tf_op jit(solution)/shard_map/ppermute | solution.py:20
  224.5 21.9 %collective-permute-start.38 = (bf16[256,1024]{1,0:T(8,128)(2,1)S(1)}, bf16[256,1024]{1,0:T(8,128)(2,1)S(1)}, u32[]{:S(2)}, u32[]{:S(2)}) collective-permute-start(bf16[256,1024]{1,0:T(8,128)(2,1)S(1)} %get-tuple-element.337.rows_ref.refs_9_), channel_id=1, source_target_pairs={{0,2},{1,3},{2,0},{3,1},{4,6},{5,7},{6,4},{7,5},{8,10},{9,11},{10,... | collective-permute-start | bytes 1572872 | tf_op jit(solution)/shard_map/ppermute | solution.py:20
  236.5 21.2 %collective-permute-start.41 = (bf16[256,1024]{1,0:T(8,128)(2,1)S(1)}, bf16[256,1024]{1,0:T(8,128)(2,1)S(1)}, u32[]{:S(2)}, u32[]{:S(2)}) collective-permute-start(bf16[256,1024]{1,0:T(8,128)(2,1)S(1)} %get-tuple-element.344.rows_ref.refs_11_), channel_id=1, source_target_pairs={{0,2},{1,3},{2,0},{3,1},{4,6},{5,7},{6,4},{7,5},{8,10},{9,11},{10,... | collective-permute-start | bytes 1572872 | tf_op jit(solution)/shard_map/ppermute | solution.py:20
  251.1 17.8 %collective-permute-start.40 = (bf16[256,1024]{1,0:T(8,128)(2,1)S(1)}, bf16[256,1024]{1,0:T(8,128)(2,1)S(1)}, u32[]{:S(2)}, u32[]{:S(2)}) collective-permute-start(bf16[256,1024]{1,0:T(8,128)(2,1)S(1)} %get-tuple-element.349.refs_6_), channel_id=1, source_target_pairs={{0,2},{1,3},{2,0},{3,1},{4,6},{5,7},{6,4},{7,5},{8,10},{9,11},{10,... | collective-permute-start | bytes 1572872 | tf_op jit(solution)/shard_map/ppermute | solution.py:20
  262.8 17.4 %collective-permute-start.43 = (bf16[256,1024]{1,0:T(8,128)(2,1)S(1)}, bf16[256,1024]{1,0:T(8,128)(2,1)S(1)}, u32[]{:S(2)}, u32[]{:S(2)}) collective-permute-start(bf16[256,1024]{1,0:T(8,128)(2,1)S(1)} %get-tuple-element.352.refs_6_), channel_id=1, source_target_pairs={{0,2},{1,3},{2,0},{3,1},{4,6},{5,7},{6,4},{7,5},{8,10},{9,11},{10,... | collective-permute-start | bytes 1572872 | tf_op jit(solution)/shard_map/ppermute | solution.py:20
  270.1 21.3 %collective-permute-start.42 = (bf16[256,1024]{1,0:T(8,128)(2,1)S(1)}, bf16[256,1024]{1,0:T(8,128)(2,1)S(1)}, u32[]{:S(2)}, u32[]{:S(2)}) collective-permute-start(bf16[256,1024]{1,0:T(8,128)(2,1)S(1)} %get-tuple-element.355.refs_6_.refs_0_.refs_7_), channel_id=1, source_target_pairs={{0,2},{1,3},{2,0},{3,1},{4,6},{5,7},{6,4},{7,5},{8,10},{9,11},{10,... | collective-permute-start | bytes 1572872 | tf_op jit(solution)/shard_map/ppermute | solution.py:20
  281.3 22.8 %collective-permute-start.45 = (bf16[256,1024]{1,0:T(8,128)(2,1)S(1)}, bf16[256,1024]{1,0:T(8,128)(2,1)S(1)}, u32[]{:S(2)}, u32[]{:S(2)}) collective-permute-start(bf16[256,1024]{1,0:T(8,128)(2,1)S(1)} %get-tuple-element.358.refs_12_.refs_0_.refs_9_), channel_id=1, source_target_pairs={{0,2},{1,3},{2,0},{3,1},{4,6},{5,7},{6,4},{7,5},{8,10},{9,11},{10,... | collective-permute-start | bytes 1572872 | tf_op jit(solution)/shard_map/ppermute | solution.py:20
  304.0 13.1 %collective-permute-start.44 = (bf16[512,1024]{1,0:T(8,128)(2,1)S(1)}, bf16[512,1024]{1,0:T(8,128)(2,1)S(1)}, u32[]{:S(2)}, u32[]{:S(2)}) collective-permute-start(bf16[512,1024]{1,0:T(8,128)(2,1)S(1)} %get-tuple-element.364), channel_id=1, source_target_pairs={{0,1},{1,0},{2,3},{3,2},{4,5},{5,4},{6,7},{7,6},{8,9},{9,8},{10,11... | collective-permute-start | bytes 3145736 | tf_op jit(solution)/shard_map/ppermute | solution.py:20
  320.0 14.9 %collective-permute-start.46 = (bf16[256,1024]{1,0:T(8,128)(2,1)S(1)}, bf16[256,1024]{1,0:T(8,128)(2,1)S(1)}, u32[]{:S(2)}, u32[]{:S(2)}) collective-permute-start(bf16[256,1024]{1,0:T(8,128)(2,1)S(1)} %get-tuple-element.369.refs_5_), channel_id=1, source_target_pairs={{0,2},{1,3},{2,0},{3,1},{4,6},{5,7},{6,4},{7,5},{8,10},{9,11},{10,... | collective-permute-start | bytes 1572872 | tf_op jit(solution)/shard_map/ppermute | solution.py:20
  327.9 17.3 %collective-permute-start.50 = (bf16[256,1024]{1,0:T(8,128)(2,1)}, bf16[256,1024]{1,0:T(8,128)(2,1)}, u32[]{:S(2)}, u32[]{:S(2)}) collective-permute-start(bf16[256,1024]{1,0:T(8,128)(2,1)} %get-tuple-element.373.refs_5_), channel_id=1, source_target_pairs={{0,2},{1,3},{2,0},{3,1},{4,6},{5,7},{6,4},{7,5},{8,10},{9,11},{10,... | collective-permute-start | bytes 1572872 | tf_op jit(solution)/shard_map/ppermute | solution.py:20
  335.7 14.1 %collective-permute-start.48 = (bf16[256,1024]{1,0:T(8,128)(2,1)S(1)}, bf16[256,1024]{1,0:T(8,128)(2,1)S(1)}, u32[]{:S(2)}, u32[]{:S(2)}) collective-permute-start(bf16[256,1024]{1,0:T(8,128)(2,1)S(1)} %get-tuple-element.377.refs_5_), channel_id=1, source_target_pairs={{16,0},{17,1},{18,2},{19,3},{20,4},{21,5},{22,6},{23,7},{24,8},{25... | collective-permute-start | bytes 1572872 | tf_op jit(solution)/shard_map/ppermute | solution.py:662
  348.5 15.0 %collective-permute-start.51 = (bf16[256,1024]{1,0:T(8,128)(2,1)S(1)}, bf16[256,1024]{1,0:T(8,128)(2,1)S(1)}, u32[]{:S(2)}, u32[]{:S(2)}) collective-permute-start(bf16[256,1024]{1,0:T(8,128)(2,1)S(1)} %get-tuple-element.384), channel_id=1, source_target_pairs={{16,0},{17,1},{18,2},{19,3},{20,4},{21,5},{22,6},{23,7},{24,8},{25... | collective-permute-start | bytes 1572872 | tf_op jit(solution)/shard_map/ppermute | solution.py:662
  351.1 18.3 %collective-permute-start.49 = (bf16[256,1024]{1,0:T(8,128)(2,1)S(1)}, bf16[256,1024]{1,0:T(8,128)(2,1)S(1)}, u32[]{:S(2)}, u32[]{:S(2)}) collective-permute-start(bf16[256,1024]{1,0:T(8,128)(2,1)S(1)} %get-tuple-element.379.rows_ref.refs_1_), channel_id=1, source_target_pairs={{0,2},{1,3},{2,0},{3,1},{4,6},{5,7},{6,4},{7,5},{8,10},{9,11},{10,... | collective-permute-start | bytes 1572872 | tf_op jit(solution)/shard_map/ppermute | solution.py:20
  363.8 12.6 %collective-permute-start.53 = (bf16[256,1024]{1,0:T(8,128)(2,1)S(1)}, bf16[256,1024]{1,0:T(8,128)(2,1)S(1)}, u32[]{:S(2)}, u32[]{:S(2)}) collective-permute-start(bf16[256,1024]{1,0:T(8,128)(2,1)S(1)} %get-tuple-element.386.rows_ref.refs_3_), channel_id=1, source_target_pairs={{0,2},{1,3},{2,0},{3,1},{4,6},{5,7},{6,4},{7,5},{8,10},{9,11},{10,... | collective-permute-start | bytes 1572872 | tf_op jit(solution)/shard_map/ppermute | solution.py:20
  375.3 18.2 %collective-permute-start.52 = (bf16[256,1024]{1,0:T(8,128)(2,1)S(1)}, bf16[256,1024]{1,0:T(8,128)(2,1)S(1)}, u32[]{:S(2)}, u32[]{:S(2)}) collective-permute-start(bf16[256,1024]{1,0:T(8,128)(2,1)S(1)} %get-tuple-element.391.refs_6_), channel_id=1, source_target_pairs={{0,2},{1,3},{2,0},{3,1},{4,6},{5,7},{6,4},{7,5},{8,10},{9,11},{10,... | collective-permute-start | bytes 1572872 | tf_op jit(solution)/shard_map/ppermute | solution.py:20
  382.1 16.4 %collective-permute-start.59 = (bf16[256,1024]{1,0:T(8,128)(2,1)S(1)}, bf16[256,1024]{1,0:T(8,128)(2,1)S(1)}, u32[]{:S(2)}, u32[]{:S(2)}) collective-permute-start(bf16[256,1024]{1,0:T(8,128)(2,1)S(1)} %get-tuple-element.402.refs_17_), channel_id=1, source_target_pairs={{0,2},{1,3},{2,0},{3,1},{4,6},{5,7},{6,4},{7,5},{8,10},{9,11},{10,... | collective-permute-start | bytes 1572872 | tf_op jit(solution)/shard_map/ppermute | solution.py:20
  398.5 20.0 %collective-permute-start.54 = (bf16[256,1024]{1,0:T(8,128)(2,1)}, bf16[256,1024]{1,0:T(8,128)(2,1)}, u32[]{:S(2)}, u32[]{:S(2)}) collective-permute-start(bf16[256,1024]{1,0:T(8,128)(2,1)} %get-tuple-element.406.refs_6_.refs_0_.refs_1_), channel_id=1, source_target_pairs={{0,2},{1,3},{2,0},{3,1},{4,6},{5,7},{6,4},{7,5},{8,10},{9,11},{10,... | collective-permute-start | bytes 1572872 | tf_op jit(solution)/shard_map/ppermute | solution.py:20
  401.7 32.7 %collective-permute-start.61 = (bf16[256,1024]{1,0:T(8,128)(2,1)S(1)}, bf16[256,1024]{1,0:T(8,128)(2,1)}, u32[]{:S(2)}, u32[]{:S(2)}) collective-permute-start(bf16[256,1024]{1,0:T(8,128)(2,1)S(1)} %get-tuple-element.421.refs_5_.refs_0_.refs_3_), channel_id=1, source_target_pairs={{0,2},{1,3},{2,0},{3,1},{4,6},{5,7},{6,4},{7,5},{8,10},{9,11},{10,... | collective-permute-start | bytes 1572872 | tf_op jit(solution)/shard_map/ppermute | solution.py:20
  408.2 93.2 %reduce-scatter.5.cloned.1.call-start = ((), (), s32[]{:S(2)}) async-start(), calls=%async_computation.3 | async-start | bytes 2621440 | tf_op jit(solution)/shard_map/reduce_scatter | solution.py:715
  418.5 31.0 %collective-permute-start.62 = (bf16[256,1024]{1,0:T(8,128)(2,1)S(1)}, bf16[256,1024]{1,0:T(8,128)(2,1)S(1)}, u32[]{:S(2)}, u32[]{:S(2)}) collective-permute-start(bf16[256,1024]{1,0:T(8,128)(2,1)S(1)} %get-tuple-element.431), channel_id=1, source_target_pairs={{0,1},{1,0},{2,3},{3,2},{4,5},{5,4},{6,7},{7,6},{8,9},{9,8},{10,11... | collective-permute-start | bytes 1572872 | tf_op jit(solution)/shard_map/ppermute | solution.py:20
  418.5 31.0 %collective-permute-start.63 = (bf16[256,1024]{1,0:T(8,128)(2,1)S(1)}, bf16[256,1024]{1,0:T(8,128)(2,1)S(1)}, u32[]{:S(2)}, u32[]{:S(2)}) collective-permute-start(bf16[256,1024]{1,0:T(8,128)(2,1)S(1)} %get-tuple-element.432), channel_id=1, source_target_pairs={{0,1},{1,0},{2,3},{3,2},{4,5},{5,4},{6,7},{7,6},{8,9},{9,8},{10,11... | collective-permute-start | bytes 1572872 | tf_op jit(solution)/shard_map/ppermute | solution.py:20
  419.0 30.5 %collective-permute-start.64 = (bf16[256,1024]{1,0:T(8,128)(2,1)S(1)}, bf16[256,1024]{1,0:T(8,128)(2,1)S(1)}, u32[]{:S(2)}, u32[]{:S(2)}) collective-permute-start(bf16[256,1024]{1,0:T(8,128)(2,1)S(1)} %get-tuple-element.433), channel_id=1, source_target_pairs={{0,1},{1,0},{2,3},{3,2},{4,5},{5,4},{6,7},{7,6},{8,9},{9,8},{10,11... | collective-permute-start | bytes 1572872 | tf_op jit(solution)/shard_map/ppermute | solution.py:20
  419.0 30.5 %collective-permute-start.65 = (bf16[256,1024]{1,0:T(8,128)(2,1)S(1)}, bf16[256,1024]{1,0:T(8,128)(2,1)S(1)}, u32[]{:S(2)}, u32[]{:S(2)}) collective-permute-start(bf16[256,1024]{1,0:T(8,128)(2,1)S(1)} %get-tuple-element.434), channel_id=1, source_target_pairs={{0,1},{1,0},{2,3},{3,2},{4,5},{5,4},{6,7},{7,6},{8,9},{9,8},{10,11... | collective-permute-start | bytes 1572872 | tf_op jit(solution)/shard_map/ppermute | solution.py:20
  454.9 16.0 %collective-permute-start.67 = (bf16[512,1024]{1,0:T(8,128)(2,1)}, bf16[512,1024]{1,0:T(8,128)(2,1)S(1)}, u32[]{:S(2)}, u32[]{:S(2)}) collective-permute-start(bf16[512,1024]{1,0:T(8,128)(2,1)} %copy-done.33), channel_id=1, source_target_pairs={{0,1},{1,0},{2,3},{3,2},{4,5},{5,4},{6,7},{7,6},{8,9},{9,8},{10,11... | collective-permute-start | bytes 3145736 | tf_op jit(solution)/shard_map/ppermute | solution.py:20
  461.6 34.3 %collective-permute-start.73 = (bf16[256,256]{1,0:T(8,128)(2,1)}, bf16[256,256]{1,0:T(8,128)(2,1)}, u32[]{:S(2)}, u32[]{:S(2)}) collective-permute-start(bf16[256,256]{1,0:T(8,128)(2,1)} %get-tuple-element.492), channel_id=1, source_target_pairs={{0,1},{1,0},{2,3},{3,2},{4,5},{5,4},{6,7},{7,6},{8,9},{9,8},{10,11... | collective-permute-start | bytes 393224 | tf_op jit(solution)/shard_map/ppermute | solution.py:20
  461.7 35.5 %collective-permute-start.74 = (bf16[256,256]{1,0:T(8,128)(2,1)}, bf16[256,256]{1,0:T(8,128)(2,1)}, u32[]{:S(2)}, u32[]{:S(2)}) collective-permute-start(bf16[256,256]{1,0:T(8,128)(2,1)} %get-tuple-element.493), channel_id=1, source_target_pairs={{0,1},{1,0},{2,3},{3,2},{4,5},{5,4},{6,7},{7,6},{8,9},{9,8},{10,11... | collective-permute-start | bytes 393224 | tf_op jit(solution)/shard_map/ppermute | solution.py:20
  462.1 36.2 %collective-permute-start.75 = (bf16[256,256]{1,0:T(8,128)(2,1)}, bf16[256,256]{1,0:T(8,128)(2,1)}, u32[]{:S(2)}, u32[]{:S(2)}) collective-permute-start(bf16[256,256]{1,0:T(8,128)(2,1)} %get-tuple-element.494), channel_id=1, source_target_pairs={{0,1},{1,0},{2,3},{3,2},{4,5},{5,4},{6,7},{7,6},{8,9},{9,8},{10,11... | collective-permute-start | bytes 393224 | tf_op jit(solution)/shard_map/ppermute | solution.py:20
  465.9 24.7 %collective-permute-start.66 = (bf16[256,1024]{1,0:T(8,128)(2,1)S(1)}, bf16[256,1024]{1,0:T(8,128)(2,1)S(1)}, u32[]{:S(2)}, u32[]{:S(2)}) collective-permute-start(bf16[256,1024]{1,0:T(8,128)(2,1)S(1)} %get-tuple-element.438.refs_5_), channel_id=1, source_target_pairs={{0,2},{1,3},{2,0},{3,1},{4,6},{5,7},{6,4},{7,5},{8,10},{9,11},{10,... | collective-permute-start | bytes 1572872 | tf_op jit(solution)/shard_map/ppermute | solution.py:20
  474.6 18.1 %collective-permute-start.68 = (bf16[256,1024]{1,0:T(8,128)(2,1)}, bf16[256,1024]{1,0:T(8,128)(2,1)}, u32[]{:S(2)}, u32[]{:S(2)}) collective-permute-start(bf16[256,1024]{1,0:T(8,128)(2,1)} %get-tuple-element.444.refs_5_), channel_id=1, source_target_pairs={{0,2},{1,3},{2,0},{3,1},{4,6},{5,7},{6,4},{7,5},{8,10},{9,11},{10,... | collective-permute-start | bytes 1572872 | tf_op jit(solution)/shard_map/ppermute | solution.py:20
  508.3 18.2 %collective-permute-start.79 = (bf16[256,1024]{1,0:T(8,128)(2,1)}, bf16[256,1024]{1,0:T(8,128)(2,1)S(1)}, u32[]{:S(2)}, u32[]{:S(2)}) collective-permute-start(bf16[256,1024]{1,0:T(8,128)(2,1)} %get-tuple-element.524), channel_id=1, source_target_pairs={{0,4},{1,5},{2,6},{3,7},{16,20},{17,21},{18,22},{19,23}} | collective-permute-start | bytes 1572872 | tf_op jit(solution)/shard_map/ppermute | solution.py:79
  511.9 14.6 %collective-permute-start.80 = (bf16[256,1024]{1,0:T(8,128)(2,1)}, bf16[256,1024]{1,0:T(8,128)(2,1)}, u32[]{:S(2)}, u32[]{:S(2)}) collective-permute-start(bf16[256,1024]{1,0:T(8,128)(2,1)} %get-tuple-element.525), channel_id=1, source_target_pairs={{12,8},{13,9},{14,10},{15,11},{28,24},{29,25},{30,26},{31,27}} | collective-permute-start | bytes 1572872 | tf_op jit(solution)/shard_map/ppermute | solution.py:80
  533.0 13.7 %collective-permute-start.82 = (bf16[256,1024]{1,0:T(8,128)(2,1)S(1)}, bf16[256,1024]{1,0:T(8,128)(2,1)S(1)}, u32[]{:S(2)}, u32[]{:S(2)}) collective-permute-start(bf16[256,1024]{1,0:T(8,128)(2,1)S(1)} %get-tuple-element.527), channel_id=1, source_target_pairs={{0,4},{4,8},{1,5},{5,9},{2,6},{6,10},{3,7},{7,11},{16,20},{20,24},... | collective-permute-start | bytes 1572872 | tf_op jit(solution)/shard_map/ppermute | solution.py:79
  546.7 16.2 %collective-permute-start.87 = (f32[2,22528]{1,0:T(2,128)S(1)}, f32[2,22528]{1,0:T(2,128)S(1)}, u32[]{:S(2)}, u32[]{:S(2)}) collective-permute-start(f32[2,22528]{1,0:T(2,128)S(1)} %pad_maximum_fusion.2), channel_id=1, source_target_pairs={{0,8},{4,12},{8,0},{12,4},{1,9},{5,13},{9,1},{13,5},{2,10},{6,14},... | collective-permute-start | bytes 540680 | tf_op jit(solution)/shard_map/ppermute | solution.py:59
  556.2 12.2 %collective-permute-start.85 = (bf16[256,1024]{1,0:T(8,128)(2,1)}, bf16[256,1024]{1,0:T(8,128)(2,1)}, u32[]{:S(2)}, u32[]{:S(2)}) collective-permute-start(bf16[256,1024]{1,0:T(8,128)(2,1)} %get-tuple-element.530), channel_id=1, source_target_pairs={{4,0},{8,4},{12,8},{5,1},{9,5},{13,9},{6,2},{10,6},{14,10},{7,3},{... | collective-permute-start | bytes 1572872 | tf_op jit(solution)/shard_map/ppermute | solution.py:80
  557.5 11.6 %collective-permute-start.84 = (bf16[256,1024]{1,0:T(8,128)(2,1)}, bf16[256,1024]{1,0:T(8,128)(2,1)}, u32[]{:S(2)}, u32[]{:S(2)}) collective-permute-start(bf16[256,1024]{1,0:T(8,128)(2,1)} %get-tuple-element.529), channel_id=1, source_target_pairs={{0,4},{4,8},{8,12},{1,5},{5,9},{9,13},{2,6},{6,10},{10,14},{3,7},{... | collective-permute-start | bytes 1572872 | tf_op jit(solution)/shard_map/ppermute | solution.py:79
  (202 other events, 3057.3 us)
Sparse Core Ops, SparseCore 0:
  408.3 45.1 reduce-scatter.2
  455.9 44.1 reduce-scatter.4
